TPU v7x, 32 devices: a whole 2x2x4 slice. The times are simulated.
32 devices in a mesh: gz: 4 (over z), gy: 8 (over y, x, core).
Axes of the slice: x: 2, y: 2, z: 4, core: 2. Of those that a mesh axis runs over, the one named last changes fastest.
Arguments:
- thermal_departure: float32 [8, 1024, 1024], P(None, 'gy', 'gz'), may hold values from -6 to 6
- speed_along_primary: float32 [8, 1024, 1024], P(None, 'gy', 'gz'), may hold values from -4 to 4
- speed_along_lateral: float32 [8, 1024, 1024], P(None, 'gy', 'gz'), may hold values from -4 to 4
- upward_speed: float32 [8, 1024, 1024], P(None, 'gy', 'gz'), may hold values from -4 to 4
- container_solid_markers: int32 [8, 1024, 1024], P(None, 'gy', 'gz'), may hold values 0 or 1
Outputs:
- temp_next: float32 [8, 1024, 1024], P(None, 'gy', 'gz')
- u_next: float32 [8, 1024, 1024], P(None, 'gy', 'gz')
- v_next: float32 [8, 1024, 1024], P(None, 'gy', 'gz')
- w_next: float32 [8, 1024, 1024], P(None, 'gy', 'gz')
- path_map: float32 [8, 1024], P('gz', 'gy')
Inputs may be any that keep to these rules, and one draw needn't show every extreme that they name: `container_solid_markers`: 1 marks air, 0 a solid cell.
All inputs are finite; a program needn't handle non-finite values. No bound on the sum of `container_solid_markers` on one device may be relied on, other than what follows from the above.
Results may differ from a plain program's by a relative error of at most 0.00002.
Values sent between devices are 32-bit elements; how exact they have to be, the bound alone decides.
No kernel may reach another device: no remote copies, remote signals or barrier semaphores. Data moves between devices by JAX's collectives and lax.ppermute only.
A program may use at most 128 MiB of HBM per device.

v0:
```python
import math

import jax
import jax.numpy as jnp
from jax import lax
from jax.sharding import PartitionSpec as P

TIME_STEP = 0.1
NU_BASE = 0.05
KAPPA_BASE = 0.05
SMAG_COEF = 0.03
PRANDTL = 0.4
BUOYANCY = 0.5


def extended(shard, sides, width, wrap):
    for axis, dim in sides:
        count, length = (lax.axis_size(axis), shard.shape[dim])
        up = [(i, (i + 1) % count) for i in range(count if wrap else count - 1)]
        down = [(j, i) for i, j in up]
        last = lax.slice_in_dim(shard, length - width, length, axis=dim)
        first = lax.slice_in_dim(shard, 0, width, axis=dim)
        before = lax.ppermute(last, axis, up)
        after = lax.ppermute(first, axis, down)
        shard = jnp.concatenate([before, shard, after], axis=dim)
    return shard


def tendencies(padded):
    centre = padded[:, :, 1:-1, 1:-1]
    east_side = jnp.roll(centre, -1, 1)
    west_side = jnp.roll(centre, 1, 1)
    north_side = padded[:, :, 2:, 1:-1]
    south_side = padded[:, :, :-2, 1:-1]
    upper_side = padded[:, :, 1:-1, 2:]
    lower_side = padded[:, :, 1:-1, :-2]
    grad_x = 0.5 * (east_side - west_side)
    grad_y = 0.5 * (north_side - south_side)
    grad_z = 0.5 * (upper_side - lower_side)
    laplace = (
        east_side + west_side + north_side + south_side + upper_side + lower_side - 6.0 * centre
    )
    advect = centre[1] * grad_x + centre[2] * grad_y + centre[3] * grad_z
    strain = grad_x[1] * grad_x[1] + grad_y[2] * grad_y[2] + grad_z[3] * grad_z[3]
    shear_a = grad_y[1] + grad_x[2]
    shear_b = grad_z[1] + grad_x[3]
    shear_c = grad_z[2] + grad_y[3]
    strain = strain + 0.5 * (shear_a * shear_a + shear_b * shear_b + shear_c * shear_c)
    eddy_visc = SMAG_COEF * jnp.sqrt(2.0 * strain + 0.01)
    diffusion = jnp.stack(
        [
            KAPPA_BASE + eddy_visc / PRANDTL,
            NU_BASE + eddy_visc,
            NU_BASE + eddy_visc,
            NU_BASE + eddy_visc,
        ]
    )
    tendency = diffusion * laplace - advect
    buoyant = tendency[3] + BUOYANCY * centre[0]
    return jnp.stack([tendency[0], tendency[1], tendency[2], buoyant])


def masked(fluid_unknowns, fluid_mask):
    return jnp.concatenate([fluid_unknowns[:1], fluid_unknowns[1:] * fluid_mask[None]], 0)


def pad_one(fluid_unknowns):
    widened = extended(fluid_unknowns, (("gy", 2),), 1, True)
    return extended(widened, (("gz", 3),), 1, False)


def on_device(
    thermal_departure,
    speed_along_primary,
    speed_along_lateral,
    upward_speed,
    container_solid_markers,
):
    fluid_mask = container_solid_markers.astype(jnp.float32)
    fluid_unknowns = jnp.stack(
        [thermal_departure, speed_along_primary, speed_along_lateral, upward_speed]
    )
    column_cells = fluid_unknowns.shape[3]
    height_count = lax.axis_size("gz")
    section_one = masked(
        fluid_unknowns + TIME_STEP * tendencies(pad_one(fluid_unknowns)), fluid_mask
    )
    section_two = masked(
        0.5 * fluid_unknowns + 0.5 * (section_one + TIME_STEP * tendencies(pad_one(section_one))),
        fluid_mask,
    )
    refraction = 8.0 * (1.0 - jnp.exp(-section_two[0] / 8.0))
    scale_factor = 1.0 / math.sqrt(column_cells * height_count)
    path_sum = lax.psum_scatter(jnp.sum(refraction, axis=2), "gz", scatter_dimension=0, tiled=True)
    path_map = path_sum * scale_factor
    return (section_two[0], section_two[1], section_two[2], section_two[3], path_map)


def solution(mesh):
    return jax.shard_map(
        on_device,
        mesh=mesh,
        in_specs=(
            P(None, "gy", "gz"),
            P(None, "gy", "gz"),
            P(None, "gy", "gz"),
            P(None, "gy", "gz"),
            P(None, "gy", "gz"),
        ),
        out_specs=(
            P(None, "gy", "gz"),
            P(None, "gy", "gz"),
            P(None, "gy", "gz"),
            P(None, "gy", "gz"),
            P("gz", "gy"),
        ),
        check_vma=False,
    )
```

profile of v0, /device:TPU:0, one launch (start us, length us, event | category | flops | bytes accessed | tf_op | source)
XLA Modules:
  0.0 162.1 jit_solution(3381450470225246093)
XLA Ops:
  0.7 3.0 %copy_multiply_fusion.2 = (f32[8,128,256]{2,0,1:T(8,128)}, f32[1,8,128,256]{3,1,2,0:T(8,128)S(1)}) fusion(f32[8,128,256]{2,1,0:T(8,128)} %param.6), kind=kLoop, calls=%fused_computation.135 | loop fusion | flops 262144 | bytes 3145728 | tf_op jit(solution)/shard_map/mul | solution.py:43
  3.7 2.2 %copy.74 = f32[8,128,256]{2,0,1:T(8,128)S(1)} copy(f32[8,128,256]{2,1,0:T(8,128)} %param.5) | data formatting | bytes 2097152 | tf_op args[0]
  5.9 2.7 %copy_multiply_fusion = (f32[8,128,256]{2,0,1:T(8,128)}, f32[1,8,128,256]{3,1,2,0:T(8,128)S(1)}, f32[1,8,128,256]{3,1,2,0:T(8,128)S(1)}, f32[8,128,256]{2,0,1:T(8,128)}) fusion(f32[8,128,256]{2,1,0:T(8,128)S(1)} %copy-done.35, f32[8,128,256]{2,1,0:T(8,128)S(1)} %copy-done.36), kind=kLoop, calls=%fused_computation.131 | loop fusion | flops 524288 | bytes 6291456 | tf_op jit(solution)/shard_map/mul | solution.py:43
  8.6 0.3 pad_maximum_fusion.35
  8.9 0.6 copy-done.8
  9.6 3.3 %collective-permute-start = (f32[4,8,1,256]{3,1,2,0:T(8,128)S(1)}, f32[4,8,1,256]{3,1,2,0:T(8,128)S(1)}, u32[]{:S(2)}, u32[]{:S(2)}) collective-permute-start(f32[4,8,1,256]{3,1,2,0:T(8,128)S(1)} %get-tuple-element.41), channel_id=1, source_target_pairs={{1,0},{2,1},{3,2},{4,3},{5,4},{6,5},{7,6},{0,7},{9,8},{10,9},{11,1... | collective-permute-start | bytes 98312 | tf_op jit(solution)/shard_map/ppermute | solution.py:24
  12.9 0.8 fusion.52
  13.7 0.6 fusion.53
  14.4 4.2 %fusion.11 = f32[4,8,128,256]{3,1,2,0:T(8,128)} fusion(f32[4,7,128,256]{3,1,2,0:T(8,128)S(1)} %get-tuple-element.37, f32[4,1,128,256]{3,1,2,0:T(1,128)S(1)} %get-tuple-element.39, f32[4,1,128,256]{3,1,2,0:T(1,128)S(1)} %get-tuple-element.38, f32[4,7,128,256]{3,1,2,0:T(8,128)S(1)} %get-tuple-element.36), kind=kLoop, calls=%fused_computation.67 | loop fusion | flops 4194304 | bytes 12582912 | tf_op jit(solution)/shard_map/mul | solution.py:37
  18.7 1.6 %copy.56 = f32[8,128,256]{2,0,1:T(8,128)} copy(f32[8,128,256]{2,1,0:T(8,128)S(1)} %convert_element_type.3) | data formatting | bytes 2097152 | tf_op jit(solution)/shard_map/convert_element_type | solution.py:79
  20.4 0.6 dynamic-slice
  21.6 1.5 pad_maximum_fusion.1
  23.1 2.6 %fusion.51 = (f32[4,8,130,1]{3,1,2,0:T(8,128)}, f32[4,8,130,1]{3,1,2,0:T(8,128)}) fusion(f32[4,8,130,256]{3,1,2,0:T(8,128)S(1)} %pad_maximum_fusion.1), kind=kLoop, calls=%fused_computation.144 | loop fusion | bytes 66560 | tf_op jit(solution)/shard_map/slice | solution.py:21
  25.7 2.8 %copy.48 = f32[4,8,130,1]{2,1,3,0:T(8,128)S(1)} copy(f32[4,8,130,1]{3,1,2,0:T(8,128)} %get-tuple-element.29) | data formatting | bytes 33280 | tf_op jit(solution)/shard_map/slice | solution.py:22
  28.6 1.3 collective-permute-start.2
  29.9 2.8 %copy.50 = f32[4,8,130,1]{2,1,3,0:T(8,128)S(1)} copy(f32[4,8,130,1]{3,1,2,0:T(8,128)} %get-tuple-element.28) | data formatting | bytes 33280 | tf_op jit(solution)/shard_map/slice | solution.py:21
  32.7 4.7 %collective-permute-start.3 = (f32[4,8,130,1]{2,1,3,0:T(8,128)S(1)}, f32[4,8,130,1]{2,1,3,0:T(8,128)S(1)}, u32[]{:S(2)}, u32[]{:S(2)}) collective-permute-start(f32[4,8,130,1]{2,1,3,0:T(8,128)S(1)} %copy.50), channel_id=1, source_target_pairs={{0,8},{8,16},{16,24},{1,9},{9,17},{17,25},{2,10},{10,18},{18,26},{... | collective-permute-start | bytes 49928 | tf_op jit(solution)/shard_map/ppermute | solution.py:23
  37.5 3.5 %broadcast_multiply_fusion.2 = f32[4,8,128,256]{3,1,2,0:T(8,128)} fusion(f32[4,8,1,256]{3,1,2,0:T(8,128)S(1)} %collective-permute-done, f32[1,8,128,256]{3,1,2,0:T(8,128)S(1)} %get-tuple-element.53, f32[1,8,128,256]{3,1,2,0:T(8,128)} %copy-done.8, f32[1,8,128,256]{3,1,2,0:T(8,128)S(1)} %get-tuple-element.49, f32[1,8,128,256]{3,1,2,0:T(8,128)S(1)} %bitcast.36, ...), kind=kLoop, calls=%fused_computation.74 | loop fusion | flops 10485760 | bytes 8454144 | tf_op jit(solution)/shard_map/mul | solution.py:38
  41.0 2.6 %copy.49 = f32[4,8,130,1]{3,1,2,0:T(8,128)} copy(f32[4,8,130,1]{2,1,3,0:T(8,128)S(1)} %collective-permute-done.2) | data formatting | bytes 33280 | tf_op jit(solution)/shard_map/ppermute | solution.py:24
  43.5 2.6 %copy.51 = f32[4,8,130,1]{3,1,2,0:T(8,128)} copy(f32[4,8,130,1]{2,1,3,0:T(8,128)S(1)} %collective-permute-done.3) | data formatting | bytes 33280 | tf_op jit(solution)/shard_map/ppermute | solution.py:23
  46.1 9.7 %broadcast_multiply_fusion.1 = f32[4,8,128,256]{3,1,2,0:T(8,128)S(1)} fusion(f32[4,8,130,1]{3,1,2,0:T(8,128)} %copy.49, f32[4,8,1,256]{3,1,2,0:T(8,128)S(1)} %collective-permute-done, f32[1,8,128,256]{3,1,2,0:T(8,128)S(1)} %get-tuple-element.53, f32[1,8,128,256]{3,1,2,0:T(8,128)} %copy-done.8, f32[1,8,128,256]{3,1,2,0:T(8,128)S(1)} %get-tuple-element.49, ...), kind=kLoop, calls=%fused_computation.73 | loop fusion | flops 14680064 | bytes 8487424 | tf_op jit(solution)/shard_map/mul | solution.py:39
  55.9 1.9 %multiply_add_fusion.3 = (f32[1,8,128,256]{3,1,2,0:T(8,128)}, f32[1,8,128,256]{3,1,2,0:T(8,128)S(1)}) fusion(f32[4,8,128,256]{3,1,2,0:T(8,128)S(1)} %copy-done.24, f32[4,8,128,256]{3,1,2,0:T(8,128)S(1)} %broadcast_multiply_fusion.1, f32[4,8,128,256]{3,1,2,0:T(8,128)S(1)} %copy-done.22), kind=kLoop, calls=%fused_computation.130 | loop fusion | flops 4980736 | bytes 11534336 | tf_op jit(solution)/shard_map/add | solution.py:52
  58.0 0.8 copy-done.14
  58.8 1.3 copy-done.16
  60.0 0.6 copy-done.18
  60.8 11.1 %fusion.2 = f32[4,8,128,256]{3,1,2,0:T(8,128)S(1)} fusion(f32[1,8,128,256]{3,1,2,0:T(8,128)S(1)} %multiply_add_fusion.2, f32[1,8,128,256]{3,1,2,0:T(8,128)} %get-tuple-element.22, f32[4,7,128,256]{3,1,2,0:T(8,128)S(1)} %copy-done.16, f32[4,1,128,256]{3,1,2,0:T(1,128)S(1)} %copy-done.32, f32[4,1,128,256]{3,1,2,0:T(1,128)S(1)} %copy-done.30, ...), kind=kLoop, calls=%fused_computation.53 | loop fusion | flops 47185920 | bytes 22118912 | tf_op jit(solution)/shard_map/sub | solution.py:58
  72.2 1.0 copy-done.33
  73.2 0.7 fusion.31
  73.9 0.6 fusion.3
  74.6 1.9 %copy-done.17 = f32[4,8,128,256]{3,1,2,0:T(8,128)} copy-done((f32[4,8,128,256]{3,1,2,0:T(8,128)}, f32[4,8,128,256]{3,1,2,0:T(8,128)S(1)}, u32[]{:S(2)}) %copy-start.17) | copy-done | bytes 4194328
  76.5 0.3 slice_multiply_fusion.1
  76.8 3.8 %fusion = (f32[4,7,128,256]{3,1,2,0:T(8,128)}, f32[4,7,128,256]{3,1,2,0:T(8,128)}) fusion(f32[3,8,128,256]{3,1,2,0:T(8,128)S(1)} %slice_multiply_fusion.1, f32[1,8,128,256]{3,1,2,0:T(8,128)S(1)} %slice.267), kind=kLoop, calls=%fused_computation.15 | loop fusion | flops 1835008 | bytes 11534336 | tf_op jit(solution)/shard_map/concatenate | solution.py:64
  80.6 1.7 %fusion.17 = (f32[8,128,256]{2,0,1:T(8,128)}, f32[8,128,256]{2,0,1:T(8,128)}, f32[8,128,256]{2,0,1:T(8,128)}) fusion(f32[3,8,128,256]{3,1,2,0:T(8,128)S(1)} %slice_multiply_fusion.1), kind=kLoop, calls=%fused_computation.86 | loop fusion | flops 786432 | bytes 6291456 | tf_op jit(solution)/shard_map/mul | solution.py:43
  82.3 2.1 %collective-permute-start.4 = (f32[4,8,1,256]{3,1,2,0:T(8,128)S(1)}, f32[4,8,1,256]{3,1,2,0:T(8,128)S(1)}, u32[]{:S(2)}, u32[]{:S(2)}) collective-permute-start(f32[4,8,1,256]{3,1,2,0:T(8,128)S(1)} %get-tuple-element.35), channel_id=1, source_target_pairs={{1,0},{2,1},{3,2},{4,3},{5,4},{6,5},{7,6},{0,7},{9,8},{10,9},{11,1... | collective-permute-start | bytes 98312 | tf_op jit(solution)/shard_map/ppermute | solution.py:24
  84.4 1.5 fusion.44
  86.0 2.6 %collective-permute-done.5 = f32[4,8,1,256]{3,1,2,0:T(8,128)S(1)} collective-permute-done((f32[4,8,1,256]{3,1,2,0:T(8,128)S(1)}, f32[4,8,1,256]{3,1,2,0:T(8,128)S(1)}, u32[]{:S(2)}, u32[]{:S(2)}) %collective-permute-start.5) | collective-permute-done | bytes 32800 | tf_op jit(solution)/shard_map/ppermute | solution.py:23
  88.7 0.3 pad_maximum_fusion.2
  89.0 2.6 %fusion.50 = (f32[4,8,130,1]{3,1,2,0:T(8,128)}, f32[4,8,130,1]{3,1,2,0:T(8,128)}) fusion(f32[4,8,130,256]{3,1,2,0:T(8,128)S(1)} %pad_maximum_fusion.2), kind=kLoop, calls=%fused_computation.143 | loop fusion | bytes 66560 | tf_op jit(solution)/shard_map/slice | solution.py:21
  91.6 2.8 %copy.57 = f32[4,8,130,1]{2,1,3,0:T(8,128)S(1)} copy(f32[4,8,130,1]{3,1,2,0:T(8,128)} %get-tuple-element.27) | data formatting | bytes 33280 | tf_op jit(solution)/shard_map/slice | solution.py:22
  94.4 1.5 collective-permute-start.6
  95.9 2.8 %copy.59 = f32[4,8,130,1]{2,1,3,0:T(8,128)S(1)} copy(f32[4,8,130,1]{3,1,2,0:T(8,128)} %get-tuple-element.26) | data formatting | bytes 33280 | tf_op jit(solution)/shard_map/slice | solution.py:21
  98.8 4.5 %collective-permute-start.7 = (f32[4,8,130,1]{2,1,3,0:T(8,128)S(1)}, f32[4,8,130,1]{2,1,3,0:T(8,128)S(1)}, u32[]{:S(2)}, u32[]{:S(2)}) collective-permute-start(f32[4,8,130,1]{2,1,3,0:T(8,128)S(1)} %copy.59), channel_id=1, source_target_pairs={{0,8},{8,16},{16,24},{1,9},{9,17},{17,25},{2,10},{10,18},{18,26},{... | collective-permute-start | bytes 49928 | tf_op jit(solution)/shard_map/ppermute | solution.py:23
  103.3 7.5 %fusion.9 = f32[4,8,128,256]{3,1,2,0:T(8,128)} fusion(f32[4,7,128,256]{3,1,2,0:T(8,128)} %get-tuple-element.31, f32[4,1,128,256]{3,1,2,0:T(1,128)} %get-tuple-element.33, f32[4,1,128,256]{3,1,2,0:T(1,128)} %get-tuple-element.32, f32[4,7,128,256]{3,1,2,0:T(8,128)} %get-tuple-element.30), kind=kLoop, calls=%fused_computation.65 | loop fusion | flops 4194304 | bytes 12582912 | tf_op jit(solution)/shard_map/mul | solution.py:37
  110.8 2.6 %copy.58 = f32[4,8,130,1]{3,1,2,0:T(8,128)} copy(f32[4,8,130,1]{2,1,3,0:T(8,128)S(1)} %collective-permute-done.6) | data formatting | bytes 33280 | tf_op jit(solution)/shard_map/ppermute | solution.py:24
  113.4 2.6 %copy.60 = f32[4,8,130,1]{3,1,2,0:T(8,128)} copy(f32[4,8,130,1]{2,1,3,0:T(8,128)S(1)} %collective-permute-done.7) | data formatting | bytes 33280 | tf_op jit(solution)/shard_map/ppermute | solution.py:23
  116.0 10.3 %broadcast_multiply_fusion = (f32[4,8,128,256]{3,1,2,0:T(8,128)S(1)}, f32[4,8,128,256]{3,1,2,0:T(8,128)}) fusion(f32[4,8,130,1]{3,1,2,0:T(8,128)} %copy.58, f32[4,8,1,256]{3,1,2,0:T(8,128)S(1)} %collective-permute-done.4, f32[3,8,128,256]{3,1,2,0:T(8,128)S(1)} %slice_multiply_fusion.1, f32[1,8,128,256]{3,1,2,0:T(8,128)} %copy-done, ...), kind=kLoop, calls=%fused_computation.72 | loop fusion | flops 16777216 | bytes 12681728 | tf_op jit(solution)/shard_map/mul | solution.py:39
  126.4 3.9 %multiply_add_fusion.1 = (f32[1,8,128,256]{3,1,2,0:T(8,128)}, f32[1,8,128,256]{3,1,2,0:T(8,128)S(1)}) fusion(f32[4,8,128,256]{3,1,2,0:T(8,128)} %get-tuple-element.25, f32[4,8,128,256]{3,1,2,0:T(8,128)S(1)} %get-tuple-element.24, f32[4,8,128,256]{3,1,2,0:T(8,128)S(1)} %copy-done.23), kind=kLoop, calls=%fused_computation.128 | loop fusion | flops 4980736 | bytes 11534336 | tf_op jit(solution)/shard_map/add | solution.py:52
  130.4 1.0 copy-done.12
  131.4 0.6 copy-done.20
  132.2 9.6 %fusion.4 = f32[4,8,128,256]{3,1,2,0:T(8,128)S(1)} fusion(f32[1,8,128,256]{3,1,2,0:T(8,128)S(1)} %multiply_add_fusion, f32[1,8,128,256]{3,1,2,0:T(8,128)} %get-tuple-element.20, f32[3,8,128,256]{3,1,2,0:T(8,128)S(1)} %slice_multiply_fusion.1, f32[1,8,128,256]{3,1,2,0:T(8,128)S(1)} %copy-done.1, f32[4,7,128,256]{3,1,2,0:T(8,128)S(1)} %copy-done.12, ...), kind=kLoop, calls=%fused_computation.59 | loop fusion | flops 36700160 | bytes 22118912 | tf_op jit(solution)/shard_map/sub | solution.py:58
  142.0 1.5 slice_add_fusion
  143.6 0.3 copy-done.7
  143.9 0.3 copy-done.10
  144.3 0.8 fusion.7
  145.1 0.4 copy-done.26
  145.5 0.3 slice_multiply_fusion
  145.8 0.3 multiply_reduce_fusion
  146.1 0.2 slice_bitcast_fusion
  146.3 1.3 copy.63
  147.6 1.3 copy.64
  148.9 1.3 copy.65
  150.2 1.3 copy.62
  151.5 9.9 %all-reduce = f32[8,128]{1,0:T(8,128)S(1)} all-reduce(f32[8,128]{1,0:T(8,128)S(1)} %copy.61), channel_id=2, replica_groups=mesh['gz'=4,'gy'=8] {'gz'}, use_global_device_ids=true, to_apply=%region_1.2.clone | all-reduce | flops 1024 | bytes 8192
  161.5 0.6 dynamic-slice_multiply_fusion
  (84 shorter events, 1.6 us)
Async XLA Ops:
  0.6 5.3 %copy-start.36 = (f32[8,128,256]{2,1,0:T(8,128)S(1)}, f32[8,128,256]{2,1,0:T(8,128)}, u32[]{:S(2)}) copy-start(f32[8,128,256]{2,1,0:T(8,128)} %param.7) | copy-start | bytes 3145732
  0.6 5.3 %copy-start.35 = (f32[8,128,256]{2,1,0:T(8,128)S(1)}, f32[8,128,256]{2,1,0:T(8,128)}, u32[]{:S(2)}) copy-start(f32[8,128,256]{2,1,0:T(8,128)} %param.8) | copy-start | bytes 3145732
  3.7 70.2 %copy-start.2 = (f32[1,8,128,256]{3,1,2,0:T(8,128)}, f32[1,8,128,256]{3,1,2,0:T(8,128)S(1)}, u32[]{:S(2)}) copy-start(f32[1,8,128,256]{3,1,2,0:T(8,128)S(1)} %get-tuple-element.49) | copy-start | bytes 3145732
  5.9 68.0 %copy-start.4 = (f32[8,128,256]{2,0,1:T(8,128)}, f32[8,128,256]{2,0,1:T(8,128)S(1)}, u32[]{:S(2)}) copy-start(f32[8,128,256]{2,0,1:T(8,128)S(1)} %copy.74) | copy-start | bytes 3145732
  8.6 1.0 copy-start.8
  8.6 65.3 %copy-start.6 = (f32[1,8,128,256]{3,1,2,0:T(8,128)}, f32[1,8,128,256]{3,1,2,0:T(8,128)S(1)}, u32[]{:S(2)}) copy-start(f32[1,8,128,256]{3,1,2,0:T(8,128)S(1)} %get-tuple-element.53) | copy-start | bytes 3145732
  9.6 12.0 %collective-permute-start = (f32[4,8,1,256]{3,1,2,0:T(8,128)S(1)}, f32[4,8,1,256]{3,1,2,0:T(8,128)S(1)}, u32[]{:S(2)}, u32[]{:S(2)}) collective-permute-start(f32[4,8,1,256]{3,1,2,0:T(8,128)S(1)} %get-tuple-element.41), channel_id=1, source_target_pairs={{1,0},{2,1},{3,2},{4,3},{5,4},{6,5},{7,6},{0,7},{9,8},{10,9},{11,1... | collective-permute-start | bytes 98312 | tf_op jit(solution)/shard_map/ppermute | solution.py:24
  12.9 8.7 %collective-permute-start.1 = (f32[4,8,1,256]{3,1,2,0:T(8,128)S(1)}, f32[4,8,1,256]{3,1,2,0:T(8,128)S(1)}, u32[]{:S(2)}, u32[]{:S(2)}) collective-permute-start(f32[4,8,1,256]{3,1,2,0:T(8,128)S(1)} %get-tuple-element.40), channel_id=1, source_target_pairs={{0,1},{1,2},{2,3},{3,4},{4,5},{5,6},{6,7},{7,0},{8,9},{9,10},{10,1... | collective-permute-start | bytes 98312 | tf_op jit(solution)/shard_map/ppermute | solution.py:23
  13.7 4.9 %copy-start.13 = (f32[4,7,128,256]{3,1,2,0:T(8,128)}, f32[4,7,128,256]{3,1,2,0:T(8,128)S(1)}, u32[]{:S(2)}) copy-start(f32[4,7,128,256]{3,1,2,0:T(8,128)S(1)} %get-tuple-element.36) | copy-start | bytes 11010052
  13.7 4.9 %copy-start.15 = (f32[4,7,128,256]{3,1,2,0:T(8,128)}, f32[4,7,128,256]{3,1,2,0:T(8,128)S(1)}, u32[]{:S(2)}) copy-start(f32[4,7,128,256]{3,1,2,0:T(8,128)S(1)} %get-tuple-element.37) | copy-start | bytes 11010052
  14.4 4.2 %copy-start.29 = (f32[4,1,128,256]{3,1,2,0:T(1,128)}, f32[4,1,128,256]{3,1,2,0:T(1,128)S(1)}, u32[]{:S(2)}) copy-start(f32[4,1,128,256]{3,1,2,0:T(1,128)S(1)} %get-tuple-element.38) | copy-start | bytes 1572868
  14.4 4.2 %copy-start.31 = (f32[4,1,128,256]{3,1,2,0:T(1,128)}, f32[4,1,128,256]{3,1,2,0:T(1,128)S(1)}, u32[]{:S(2)}) copy-start(f32[4,1,128,256]{3,1,2,0:T(1,128)S(1)} %get-tuple-element.39) | copy-start | bytes 1572868
  14.4 4.2 %copy-start.34 = (s32[8,128,256]{2,1,0:T(8,128)S(1)}, s32[8,128,256]{2,1,0:T(8,128)}, u32[]{:S(2)}) copy-start(s32[8,128,256]{2,1,0:T(8,128)} %param.9) | copy-start | bytes 3145732
  18.6 1.8 %copy-start.37 = (u32[32]{0:T(128)S(1)}, u32[32]{0:T(128)}, u32[]{:S(2)}) copy-start(u32[32]{0:T(128)} %constant.33) | copy-start | bytes 388
  28.6 12.4 %collective-permute-start.2 = (f32[4,8,130,1]{2,1,3,0:T(8,128)S(1)}, f32[4,8,130,1]{2,1,3,0:T(8,128)S(1)}, u32[]{:S(2)}, u32[]{:S(2)}) collective-permute-start(f32[4,8,130,1]{2,1,3,0:T(8,128)S(1)} %copy.48), channel_id=1, source_target_pairs={{8,0},{16,8},{24,16},{9,1},{17,9},{25,17},{10,2},{18,10},{26,18},{... | collective-permute-start | bytes 49928 | tf_op jit(solution)/shard_map/ppermute | solution.py:24
  32.7 10.8 %collective-permute-start.3 = (f32[4,8,130,1]{2,1,3,0:T(8,128)S(1)}, f32[4,8,130,1]{2,1,3,0:T(8,128)S(1)}, u32[]{:S(2)}, u32[]{:S(2)}) collective-permute-start(f32[4,8,130,1]{2,1,3,0:T(8,128)S(1)} %copy.50), channel_id=1, source_target_pairs={{0,8},{8,16},{16,24},{1,9},{9,17},{17,25},{2,10},{10,18},{18,26},{... | collective-permute-start | bytes 49928 | tf_op jit(solution)/shard_map/ppermute | solution.py:23
  46.1 9.7 %copy-start.22 = (f32[4,8,128,256]{3,1,2,0:T(8,128)S(1)}, f32[4,8,128,256]{3,1,2,0:T(8,128)}, u32[]{:S(2)}) copy-start(f32[4,8,128,256]{3,1,2,0:T(8,128)} %fusion.11) | copy-start | bytes 12582916
  46.1 9.7 %copy-start.24 = (f32[4,8,128,256]{3,1,2,0:T(8,128)S(1)}, f32[4,8,128,256]{3,1,2,0:T(8,128)}, u32[]{:S(2)}) copy-start(f32[4,8,128,256]{3,1,2,0:T(8,128)} %broadcast_multiply_fusion.2) | copy-start | bytes 12582916
  46.1 11.8 %copy-start.19 = (f32[4,8,130,1]{3,1,2,0:T(8,128)S(1)}, f32[4,8,130,1]{3,1,2,0:T(8,128)}, u32[]{:S(2)}) copy-start(f32[4,8,130,1]{3,1,2,0:T(8,128)} %copy.51) | copy-start | bytes 49924
  55.9 2.1 %copy-start.9 = (f32[1,8,128,256]{3,1,2,0:T(8,128)S(1)}, f32[1,8,128,256]{3,1,2,0:T(8,128)}, u32[]{:S(2)}) copy-start(f32[1,8,128,256]{3,1,2,0:T(8,128)} %copy-done.8) | copy-start | bytes 3145732
  55.9 2.9 %copy-start.14 = (f32[4,7,128,256]{3,1,2,0:T(8,128)S(1)}, f32[4,7,128,256]{3,1,2,0:T(8,128)}, u32[]{:S(2)}) copy-start(f32[4,7,128,256]{3,1,2,0:T(8,128)} %copy-done.13) | copy-start | bytes 11010052
  55.9 4.1 %copy-start.16 = (f32[4,7,128,256]{3,1,2,0:T(8,128)S(1)}, f32[4,7,128,256]{3,1,2,0:T(8,128)}, u32[]{:S(2)}) copy-start(f32[4,7,128,256]{3,1,2,0:T(8,128)} %copy-done.15) | copy-start | bytes 11010052
  55.9 4.7 %copy-start.18 = (f32[4,8,130,1]{3,1,2,0:T(8,128)S(1)}, f32[4,8,130,1]{3,1,2,0:T(8,128)}, u32[]{:S(2)}) copy-start(f32[4,8,130,1]{3,1,2,0:T(8,128)} %copy.49) | copy-start | bytes 49924
  55.9 4.7 %copy-start.30 = (f32[4,1,128,256]{3,1,2,0:T(1,128)S(1)}, f32[4,1,128,256]{3,1,2,0:T(1,128)}, u32[]{:S(2)}) copy-start(f32[4,1,128,256]{3,1,2,0:T(1,128)} %copy-done.29) | copy-start | bytes 1572868
  55.9 4.9 %copy-start.32 = (f32[4,1,128,256]{3,1,2,0:T(1,128)S(1)}, f32[4,1,128,256]{3,1,2,0:T(1,128)}, u32[]{:S(2)}) copy-start(f32[4,1,128,256]{3,1,2,0:T(1,128)} %copy-done.31) | copy-start | bytes 1572868
  71.9 1.2 copy-start.33
  73.9 2.6 %copy-start.25 = (f32[8,128,256]{2,0,1:T(8,128)S(1)}, f32[8,128,256]{2,0,1:T(8,128)}, u32[]{:S(2)}) copy-start(f32[8,128,256]{2,0,1:T(8,128)} %copy.56) | copy-start | bytes 3145732
  74.5 2.0 %copy-start.17 = (f32[4,8,128,256]{3,1,2,0:T(8,128)}, f32[4,8,128,256]{3,1,2,0:T(8,128)S(1)}, u32[]{:S(2)}) copy-start(f32[4,8,128,256]{3,1,2,0:T(8,128)S(1)} %fusion.3) | copy-start | bytes 12582916
  76.5 12.2 %copy-start = (f32[1,8,128,256]{3,1,2,0:T(8,128)}, f32[1,8,128,256]{3,1,2,0:T(8,128)S(1)}, u32[]{:S(2)}) copy-start(f32[1,8,128,256]{3,1,2,0:T(8,128)S(1)} %slice.267) | copy-start | bytes 3145732
  82.3 3.7 %collective-permute-start.4 = (f32[4,8,1,256]{3,1,2,0:T(8,128)S(1)}, f32[4,8,1,256]{3,1,2,0:T(8,128)S(1)}, u32[]{:S(2)}, u32[]{:S(2)}) collective-permute-start(f32[4,8,1,256]{3,1,2,0:T(8,128)S(1)} %get-tuple-element.35), channel_id=1, source_target_pairs={{1,0},{2,1},{3,2},{4,3},{5,4},{6,5},{7,6},{0,7},{9,8},{10,9},{11,1... | collective-permute-start | bytes 98312 | tf_op jit(solution)/shard_map/ppermute | solution.py:24
  84.4 4.2 %collective-permute-start.5 = (f32[4,8,1,256]{3,1,2,0:T(8,128)S(1)}, f32[4,8,1,256]{3,1,2,0:T(8,128)S(1)}, u32[]{:S(2)}, u32[]{:S(2)}) collective-permute-start(f32[4,8,1,256]{3,1,2,0:T(8,128)S(1)} %get-tuple-element.34), channel_id=1, source_target_pairs={{0,1},{1,2},{2,3},{3,4},{4,5},{5,6},{6,7},{7,0},{8,9},{9,10},{10,1... | collective-permute-start | bytes 98312 | tf_op jit(solution)/shard_map/ppermute | solution.py:23
  94.4 16.4 %collective-permute-start.6 = (f32[4,8,130,1]{2,1,3,0:T(8,128)S(1)}, f32[4,8,130,1]{2,1,3,0:T(8,128)S(1)}, u32[]{:S(2)}, u32[]{:S(2)}) collective-permute-start(f32[4,8,130,1]{2,1,3,0:T(8,128)S(1)} %copy.57), channel_id=1, source_target_pairs={{8,0},{16,8},{24,16},{9,1},{17,9},{25,17},{10,2},{18,10},{26,18},{... | collective-permute-start | bytes 49928 | tf_op jit(solution)/shard_map/ppermute | solution.py:24
  98.8 14.6 %collective-permute-start.7 = (f32[4,8,130,1]{2,1,3,0:T(8,128)S(1)}, f32[4,8,130,1]{2,1,3,0:T(8,128)S(1)}, u32[]{:S(2)}, u32[]{:S(2)}) collective-permute-start(f32[4,8,130,1]{2,1,3,0:T(8,128)S(1)} %copy.59), channel_id=1, source_target_pairs={{0,8},{8,16},{16,24},{1,9},{9,17},{17,25},{2,10},{10,18},{18,26},{... | collective-permute-start | bytes 49928 | tf_op jit(solution)/shard_map/ppermute | solution.py:23
  116.0 10.3 %copy-start.23 = (f32[4,8,128,256]{3,1,2,0:T(8,128)S(1)}, f32[4,8,128,256]{3,1,2,0:T(8,128)}, u32[]{:S(2)}) copy-start(f32[4,8,128,256]{3,1,2,0:T(8,128)} %fusion.9) | copy-start | bytes 12582916
  116.0 14.4 %copy-start.21 = (f32[4,8,130,1]{3,1,2,0:T(8,128)S(1)}, f32[4,8,130,1]{3,1,2,0:T(8,128)}, u32[]{:S(2)}) copy-start(f32[4,8,130,1]{3,1,2,0:T(8,128)} %copy.60) | copy-start | bytes 49924
  126.3 4.1 %copy-start.1 = (f32[1,8,128,256]{3,1,2,0:T(8,128)S(1)}, f32[1,8,128,256]{3,1,2,0:T(8,128)}, u32[]{:S(2)}) copy-start(f32[1,8,128,256]{3,1,2,0:T(8,128)} %copy-done) | copy-start | bytes 3145732
  126.3 4.1 %copy-start.11 = (f32[4,7,128,256]{3,1,2,0:T(8,128)S(1)}, f32[4,7,128,256]{3,1,2,0:T(8,128)}, u32[]{:S(2)}) copy-start(f32[4,7,128,256]{3,1,2,0:T(8,128)} %get-tuple-element.30) | copy-start | bytes 11010052
  126.3 5.1 %copy-start.12 = (f32[4,7,128,256]{3,1,2,0:T(8,128)S(1)}, f32[4,7,128,256]{3,1,2,0:T(8,128)}, u32[]{:S(2)}) copy-start(f32[4,7,128,256]{3,1,2,0:T(8,128)} %get-tuple-element.31) | copy-start | bytes 11010052
  126.3 5.7 %copy-start.20 = (f32[4,8,130,1]{3,1,2,0:T(8,128)S(1)}, f32[4,8,130,1]{3,1,2,0:T(8,128)}, u32[]{:S(2)}) copy-start(f32[4,8,130,1]{3,1,2,0:T(8,128)} %copy.58) | copy-start | bytes 49924
  126.3 5.7 %copy-start.27 = (f32[4,1,128,256]{3,1,2,0:T(1,128)S(1)}, f32[4,1,128,256]{3,1,2,0:T(1,128)}, u32[]{:S(2)}) copy-start(f32[4,1,128,256]{3,1,2,0:T(1,128)} %get-tuple-element.32) | copy-start | bytes 1572868
  126.3 5.8 %copy-start.28 = (f32[4,1,128,256]{3,1,2,0:T(1,128)S(1)}, f32[4,1,128,256]{3,1,2,0:T(1,128)}, u32[]{:S(2)}) copy-start(f32[4,1,128,256]{3,1,2,0:T(1,128)} %get-tuple-element.33) | copy-start | bytes 1572868
  141.8 1.8 %copy-start.3 = (f32[1,8,128,256]{3,1,2,0:T(8,128)S(1)}, f32[1,8,128,256]{3,1,2,0:T(8,128)}, u32[]{:S(2)}) copy-start(f32[1,8,128,256]{3,1,2,0:T(8,128)} %copy-done.2) | copy-start | bytes 3145732
  141.8 1.8 %copy-start.5 = (f32[8,128,256]{2,0,1:T(8,128)S(1)}, f32[8,128,256]{2,0,1:T(8,128)}, u32[]{:S(2)}) copy-start(f32[8,128,256]{2,0,1:T(8,128)} %copy-done.4) | copy-start | bytes 3145732
  141.8 2.2 %copy-start.7 = (f32[1,8,128,256]{3,1,2,0:T(8,128)S(1)}, f32[1,8,128,256]{3,1,2,0:T(8,128)}, u32[]{:S(2)}) copy-start(f32[1,8,128,256]{3,1,2,0:T(8,128)} %copy-done.6) | copy-start | bytes 3145732
  141.8 2.5 %copy-start.10 = (f32[1,8,128,256]{3,1,2,0:T(8,128)S(1)}, f32[1,8,128,256]{3,1,2,0:T(8,128)}, u32[]{:S(2)}) copy-start(f32[1,8,128,256]{3,1,2,0:T(8,128)} %copy-done.8) | copy-start | bytes 3145732
  144.3 1.2 copy-start.26
where the time goes:
time: 163 us; the launch traced here: 162 us
  other arithmetic  81.9 us (50%)
  local copies, waits for them, and re-layouts  48.2 us (30%)
  starting transfers between devices  17.5 us (11%)
  blocking collectives  9.94 us (6%)
  waiting for transfers between devices  2.7 us (2%)
  between operations  1.85 us (1%)
    sub x2, other arithmetic, tendencies(): tendency = diffusion * laplace - advect  20.7 us
    mul x2, other arithmetic, tendencies(): grad_z = 0.5 * (upper_side - lower_side)  20 us
    unnamed x82, local copies, waits for them, and re-layouts  17.3 us
    mul x2, other arithmetic, tendencies(): grad_x = 0.5 * (east_side - west_side)  11.7 us
    slice x5, local copies, waits for them, and re-layouts, extended(): last = lax.slice_in_dim(shard, length - width, length, axis=dim)  10.9 us
    unnamed x1, blocking collectives  9.94 us
    ppermute x4, starting transfers between devices, extended(): before = lax.ppermute(last, axis, up)  9.28 us
    ppermute x4, starting transfers between devices, extended(): after = lax.ppermute(first, axis, down)  8.22 us
  transfers between devices with their start and end apart: 8, of which 1 were waited for; matrix products, arithmetic and copies ran while one was open for 19% of the time, Pallas kernels for 0%

commit v1 on v0

v1 whole, which is shorter than its diff:
```python
import functools
import math

import jax
import jax.numpy as jnp
from jax import lax
from jax.experimental import pallas as pl
from jax.experimental.pallas import tpu as pltpu
from jax.sharding import PartitionSpec as P

TIME_STEP = 0.1
NU_BASE = 0.05
KAPPA_BASE = 0.05
SMAG_COEF = 0.03
PRANDTL = 0.4
BUOYANCY = 0.5
LANES = 128
PAD = 8
LIMIT = 16 << 20
HBM = pl.BlockSpec(memory_space=pltpu.HBM)
VMEM = pl.BlockSpec(memory_space=pltpu.VMEM)


def lane_iota():
    return lax.broadcasted_iota(jnp.int32, (8, LANES), 1)


def stepped(base, c, e, w, n, s, u, l, scale):
    h = TIME_STEP * scale
    dx = [a - b for a, b in zip(e, w)]
    dy = [a - b for a, b in zip(n, s)]
    dz = [a - b for a, b in zip(u, l)]
    lap = [
        ((a + b) + (p + q)) + ((r + t) - 6.0 * m)
        for a, b, p, q, r, t, m in zip(e, w, n, s, u, l, c)
    ]
    straight = dx[1] * dx[1] + dy[2] * dy[2] + dz[3] * dz[3]
    shear_a = dy[1] + dx[2]
    shear_b = dz[1] + dx[3]
    shear_c = dz[2] + dy[3]
    shear = shear_a * shear_a + shear_b * shear_b + shear_c * shear_c
    k = (SMAG_COEF * h) ** 2
    arg = (straight + straight + shear) * (0.25 * k) + 0.01 * k
    eddy = arg * lax.rsqrt(arg)
    c_mom = eddy + NU_BASE * h
    c_heat = eddy * (1.0 / PRANDTL) + KAPPA_BASE * h
    vel = [(0.5 * h) * q for q in c[1:]]
    out = []
    for i in range(4):
        coef = c_heat if i == 0 else c_mom
        adv = vel[0] * dx[i] + vel[1] * dy[i] + vel[2] * dz[i]
        out.append((base[i] + coef * lap[i]) - adv)
    out[3] = out[3] + (BUOYANCY * h) * c[0]
    return out


def lane_next(blocks, lane):
    r = [pltpu.roll(b, LANES - 1, 1) for b in blocks]
    if len(r) == 1:
        return r
    return [jnp.where(lane == LANES - 1, r[(i + 1) % len(r)], r[i]) for i in range(len(r))]


def lane_prev(blocks, lane):
    r = [pltpu.roll(b, 1, 1) for b in blocks]
    if len(r) == 1:
        return r
    return [jnp.where(lane == 0, r[i - 1], r[i]) for i in range(len(r))]


def height_pair(blocks, lane):
    count = len(blocks)
    up = [pltpu.roll(b, LANES - 1, 1) for b in blocks]
    lo = [pltpu.roll(b, 1, 1) for b in blocks]
    upper = [
        up[i] if i == count - 1 else jnp.where(lane == LANES - 1, up[i + 1], up[i])
        for i in range(count)
    ]
    lower = [lo[i] if i == 0 else jnp.where(lane == 0, lo[i - 1], lo[i]) for i in range(count)]
    return upper, lower


def east(q):
    return pltpu.roll(q, 7, 0)


def west(q):
    return pltpu.roll(q, 1, 0)


def flat(ref):
    return ref.reshape(math.prod(ref.shape[:-1]), LANES)


def row_of(ref, lead, x_stride, start, x):
    return ref[pl.ds(lead + start, x, stride=x_stride), :]


def pack_kernel(dims, *refs):
    x_n, h_n, ny = dims
    ins = refs[:5]
    s0, mk, ys_a, ys_b, zown, part, turned, sem = refs[5:]
    nyp = ny + 2 * PAD
    lane = lane_iota()
    copies = []
    for f in range(5):
        for h in range(h_n):
            dst = s0.at[f] if f < 4 else mk
            copies.append(
                pltpu.make_async_copy(
                    ins[f].at[:, :, pl.ds(h * LANES, LANES)],
                    dst.at[:, h, pl.ds(PAD, ny), :],
                    sem.at[f, h],
                )
            )
    for c in copies:
        c.start()
    for c in copies:
        c.wait()
    even = lax.rem(lax.axis_index("gy"), 2) == 0
    s0_flat, mk_flat = flat(s0), flat(mk)
    stride = h_n * nyp

    def rows(dst, ys):
        for r, y in enumerate(ys):
            for h in range(h_n):
                cols = slice(h * LANES, (h + 1) * LANES)
                for f in range(4):
                    block = row_of(s0_flat, (f * x_n * h_n + h) * nyp, stride, PAD + y, x_n)
                    dst[(r * 4 + f) * 8 : (r * 4 + f) * 8 + 8, cols] = block
                if r == 0:
                    block = row_of(mk_flat, h * nyp, stride, PAD + y, x_n)
                    dst[64:72, cols] = block.astype(jnp.float32)

    first, last = (0, 1), (ny - 1, ny - 2)

    @pl.when(even)
    def _():
        rows(ys_a, last)
        rows(ys_b, first)

    @pl.when(jnp.logical_not(even))
    def _():
        rows(ys_a, first)
        rows(ys_b, last)

    group = lane // 8

    def tile(t, carry):
        y = pl.multiple_of(PAD + t * 8, 8)
        yo = pl.multiple_of(t * 8, 8)
        for a in range(3):
            acc = jnp.zeros((8, LANES), jnp.float32)
            for g in range(16 if a < 2 else 8):
                f, x = a * 2 + g // 8, g % 8
                if a < 2:
                    lo, hi = s0[f, x, 0, pl.ds(y, 8), :], s0[f, x, h_n - 1, pl.ds(y, 8), :]
                else:
                    lo, hi = mk[x, 0, pl.ds(y, 8), :], mk[x, h_n - 1, pl.ds(y, 8), :]
                both = jnp.where(lane < LANES // 2, lo, hi).astype(jnp.float32)
                acc = jnp.where(group == g, pltpu.roll(both, (g * 8 + 4) % LANES, 1), acc)
            part[a, pl.ds(yo, 8), :] = acc
        return carry

    lax.fori_loop(0, ny // 8, tile, 0, unroll=2)
    for a in range(3):
        for b in range(ny // LANES):
            cols = slice(b * LANES, (b + 1) * LANES)
            turned[a, b] = part[a, cols, :].T
    for side in range(2):
        for l in range(4):
            j = 4 + l if side == 0 else 3 - l
            for b in range(ny // LANES):
                cols = slice(b * LANES, (b + 1) * LANES)
                for f in range(4):
                    k = f * 4 + l
                    zown[side, k * 8 : k * 8 + 8, cols] = turned[
                        f // 2, b, pl.ds((f % 2) * 64 + j, 8, stride=8), :
                    ]
                if l < 3:
                    k = 16 + l
                    zown[side, k * 8 : k * 8 + 8, cols] = turned[2, b, pl.ds(j, 8, stride=8), :]


def y_halo(even, a_ref, b_ref, k, cols):
    a, b = a_ref[k * 8 : k * 8 + 8, cols], b_ref[k * 8 : k * 8 + 8, cols]
    return jnp.where(even, b, a), jnp.where(even, a, b)


def beyond(lane, even, ya, yb, h_n, side, f, l, rows):
    h = 0 if side == 0 else h_n - 1
    at = l if side == 0 else LANES - 1 - l
    out = jnp.zeros((8, LANES), jnp.float32)
    for r in rows:
        k = r * 4 + f if f < 4 else 8
        before, after = y_halo(even, ya, yb, k, slice(h * LANES, (h + 1) * LANES))
        out = jnp.where(
            lane == LANES - 1 - r, pltpu.roll(before, (LANES - 1 - r - at) % LANES, 1), out
        )
        out = jnp.where(lane == r, pltpu.roll(after, (r - at) % LANES, 1), out)
    return out


def corner_kernel(dims, ya, yb, zown, zs_a, zs_b):
    x_n, h_n, ny = dims
    lane = lane_iota()
    even = lax.rem(lax.axis_index("gy"), 2) == 0
    even_z = lax.rem(lax.axis_index("gz"), 2) == 0

    def strip(dst, side):
        for l in range(2):
            for f in range(4):
                k, m = l * 4 + f, f * 4 + l
                dst[k * 8 : k * 8 + 8, :] = zown[side, m * 8 : m * 8 + 8, :]
        dst[64:72, :] = zown[side, 128:136, :]
        for f in range(4):
            dst[72 + f * 8 : 80 + f * 8, 0:LANES] = beyond(
                lane, even, ya, yb, h_n, side, f, 0, (0,)
            )
            if ny > LANES:
                dst[72 + f * 8 : 80 + f * 8, LANES:] = jnp.zeros((8, ny - LANES), jnp.float32)

    @pl.when(even_z)
    def _():
        strip(zs_a, 1)
        strip(zs_b, 0)

    @pl.when(jnp.logical_not(even_z))
    def _():
        strip(zs_a, 0)
        strip(zs_b, 1)


def load4(ref, x, h, y):
    return [ref[f, x, h, pl.ds(y, 8), :] for f in range(4)]


def section_one_kernel(dims, s0, mk, s1):
    x_n, h_n, ny = dims
    lane = lane_iota()

    def tile(y, x):
        c = [load4(s0, x, h, y) for h in range(h_n)]
        pairs = [height_pair([c[h][f] for h in range(h_n)], lane) for f in range(4)]
        for h in range(h_n):
            r = stepped(
                c[h],
                c[h],
                load4(s0, (x + 1) % x_n, h, y),
                load4(s0, (x - 1) % x_n, h, y),
                load4(s0, x, h, y + 1),
                load4(s0, x, h, y - 1),
                [p[0][h] for p in pairs],
                [p[1][h] for p in pairs],
                1.0,
            )
            open_cell = mk[x, h, pl.ds(y, 8), :] != 0
            s1[0, x, h, pl.ds(y, 8), :] = r[0]
            for f in range(1, 4):
                s1[f, x, h, pl.ds(y, 8), :] = jnp.where(open_cell, r[f], 0.0)

    def body(t, carry):
        for j in range(2):
            y = pl.multiple_of(PAD + t * 16 + j * 8, 8)
            for x in range(x_n):
                tile(y, x)
        return carry

    lax.fori_loop(0, ny // 16, body, 0)


def section_two_kernel(dims, s0, mk, s1, s2, path, acc):
    x_n, h_n, ny = dims
    lane = lane_iota()

    def tile(y, yo, x):
        c = [load4(s1, x, h, y) for h in range(h_n)]
        pairs = [height_pair([c[h][f] for h in range(h_n)], lane) for f in range(4)]
        total = None
        for h in range(h_n):
            start = load4(s0, x, h, y)
            r = stepped(
                [0.5 * (a + b) for a, b in zip(start, c[h])],
                c[h],
                load4(s1, (x + 1) % x_n, h, y),
                load4(s1, (x - 1) % x_n, h, y),
                load4(s1, x, h, y + 1),
                load4(s1, x, h, y - 1),
                [p[0][h] for p in pairs],
                [p[1][h] for p in pairs],
                0.5,
            )
            open_cell = mk[x, h, pl.ds(y, 8), :] != 0
            cols = slice(h * LANES, (h + 1) * LANES)
            s2[0, x, pl.ds(yo, 8), cols] = r[0]
            for f in range(1, 4):
                s2[f, x, pl.ds(yo, 8), cols] = jnp.where(open_cell, r[f], 0.0)
            refr = 1.0 - jnp.exp(r[0] * (-0.125))
            if h == 0:
                refr = jnp.where(lane < 2, 0.0, refr)
            if h == h_n - 1:
                refr = jnp.where(lane >= LANES - 2, 0.0, refr)
            total = refr if total is None else total + refr
        acc[x, pl.ds(yo, 8), :] = total

    def body(t, carry):
        for j in range(2):
            y = pl.multiple_of(PAD + t * 16 + j * 8, 8)
            yo = pl.multiple_of(t * 16 + j * 8, 8)
            for x in range(x_n):
                tile(y, yo, x)
        return carry

    lax.fori_loop(0, ny // 16, body, 0)
    for x in range(x_n):
        for b in range(ny // LANES):
            cols = slice(b * LANES, (b + 1) * LANES)
            path[x : x + 1, cols] = jnp.sum(acc[x, cols, :].T, axis=0, keepdims=True)


def edge_kernel(dims, count_z, *refs):
    x_n, h_n, ny = dims
    s0, mk, s1, zown, ya, yb, za, zb, path_in = refs[:9]
    zp, yp, own = refs[9:12]
    sends = refs[12 : 12 + count_z - 1]
    turned, path = refs[12 + count_z - 1 :]
    nyp = ny + 2 * PAD
    nb = ny // LANES
    lane = lane_iota()
    even = lax.rem(lax.axis_index("gy"), 2) == 0
    gz = lax.axis_index("gz")
    even_z = lax.rem(gz, 2) == 0
    s0_flat, s1_flat, mk_flat = flat(s0), flat(s1), flat(mk)
    stride = h_n * nyp
    blk = [slice(b * LANES, (b + 1) * LANES) for b in range(max(nb, h_n))]

    y_sums = []
    for side in range(2):

        def at(r):
            return PAD + (r if side == 0 else ny - 1 - r)

        def own_rows(ref, r):
            return [
                [row_of(ref, (f * x_n * h_n + h) * nyp, stride, at(r), x_n) for h in range(h_n)]
                for f in range(4)
            ]

        def halo(k):
            return [y_halo(even, ya, yb, k, blk[h])[side] for h in range(h_n)]

        zero = {
            -2: [halo(4 + f) for f in range(4)],
            -1: [halo(f) for f in range(4)],
        }
        for r in range(3):
            zero[r] = own_rows(s0_flat, r)
        open_at = {-1: [m != 0.0 for m in halo(8)]}
        for r in range(2):
            open_at[r] = [
                row_of(mk_flat, h * nyp, stride, at(r), x_n) != 0 for h in range(h_n)
            ]
        one = {r: own_rows(s1_flat, r) for r in (1, 2)}

        def advance(state, base, r, scale, fields=4):
            pairs = [height_pair(state[r][f], lane) for f in range(4)]
            ahead, behind = (r + 1, r - 1) if side == 0 else (r - 1, r + 1)
            out = [[None] * h_n for _ in range(4)]
            for h in range(h_n):
                c = [state[r][f][h] for f in range(4)]
                q = stepped(
                    [base[f][h] for f in range(4)],
                    c,
                    [east(v) for v in c],
                    [west(v) for v in c],
                    [state[ahead][f][h] for f in range(4)],
                    [state[behind][f][h] for f in range(4)],
                    [p[0][h] for p in pairs],
                    [p[1][h] for p in pairs],
                    scale,
                )
                for f in range(4):
                    out[f][h] = q[f] if f == 0 else jnp.where(open_at[r][h], q[f], 0.0)
            return out

        for r in (-1, 0):
            one[r] = advance(zero, zero[r], r, 1.0)
        for r in (0, 1):
            base = [
                [0.5 * (zero[r][f][h] + one[r][f][h]) for h in range(h_n)] for f in range(4)
            ]
            two = advance(one, base, r, 0.5)
            for f in range(4):
                for h in range(h_n):
                    yp[side * 8 + r * 4 + f, :, blk[h]] = two[f][h]
            total = None
            for h in range(h_n):
                refr = 1.0 - jnp.exp(two[0][h] * (-0.125))
                if h == 0:
                    refr = jnp.where(lane < 2, 0.0, refr)
                if h == h_n - 1:
                    refr = jnp.where(lane >= LANES - 2, 0.0, refr)
                total = refr if total is None else total + refr
            y_sums.append((r if side == 0 else ny - 1 - r, jnp.sum(total, axis=1, keepdims=True)))

    sums = [path_in[:, blk[b]] for b in range(nb)]
    for y, value in y_sums:
        b = y // LANES
        sums[b] = jnp.where(lane == y % LANES, value, sums[b])

    for side in range(2):
        exists = (gz > 0) if side == 0 else (gz < count_z - 1)

        def halo(k):
            cols = [slice(b * LANES, (b + 1) * LANES) for b in range(nb)]
            rows = slice(k * 8, k * 8 + 8)
            take_a = jnp.logical_not(even_z) if side == 0 else even_z
            return [jnp.where(take_a, za[rows, c], zb[rows, c]) for c in cols]

        def mine(k):
            return [zown[side, k * 8 : k * 8 + 8, blk[b]] for b in range(nb)]

        def extra(f, l, rows):
            return [beyond(lane, even, ya, yb, h_n, side, f, l, rows)]

        blank = [jnp.zeros((8, LANES), jnp.float32)]
        zero = {
            -2: [halo(4 + f) + blank for f in range(4)],
            -1: [halo(f) + halo(9 + f)[:1] for f in range(4)],
        }
        for l in range(4):
            zero[l] = [
                mine(f * 4 + l) + (extra(f, l, (0, 1)) if l < 3 else blank) for f in range(4)
            ]
        open_at = {-1: [m != 0.0 for m in halo(8)]}
        for l in range(3):
            open_at[l] = [m != 0.0 for m in mine(16 + l)]
        for l in range(2):
            open_at[l] = open_at[l] + [extra(4, l, (0,))[0] != 0.0]

        def advance(state, base, l, scale, blocks):
            norths = [lane_next(state[l][f], lane) for f in range(4)]
            souths = [lane_prev(state[l][f], lane) for f in range(4)]
            above, below = (l + 1, l - 1) if side == 0 else (l - 1, l + 1)
            out = [[None] * blocks for _ in range(4)]
            for b in range(blocks):
                c = [state[l][f][b] for f in range(4)]
                q = stepped(
                    [base[f][b] for f in range(4)],
                    c,
                    [east(v) for v in c],
                    [west(v) for v in c],
                    [norths[f][b] for f in range(4)],
                    [souths[f][b] for f in range(4)],
                    [state[above][f][b] for f in range(4)],
                    [state[below][f][b] for f in range(4)],
                    scale,
                )
                for f in range(4):
                    out[f][b] = q[f] if f == 0 else jnp.where(open_at[l][b], q[f], 0.0)
            return out

        one = {}
        for l in range(-1, 3):
            got = advance(zero, zero[l], l, 1.0, nb + 1 if l in (0, 1) else nb)
            if l == -1:
                got = [[jnp.where(exists, v, 0.0) for v in row] for row in got]
            one[l] = got if l in (0, 1) else [row + blank for row in got]
        for l in range(2):
            base = [
                [0.5 * (zero[l][f][b] + one[l][f][b]) for b in range(nb)] for f in range(4)
            ]
            two = advance(one, base, l, 0.5, nb)
            slot = 2 + l if side == 0 else 1 - l
            for b in range(nb):
                for f in range(4):
                    turned[b, pl.ds(f * 32 + slot, 8, stride=4), :] = two[f][b]
                sums[b] = sums[b] + (1.0 - jnp.exp(two[0][b] * (-0.125)))
    for b in range(nb):
        zp[b * LANES : (b + 1) * LANES, :] = turned[b].T

    per = x_n // count_z
    scale = 8.0 / math.sqrt(h_n * LANES * count_z)
    for b in range(nb):
        path[b] = sums[b] * scale
    for b in range(nb):
        own[:, blk[b]] = path[b, pl.ds(gz * per, per), :]
        for k in range(1, count_z):
            sends[k - 1][:, blk[b]] = path[b, pl.ds((gz ^ k) * per, per), :]


def write_kernel(dims, s2, zp, yp, o0, o1, o2, o3, buf, sem):
    x_n, h_n, ny = dims
    lane = lane_iota()
    sub = lax.broadcasted_iota(jnp.int32, (8, LANES), 0)
    outs = (o0, o1, o2, o3)
    tiles = ny // 8
    copies = []
    for f in range(4):
        for x in range(x_n):
            shift = (LANES - ((f * x_n + x) * 4 + 2)) % LANES

            def tile(t, carry, f=f, x=x, shift=shift):
                y = pl.multiple_of(t * 8, 8)
                edge = pltpu.roll(zp[pl.ds(y, 8), :], shift, 1)
                for h in range(h_n):
                    cols = slice(h * LANES, (h + 1) * LANES)
                    v = s2[f, x, pl.ds(y, 8), cols]
                    if h == 0:
                        v = jnp.where(lane < 2, edge, v)
                    if h == h_n - 1:
                        v = jnp.where(lane >= LANES - 2, edge, v)
                    buf[f, x, pl.ds(y, 8), cols] = v
                return carry

            for t in range(tiles):
                tile(t, 0)
            for side in range(2):
                t = 0 if side == 0 else tiles - 1
                for h in range(h_n):
                    cols = slice(h * LANES, (h + 1) * LANES)
                    v = buf[f, x, t * 8 : t * 8 + 8, cols]
                    for r in range(2):
                        at = r if side == 0 else 7 - r
                        row = yp[side * 8 + r * 4 + f, x : x + 1, cols]
                        keep = sub == at
                        if h == 0:
                            keep = keep & (lane >= 2)
                        if h == h_n - 1:
                            keep = keep & (lane < LANES - 2)
                        v = jnp.where(keep, row, v)
                    buf[f, x, t * 8 : t * 8 + 8, cols] = v
        copy = pltpu.make_async_copy(buf.at[f], outs[f], sem.at[f])
        copy.start()
        copies.append(copy)
    for c in copies:
        c.wait()


def pairs_of(count, wrap):
    a = [(i, i ^ 1) for i in range(count)]
    b = [(i, (i + 1) % count if i % 2 else (i - 1) % count) for i in range(count)]
    if not wrap:
        b = [(i, j) for i, j in b if abs(i - j) == 1]
    return a, b


def params(limit=LIMIT):
    return pltpu.CompilerParams(vmem_limit_bytes=limit)


def on_device(theta, u, v, w, markers):
    x_n, ny, nz = theta.shape
    h_n = nz // LANES
    count_z, count_y = lax.axis_size("gz"), lax.axis_size("gy")
    dims = (x_n, h_n, ny)
    nyp = ny + 2 * PAD
    f32 = jnp.float32
    fields = pltpu.VMEM((4, x_n, h_n, nyp, LANES), f32)
    args = [pltpu.with_memory_space_constraint(a, pltpu.HBM) for a in (theta, u, v, w, markers)]
    cells = x_n * ny * nz

    def cost(flops, moved):
        return pl.CostEstimate(flops=flops, bytes_accessed=moved, transcendentals=0)

    s0, mk, ys_a, ys_b, zown = pl.pallas_call(
        functools.partial(pack_kernel, dims),
        out_shape=(
            fields,
            pltpu.VMEM((x_n, h_n, nyp, LANES), jnp.int32),
            jax.ShapeDtypeStruct((72, nz), f32),
            jax.ShapeDtypeStruct((72, nz), f32),
            jax.ShapeDtypeStruct((2, 152, ny), f32),
        ),
        in_specs=[HBM] * 5,
        out_specs=(VMEM,) * 5,
        scratch_shapes=[
            pltpu.VMEM((3, ny, LANES), f32),
            pltpu.VMEM((3, ny // LANES, LANES, LANES), f32),
            pltpu.SemaphoreType.DMA((5, h_n)),
        ],
        compiler_params=params(),
        name="load_and_pack",
    )(*args)

    y_pairs = pairs_of(count_y, True)
    ya = lax.ppermute(ys_a, "gy", y_pairs[0])
    yb = lax.ppermute(ys_b, "gy", y_pairs[1])

    s1 = pl.pallas_call(
        functools.partial(section_one_kernel, dims),
        out_shape=fields,
        in_specs=[VMEM] * 2,
        out_specs=VMEM,
        compiler_params=params(),
        cost_estimate=cost(100 * cells, 36 * cells),
        name="section_one",
    )(s0, mk)

    zs_a, zs_b = pl.pallas_call(
        functools.partial(corner_kernel, dims),
        out_shape=(jax.ShapeDtypeStruct((104, ny), f32),) * 2,
        in_specs=[VMEM] * 3,
        out_specs=(VMEM,) * 2,
        compiler_params=params(),
        name="corners",
    )(ya, yb, zown)

    z_pairs = pairs_of(count_z, False)
    za = lax.ppermute(zs_a, "gz", z_pairs[0])
    zb = lax.ppermute(zs_b, "gz", z_pairs[1])

    s2, path = pl.pallas_call(
        functools.partial(section_two_kernel, dims),
        out_shape=(pltpu.VMEM((4, x_n, ny, nz), f32), jax.ShapeDtypeStruct((x_n, ny), f32)),
        in_specs=[VMEM] * 3,
        out_specs=(VMEM,) * 2,
        scratch_shapes=[pltpu.VMEM((x_n, ny, LANES), f32)],
        compiler_params=params(),
        cost_estimate=cost(110 * cells, 52 * cells),
        name="section_two",
    )(s0, mk, s1)

    per = x_n // count_z
    edges = pl.pallas_call(
        functools.partial(edge_kernel, dims, count_z),
        out_shape=(
            jax.ShapeDtypeStruct((ny, LANES), f32),
            jax.ShapeDtypeStruct((16, 8, nz), f32),
        )
        + (jax.ShapeDtypeStruct((per, ny), f32),) * count_z,
        in_specs=[VMEM] * 9,
        out_specs=(VMEM,) * (2 + count_z),
        scratch_shapes=[
            pltpu.VMEM((ny // LANES, LANES, LANES), f32),
            pltpu.VMEM((ny // LANES, 8, LANES), f32),
        ],
        compiler_params=params(),
        name="edges",
    )(s0, mk, s1, zown, ya, yb, za, zb, path)
    zp, yp, own = edges[:3]

    got = [
        lax.ppermute(part, "gz", [(i, i ^ k) for i in range(count_z)])
        for k, part in enumerate(edges[3:], start=1)
    ]

    outs = pl.pallas_call(
        functools.partial(write_kernel, dims),
        out_shape=(pltpu.HBM((x_n, ny, nz), f32),) * 4,
        in_specs=[VMEM] * 3,
        out_specs=(HBM,) * 4,
        scratch_shapes=[pltpu.VMEM((4, x_n, ny, nz), f32), pltpu.SemaphoreType.DMA((4,))],
        compiler_params=params(),
        cost_estimate=cost(cells, 32 * cells),
        name="write",
    )(s2, zp, yp)

    total = own
    for part in got:
        total = total + part
    return (*outs, total)


def solution(mesh):
    spec = P(None, "gy", "gz")
    return jax.shard_map(
        on_device,
        mesh=mesh,
        in_specs=(spec,) * 5,
        out_specs=(spec,) * 4 + (P("gz", "gy"),),
        check_vma=False,
    )
```

time: 163 us -> 35.3 us (0.22)
  other arithmetic: 81.9 us -> 0.57 us
  local copies, waits for them, and re-layouts: 48.2 us -> 0 us
  Pallas kernels: 0 us -> 17.9 us
  blocking collectives: 9.94 us -> 0 us
  starting transfers between devices: 17.5 us -> 12.6 us
    mul x11 -> x0, other arithmetic: 43.8 us -> none  [the longest x2 20 us: tendencies(): grad_z = 0.5 * (upper_side - lower_side)]
    sub x2 -> x0, other arithmetic: 20.7 us -> none  [tendencies(): tendency = diffusion * laplace - advect]
    slice x12 -> x0, local copies, waits for them, and re-layouts: 18.5 us -> none  [the longest x5 10.9 us: extended(): last = lax.slice_in_dim(shard, length - width, length, axis=dim)]
    pallas_call x0 -> x6, Pallas kernels: none -> 17.9 us  [the longest x1 5.49 us: on_device(): pl.pallas_call(functools.partial(section_two_kernel, dims), out_shape=(pl...]
    unnamed x82 -> x0, local copies, waits for them, and re-layouts: 17.3 us -> none
    ppermute x4 -> x0, local copies, waits for them, and re-layouts: 10.3 us -> none  [the longest x2 5.18 us: extended(): before = lax.ppermute(last, axis, up)]
    unnamed x1 -> x0, blocking collectives: 9.94 us -> none
    add x7 -> x1, other arithmetic: 8.98 us -> 0.57 us  [on_device(): total = total + part]
  transfers between devices with their start and end apart: 8 -> 7, of which waited for: 1 -> 2; matrix products, arithmetic and copies ran while one was open for 19% -> 0% of each run, Pallas kernels for 0% -> 36%
where the time goes in v1:
time: 35.3 us; the launch traced here: 35.1 us
  Pallas kernels  17.9 us (51%)
  starting transfers between devices  12.6 us (36%)
  waiting for transfers between devices  3.34 us (9%)
  between operations  0.72 us (2%)
  other arithmetic  0.57 us (2%)
    ppermute x3, starting transfers between devices, on_device(): lax.ppermute(part, 'gz', [(i, i ^ k) for i in range(count_z)])  5.93 us
    pallas_call x1, Pallas kernels, on_device(): pl.pallas_call(functools.partial(section_two_kernel, dims), out_shape=(pl...  5.49 us
    pallas_call x1, Pallas kernels, on_device(): pl.pallas_call(functools.partial(section_one_kernel, dims), out_shape=fie...  4.86 us
    pallas_call x1, Pallas kernels, on_device(): pl.pallas_call(functools.partial(pack_kernel, dims), out_shape=(fields, p...  4.14 us
    ppermute x1, starting transfers between devices, on_device(): yb = lax.ppermute(ys_b, 'gy', y_pairs[1])  3.56 us
    pallas_call x1, Pallas kernels, on_device(): pl.pallas_call(functools.partial(write_kernel, dims), out_shape=(pltpu.HB...  2.24 us
    ppermute x1, waiting for transfers between devices, on_device(): yb = lax.ppermute(ys_b, 'gy', y_pairs[1])  2.03 us
    ppermute x1, starting transfers between devices, on_device(): za = lax.ppermute(zs_a, 'gz', z_pairs[0])  1.91 us
  transfers between devices with their start and end apart: 7, of which 2 were waited for; matrix products, arithmetic and copies ran while one was open for 0% of the time, Pallas kernels for 36%

profile of v1, /device:TPU:0, one launch (start us, length us, event | category | flops | bytes accessed | tf_op | source)
XLA Modules:
  0.0 35.1 jit_solution(14605555759356916517)
XLA Ops:
  0.6 4.1 %load_and_pack.1 = (f32[4,8,2,144,128]{4,3,2,1,0:T(8,128)S(1)}, s32[8,2,144,128]{3,2,1,0:T(8,128)S(1)}, f32[72,256]{1,0:T(8,128)S(1)}, f32[72,256]{1,0:T(8,128)S(1)}, f32[2,152,128]{2,1,0:T(8,128)S(1)}) custom-call(f32[8,128,256]{2,1,0:T(8,128)} %refs_0_.1, f32[8,128,256]{2,1,0:T(8,128)} %refs_1_.1, f32[8,128,256]{2,1,0:T(8,128)} %refs_2_.1, ...), custom_call_target="tpu_custom_call" | custom-call | tf_op jit(solution)/shard_map/load_and_pack/pallas_call | solution.py:566
  4.8 0.5 %collective-permute-start = (f32[72,256]{1,0:T(8,128)S(1)}, f32[72,256]{1,0:T(8,128)S(1)}, u32[]{:S(2)}, u32[]{:S(2)}) collective-permute-start(f32[72,256]{1,0:T(8,128)S(1)} %get-tuple-element.28), channel_id=1, source_target_pairs={{0,1},{1,0},{2,3},{3,2},{4,5},{5,4},{6,7},{7,6},{8,9},{9,8},{10,11... | collective-permute-start | bytes 221192 | tf_op jit(solution)/shard_map/ppermute | solution.py:587
  5.3 3.6 %collective-permute-start.1 = (f32[72,256]{1,0:T(8,128)S(1)}, f32[72,256]{1,0:T(8,128)S(1)}, u32[]{:S(2)}, u32[]{:S(2)}) collective-permute-start(f32[72,256]{1,0:T(8,128)S(1)} %get-tuple-element.29), channel_id=1, source_target_pairs={{0,7},{1,2},{2,1},{3,4},{4,3},{5,6},{6,5},{7,0},{8,15},{9,10},{10,... | collective-permute-start | bytes 221192 | tf_op jit(solution)/shard_map/ppermute | solution.py:588
  8.9 0.0 collective-permute-done.ya.refs_4_
  8.9 2.0 %collective-permute-done.1.yb.refs_5_ = f32[72,256]{1,0:T(8,128)S(1)} collective-permute-done((f32[72,256]{1,0:T(8,128)S(1)}, f32[72,256]{1,0:T(8,128)S(1)}, u32[]{:S(2)}, u32[]{:S(2)}) %collective-permute-start.1) | collective-permute-done | bytes 73760 | tf_op jit(solution)/shard_map/ppermute | solution.py:588
  10.9 0.1 corners.1
  11.0 1.9 %collective-permute-start.2 = (f32[104,128]{1,0:T(8,128)S(1)}, f32[104,128]{1,0:T(8,128)S(1)}, u32[]{:S(2)}, u32[]{:S(2)}) collective-permute-start(f32[104,128]{1,0:T(8,128)S(1)} %get-tuple-element.30), channel_id=1, source_target_pairs={{0,8},{8,0},{16,24},{24,16},{1,9},{9,1},{17,25},{25,17},{2,10},{10... | collective-permute-start | bytes 159752 | tf_op jit(solution)/shard_map/ppermute | solution.py:610
  12.9 0.7 %collective-permute-start.3 = (f32[104,128]{1,0:T(8,128)S(1)}, f32[104,128]{1,0:T(8,128)S(1)}, u32[]{:S(2)}, u32[]{:S(2)}) collective-permute-start(f32[104,128]{1,0:T(8,128)S(1)} %get-tuple-element.31), channel_id=1, source_target_pairs={{8,16},{16,8},{9,17},{17,9},{10,18},{18,10},{11,19},{19,11},{12,20... | collective-permute-start | bytes 159752 | tf_op jit(solution)/shard_map/ppermute | solution.py:611
  13.5 4.9 %section_one.1.s1.refs_2_ = f32[4,8,2,144,128]{4,3,2,1,0:T(8,128)S(1)} custom-call(f32[4,8,2,144,128]{4,3,2,1,0:T(8,128)S(1)} %get-tuple-element.24.s0.refs_0_, s32[8,2,144,128]{3,2,1,0:T(8,128)S(1)} %get-tuple-element.25.mk.refs_1_), custom_call_target="tpu_custom_call" | custom-call | flops 26214400 | bytes 9437184 | tf_op jit(solution)/shard_map/section_one/pallas_call | solution.py:590
  18.4 5.5 %section_two.1 = (f32[4,8,128,256]{3,2,1,0:T(8,128)S(1)}, f32[8,128]{1,0:T(8,128)S(1)}) custom-call(f32[4,8,2,144,128]{4,3,2,1,0:T(8,128)S(1)} %get-tuple-element.24.s0.refs_0_, s32[8,2,144,128]{3,2,1,0:T(8,128)S(1)} %get-tuple-element.25.mk.refs_1_, f32[4,8,2,144,128]{4,3,2,1,0:T(8,128)S(1)} %section_one.1.s1.refs_2_), custom_call_target="tpu_custom_call" | custom-call | flops 28835840 | bytes 13631488 | tf_op jit(solution)/shard_map/section_two/pallas_call | solution.py:613
  23.9 0.0 collective-permute-done.2.refs_6_
  23.9 0.0 collective-permute-done.3.refs_7_
  23.9 1.1 %edges.1 = (f32[128,128]{1,0:T(8,128)S(1)}, f32[16,8,256]{2,1,0:T(8,128)S(1)}, f32[2,128]{1,0:T(2,128)S(1)}, f32[2,128]{1,0:T(2,128)S(1)}, f32[2,128]{1,0:T(2,128)S(1)}, /*index=5*/f32[2,128]{1,0:T(2,128)S(1)}) custom-call(f32[4,8,2,144,128]{4,3,2,1,0:T(8,128)S(1)} %get-tuple-element.24.s0.refs_0_, s32[8,2,144,128]{3,2,1,0:T(8,128)S(1)} %get-tuple-element.25.mk.refs_1_, ...), custom_call_target="tpu_custom_call" | custom-call | tf_op jit(solution)/shard_map/edges/pallas_call | solution.py:625
  25.1 2.5 %collective-permute-start.6 = (f32[2,128]{1,0:T(2,128)S(1)}, f32[2,128]{1,0:T(2,128)S(1)}, u32[]{:S(2)}, u32[]{:S(2)}) collective-permute-start(f32[2,128]{1,0:T(2,128)S(1)} %get-tuple-element.42), channel_id=1, source_target_pairs={{0,24},{8,16},{16,8},{24,0},{1,25},{9,17},{17,9},{25,1},{2,26},{10... | collective-permute-start | bytes 3080 | tf_op jit(solution)/shard_map/ppermute | solution.py:644
  27.6 3.4 %collective-permute-start.5 = (f32[2,128]{1,0:T(2,128)S(1)}, f32[2,128]{1,0:T(2,128)S(1)}, u32[]{:S(2)}, u32[]{:S(2)}) collective-permute-start(f32[2,128]{1,0:T(2,128)S(1)} %get-tuple-element.41), channel_id=1, source_target_pairs={{0,16},{8,24},{16,0},{24,8},{1,17},{9,25},{17,1},{25,9},{2,18},{10... | collective-permute-start | bytes 3080 | tf_op jit(solution)/shard_map/ppermute | solution.py:644
  31.0 0.0 collective-permute-start.4
  31.0 2.2 %write.1 = (f32[8,128,256]{2,1,0:T(8,128)}, f32[8,128,256]{2,1,0:T(8,128)}, f32[8,128,256]{2,1,0:T(8,128)}, f32[8,128,256]{2,1,0:T(8,128)}) custom-call(f32[4,8,128,256]{3,2,1,0:T(8,128)S(1)} %get-tuple-element.26.s2, f32[128,128]{1,0:T(8,128)S(1)} %get-tuple-element.33.zp, f32[16,8,256]{2,1,0:T(8,128)S(1)} %get-tuple-element.34.yp), custom_call_target="tpu_custom_call" | custom-call | flops 262144 | bytes 8388608 | tf_op jit(solution)/shard_map/write/pallas_call | solution.py:648
  33.2 0.0 collective-permute-done.6
  33.3 0.0 collective-permute-done.5
  33.3 1.3 %collective-permute-done.4 = f32[2,128]{1,0:T(2,128)S(1)} collective-permute-done((f32[2,128]{1,0:T(2,128)S(1)}, f32[2,128]{1,0:T(2,128)S(1)}, u32[]{:S(2)}, u32[]{:S(2)}) %collective-permute-start.4) | collective-permute-done | bytes 1056 | tf_op jit(solution)/shard_map/ppermute | solution.py:644
  34.6 0.6 %add_add_fusion = f32[2,128]{1,0:T(2,128)} fusion(f32[2,128]{1,0:T(2,128)S(1)} %collective-permute-done.6, f32[2,128]{1,0:T(2,128)S(1)} %collective-permute-done.5, f32[2,128]{1,0:T(2,128)S(1)} %get-tuple-element.39, f32[2,128]{1,0:T(2,128)S(1)} %collective-permute-done.4), kind=kLoop, calls=%fused_computation | loop fusion | flops 768 | bytes 5120 | tf_op jit(solution)/shard_map/add | solution.py:661
Async XLA Ops:
  4.8 4.1 %collective-permute-start = (f32[72,256]{1,0:T(8,128)S(1)}, f32[72,256]{1,0:T(8,128)S(1)}, u32[]{:S(2)}, u32[]{:S(2)}) collective-permute-start(f32[72,256]{1,0:T(8,128)S(1)} %get-tuple-element.28), channel_id=1, source_target_pairs={{0,1},{1,0},{2,3},{3,2},{4,5},{5,4},{6,7},{7,6},{8,9},{9,8},{10,11... | collective-permute-start | bytes 221192 | tf_op jit(solution)/shard_map/ppermute | solution.py:587
  5.3 5.6 %collective-permute-start.1 = (f32[72,256]{1,0:T(8,128)S(1)}, f32[72,256]{1,0:T(8,128)S(1)}, u32[]{:S(2)}, u32[]{:S(2)}) collective-permute-start(f32[72,256]{1,0:T(8,128)S(1)} %get-tuple-element.29), channel_id=1, source_target_pairs={{0,7},{1,2},{2,1},{3,4},{4,3},{5,6},{6,5},{7,0},{8,15},{9,10},{10,... | collective-permute-start | bytes 221192 | tf_op jit(solution)/shard_map/ppermute | solution.py:588
  11.0 12.9 %collective-permute-start.2 = (f32[104,128]{1,0:T(8,128)S(1)}, f32[104,128]{1,0:T(8,128)S(1)}, u32[]{:S(2)}, u32[]{:S(2)}) collective-permute-start(f32[104,128]{1,0:T(8,128)S(1)} %get-tuple-element.30), channel_id=1, source_target_pairs={{0,8},{8,0},{16,24},{24,16},{1,9},{9,1},{17,25},{25,17},{2,10},{10... | collective-permute-start | bytes 159752 | tf_op jit(solution)/shard_map/ppermute | solution.py:610
  12.9 11.0 %collective-permute-start.3 = (f32[104,128]{1,0:T(8,128)S(1)}, f32[104,128]{1,0:T(8,128)S(1)}, u32[]{:S(2)}, u32[]{:S(2)}) collective-permute-start(f32[104,128]{1,0:T(8,128)S(1)} %get-tuple-element.31), channel_id=1, source_target_pairs={{8,16},{16,8},{9,17},{17,9},{10,18},{18,10},{11,19},{19,11},{12,20... | collective-permute-start | bytes 159752 | tf_op jit(solution)/shard_map/ppermute | solution.py:611
  25.1 8.2 %collective-permute-start.6 = (f32[2,128]{1,0:T(2,128)S(1)}, f32[2,128]{1,0:T(2,128)S(1)}, u32[]{:S(2)}, u32[]{:S(2)}) collective-permute-start(f32[2,128]{1,0:T(2,128)S(1)} %get-tuple-element.42), channel_id=1, source_target_pairs={{0,24},{8,16},{16,8},{24,0},{1,25},{9,17},{17,9},{25,1},{2,26},{10... | collective-permute-start | bytes 3080 | tf_op jit(solution)/shard_map/ppermute | solution.py:644
  27.6 5.6 %collective-permute-start.5 = (f32[2,128]{1,0:T(2,128)S(1)}, f32[2,128]{1,0:T(2,128)S(1)}, u32[]{:S(2)}, u32[]{:S(2)}) collective-permute-start(f32[2,128]{1,0:T(2,128)S(1)} %get-tuple-element.41), channel_id=1, source_target_pairs={{0,16},{8,24},{16,0},{24,8},{1,17},{9,25},{17,1},{25,9},{2,18},{10... | collective-permute-start | bytes 3080 | tf_op jit(solution)/shard_map/ppermute | solution.py:644
  31.0 3.6 %collective-permute-start.4 = (f32[2,128]{1,0:T(2,128)S(1)}, f32[2,128]{1,0:T(2,128)S(1)}, u32[]{:S(2)}, u32[]{:S(2)}) collective-permute-start(f32[2,128]{1,0:T(2,128)S(1)} %get-tuple-element.40), channel_id=1, source_target_pairs={{0,8},{8,0},{16,24},{24,16},{1,9},{9,1},{17,25},{25,17},{2,10},{10... | collective-permute-start | bytes 3080 | tf_op jit(solution)/shard_map/ppermute | solution.py:644

commit v2 on v1

--- a/solution.py
+++ b/solution.py
@@ -115,11 +115,34 @@
             )
     for c in copies:
         c.start()
-    for c in copies:
-        c.wait()
     even = lax.rem(lax.axis_index("gy"), 2) == 0
     s0_flat, mk_flat = flat(s0), flat(mk)
     stride = h_n * nyp
+    group = lane // 8
+
+    def arrived(f):
+        for c in copies[f * h_n : (f + 1) * h_n]:
+            c.wait()
+
+    def pack_columns(a):
+        def tile(t, carry):
+            y = pl.multiple_of(PAD + t * 8, 8)
+            yo = pl.multiple_of(t * 8, 8)
+            acc = jnp.zeros((8, LANES), jnp.float32)
+            for g in range(16 if a < 2 else 8):
+                f, x = a * 2 + g // 8, g % 8
+                if a < 2:
+                    lo, hi = s0[f, x, 0, pl.ds(y, 8), :], s0[f, x, h_n - 1, pl.ds(y, 8), :]
+                else:
+                    lo, hi = mk[x, 0, pl.ds(y, 8), :], mk[x, h_n - 1, pl.ds(y, 8), :]
+                both = jnp.where(lane < LANES // 2, lo, hi).astype(jnp.float32)
+                acc = jnp.where(group == g, pltpu.roll(both, (g * 8 + 4) % LANES, 1), acc)
+            part[a, pl.ds(yo, 8), :] = acc
+            return carry
+
+        lax.fori_loop(0, ny // 8, tile, 0, unroll=4)
+        for b in range(ny // LANES):
+            turned[a, b] = part[a, b * LANES : (b + 1) * LANES, :].T
 
     def rows(dst, ys):
         for r, y in enumerate(ys):
@@ -132,6 +155,11 @@
                     block = row_of(mk_flat, h * nyp, stride, PAD + y, x_n)
                     dst[64:72, cols] = block.astype(jnp.float32)
 
+    for a, fields in enumerate(((0, 1), (2, 3), (4,))):
+        for f in fields:
+            arrived(f)
+        pack_columns(a)
+
     first, last = (0, 1), (ny - 1, ny - 2)
 
     @pl.when(even)
@@ -144,29 +172,6 @@
         rows(ys_a, first)
         rows(ys_b, last)
 
-    group = lane // 8
-
-    def tile(t, carry):
-        y = pl.multiple_of(PAD + t * 8, 8)
-        yo = pl.multiple_of(t * 8, 8)
-        for a in range(3):
-            acc = jnp.zeros((8, LANES), jnp.float32)
-            for g in range(16 if a < 2 else 8):
-                f, x = a * 2 + g // 8, g % 8
-                if a < 2:
-                    lo, hi = s0[f, x, 0, pl.ds(y, 8), :], s0[f, x, h_n - 1, pl.ds(y, 8), :]
-                else:
-                    lo, hi = mk[x, 0, pl.ds(y, 8), :], mk[x, h_n - 1, pl.ds(y, 8), :]
-                both = jnp.where(lane < LANES // 2, lo, hi).astype(jnp.float32)
-                acc = jnp.where(group == g, pltpu.roll(both, (g * 8 + 4) % LANES, 1), acc)
-            part[a, pl.ds(yo, 8), :] = acc
-        return carry
-
-    lax.fori_loop(0, ny // 8, tile, 0, unroll=2)
-    for a in range(3):
-        for b in range(ny // LANES):
-            cols = slice(b * LANES, (b + 1) * LANES)
-            turned[a, b] = part[a, cols, :].T
     for side in range(2):
         for l in range(4):
             j = 4 + l if side == 0 else 3 - l
@@ -201,7 +206,8 @@
     return out
 
 
-def corner_kernel(dims, ya, yb, zown, zs_a, zs_b):
+def corner_kernel(dims, ya, yb, zown, after, zs_a, zs_b):
+    del after
     x_n, h_n, ny = dims
     lane = lane_iota()
     even = lax.rem(lax.axis_index("gy"), 2) == 0
@@ -272,6 +278,7 @@
 def section_two_kernel(dims, s0, mk, s1, s2, path, acc):
     x_n, h_n, ny = dims
     lane = lane_iota()
+    sub = lax.broadcasted_iota(jnp.int32, (8, LANES), 0)
 
     def tile(y, yo, x):
         c = [load4(s1, x, h, y) for h in range(h_n)]
@@ -301,21 +308,31 @@
             if h == h_n - 1:
                 refr = jnp.where(lane >= LANES - 2, 0.0, refr)
             total = refr if total is None else total + refr
-        acc[x, pl.ds(yo, 8), :] = total
+        return total
 
     def body(t, carry):
         for j in range(2):
             y = pl.multiple_of(PAD + t * 16 + j * 8, 8)
             yo = pl.multiple_of(t * 16 + j * 8, 8)
             for x in range(x_n):
-                tile(y, yo, x)
+                acc[x, pl.ds(yo, 8), :] = tile(y, yo, x)
         return carry
 
     lax.fori_loop(0, ny // 16, body, 0)
-    for x in range(x_n):
-        for b in range(ny // LANES):
-            cols = slice(b * LANES, (b + 1) * LANES)
-            path[x : x + 1, cols] = jnp.sum(acc[x, cols, :].T, axis=0, keepdims=True)
+    ones = jnp.ones((LANES, LANES), jnp.bfloat16)
+    diagonal = lax.broadcasted_iota(jnp.int32, (LANES, LANES), 0) == lax.broadcasted_iota(
+        jnp.int32, (LANES, LANES), 1
+    )
+    for b in range(ny // LANES):
+        cols = slice(b * LANES, (b + 1) * LANES)
+        rows = jnp.concatenate([acc[x, cols, :] for x in range(x_n)], axis=0)
+        high = rows.astype(jnp.bfloat16)
+        rest = (rows - high.astype(jnp.float32)).astype(jnp.bfloat16)
+        sums = jnp.dot(high, ones, preferred_element_type=jnp.float32)
+        sums = sums + jnp.dot(rest, ones, preferred_element_type=jnp.float32)
+        for x in range(x_n):
+            one = jnp.where(diagonal, sums[x * LANES : (x + 1) * LANES], 0.0)
+            path[x : x + 1, cols] = jnp.sum(one, axis=0, keepdims=True)
 
 
 def edge_kernel(dims, count_z, *refs):
@@ -415,7 +432,8 @@
             cols = [slice(b * LANES, (b + 1) * LANES) for b in range(nb)]
             rows = slice(k * 8, k * 8 + 8)
             take_a = jnp.logical_not(even_z) if side == 0 else even_z
-            return [jnp.where(take_a, za[rows, c], zb[rows, c]) for c in cols]
+            got = [jnp.where(take_a, za[rows, c], zb[rows, c]) for c in cols]
+            return [jnp.where(exists, v, 0.0) for v in got]
 
         def mine(k):
             return [zown[side, k * 8 : k * 8 + 8, blk[b]] for b in range(nb)]
@@ -489,19 +507,19 @@
             sends[k - 1][:, blk[b]] = path[b, pl.ds((gz ^ k) * per, per), :]
 
 
-def write_kernel(dims, s2, zp, yp, o0, o1, o2, o3, buf, sem):
+def write_kernel(dims, s2, zp, yp, *refs):
     x_n, h_n, ny = dims
+    outs, (buf, sem) = refs[:4], refs[4:]
     lane = lane_iota()
     sub = lax.broadcasted_iota(jnp.int32, (8, LANES), 0)
-    outs = (o0, o1, o2, o3)
     tiles = ny // 8
     copies = []
     for f in range(4):
         for x in range(x_n):
             shift = (LANES - ((f * x_n + x) * 4 + 2)) % LANES
 
-            def tile(t, carry, f=f, x=x, shift=shift):
-                y = pl.multiple_of(t * 8, 8)
+            def tile(t, f=f, x=x, shift=shift):
+                y = t * 8
                 edge = pltpu.roll(zp[pl.ds(y, 8), :], shift, 1)
                 for h in range(h_n):
                     cols = slice(h * LANES, (h + 1) * LANES)
@@ -511,10 +529,9 @@
                     if h == h_n - 1:
                         v = jnp.where(lane >= LANES - 2, edge, v)
                     buf[f, x, pl.ds(y, 8), cols] = v
-                return carry
 
             for t in range(tiles):
-                tile(t, 0)
+                tile(t)
             for side in range(2):
                 t = 0 if side == 0 else tiles - 1
                 for h in range(h_n):
@@ -537,12 +554,19 @@
         c.wait()
 
 
-def pairs_of(count, wrap):
+def pairs_of(count):
     a = [(i, i ^ 1) for i in range(count)]
     b = [(i, (i + 1) % count if i % 2 else (i - 1) % count) for i in range(count)]
-    if not wrap:
-        b = [(i, j) for i, j in b if abs(i - j) == 1]
     return a, b
+
+
+def inner_pairs(count_z, count_y):
+    pairs = []
+    for z, other in pairs_of(count_z)[1]:
+        for y in range(count_y):
+            to = other * count_y + y if abs(z - other) == 1 else z * count_y + (y ^ 1)
+            pairs.append((z * count_y + y, to))
+    return pairs
 
 
 def params(limit=LIMIT):
@@ -583,7 +607,7 @@
         name="load_and_pack",
     )(*args)
 
-    y_pairs = pairs_of(count_y, True)
+    y_pairs = pairs_of(count_y)
     ya = lax.ppermute(ys_a, "gy", y_pairs[0])
     yb = lax.ppermute(ys_b, "gy", y_pairs[1])
 
@@ -600,15 +624,14 @@
     zs_a, zs_b = pl.pallas_call(
         functools.partial(corner_kernel, dims),
         out_shape=(jax.ShapeDtypeStruct((104, ny), f32),) * 2,
-        in_specs=[VMEM] * 3,
+        in_specs=[VMEM] * 4,
         out_specs=(VMEM,) * 2,
         compiler_params=params(),
         name="corners",
-    )(ya, yb, zown)
-
-    z_pairs = pairs_of(count_z, False)
-    za = lax.ppermute(zs_a, "gz", z_pairs[0])
-    zb = lax.ppermute(zs_b, "gz", z_pairs[1])
+    )(ya, yb, zown, s1)
+
+    za = lax.ppermute(zs_a, "gz", pairs_of(count_z)[0])
+    zb = lax.ppermute(zs_b, ("gz", "gy"), inner_pairs(count_z, count_y))
 
     s2, path = pl.pallas_call(
         functools.partial(section_two_kernel, dims),
@@ -621,7 +644,7 @@
         name="section_two",
     )(s0, mk, s1)
 
-    per = x_n // count_z
+    per, nb = x_n // count_z, ny // LANES
     edges = pl.pallas_call(
         functools.partial(edge_kernel, dims, count_z),
         out_shape=(
@@ -632,18 +655,19 @@
         in_specs=[VMEM] * 9,
         out_specs=(VMEM,) * (2 + count_z),
         scratch_shapes=[
-            pltpu.VMEM((ny // LANES, LANES, LANES), f32),
-            pltpu.VMEM((ny // LANES, 8, LANES), f32),
+            pltpu.VMEM((nb, LANES, LANES), f32),
+            pltpu.VMEM((nb, x_n, LANES), f32),
         ],
         compiler_params=params(),
         name="edges",
     )(s0, mk, s1, zown, ya, yb, za, zb, path)
     zp, yp, own = edges[:3]
 
-    got = [
-        lax.ppermute(part, "gz", [(i, i ^ k) for i in range(count_z)])
-        for k, part in enumerate(edges[3:], start=1)
-    ]
+    total = own
+    for k in range(count_z - 1, 0, -1):
+        total = total + lax.ppermute(
+            edges[2 + k], "gz", [(i, i ^ k) for i in range(count_z)]
+        )
 
     outs = pl.pallas_call(
         functools.partial(write_kernel, dims),
@@ -655,10 +679,6 @@
         cost_estimate=cost(cells, 32 * cells),
         name="write",
     )(s2, zp, yp)
-
-    total = own
-    for part in got:
-        total = total + part
     return (*outs, total)
 
 

time: 35.3 us -> 31 us (0.88)
  waiting for transfers between devices: 3.34 us -> 0.67 us
  starting transfers between devices: 12.6 us -> 11.3 us
    ppermute x1, waiting for transfers between devices: 2.03 us -> 0.01 us  [on_device(): yb = lax.ppermute(ys_b, 'gy', y_pairs[1])]
    ppermute x5, starting transfers between devices: 8.49 us -> 7.25 us  [the longest x3 5.65 us: on_device(): lax.ppermute(edges[2 + k], 'gz', [(i, i ^ k) for i in range(count_z)])]
    ppermute x5, waiting for transfers between devices: 1.31 us -> 0.66 us  [the longest x3 0.66 us: on_device(): lax.ppermute(edges[2 + k], 'gz', [(i, i ^ k) for i in range(count_z)])]
    pallas_call x1, Pallas kernels: 4.14 us -> 3.58 us  [on_device(): pl.pallas_call(functools.partial(pack_kernel, dims), out_shape=(fields, p...]
  transfers between devices with their start and end apart: 7 -> 7, of which waited for: 2 -> 1; matrix products, arithmetic and copies ran while one was open for 0% -> 0% of each run, Pallas kernels for 36% -> 41%
where the time goes in v2:
time: 31 us; the launch traced here: 30.8 us
  Pallas kernels  17.6 us (57%)
  starting transfers between devices  11.3 us (36%)
  between operations  0.72 us (2%)
  waiting for transfers between devices  0.67 us (2%)
  other arithmetic  0.57 us (2%)
    ppermute x3, starting transfers between devices, on_device(): lax.ppermute(edges[2 + k], 'gz', [(i, i ^ k) for i in range(count_z)])  5.65 us
    pallas_call x1, Pallas kernels, on_device(): pl.pallas_call(functools.partial(section_two_kernel, dims), out_shape=(pl...  5.65 us
    pallas_call x1, Pallas kernels, on_device(): pl.pallas_call(functools.partial(section_one_kernel, dims), out_shape=fie...  4.86 us
    pallas_call x1, Pallas kernels, on_device(): pl.pallas_call(functools.partial(pack_kernel, dims), out_shape=(fields, p...  3.58 us
    ppermute x1, starting transfers between devices, on_device(): yb = lax.ppermute(ys_b, 'gy', y_pairs[1])  3.53 us
    pallas_call x1, Pallas kernels, on_device(): pl.pallas_call(functools.partial(write_kernel, dims), out_shape=(pltpu.HB...  2.25 us
    ppermute x1, starting transfers between devices, on_device(): za = lax.ppermute(zs_a, 'gz', pairs_of(count_z)[0])  1.59 us
    pallas_call x1, Pallas kernels, on_device(): pl.pallas_call(functools.partial(edge_kernel, dims, count_z), out_shape=(...  1.13 us
  transfers between devices with their start and end apart: 7, of which 1 were waited for; matrix products, arithmetic and copies ran while one was open for 0% of the time, Pallas kernels for 41%

profile of v2, /device:TPU:0, one launch (start us, length us, event | category | flops | bytes accessed | tf_op | source)
XLA Modules:
  0.0 30.8 jit_solution(18016127496616195580)
XLA Ops:
  0.6 3.6 %load_and_pack.1 = (f32[4,8,2,144,128]{4,3,2,1,0:T(8,128)S(1)}, s32[8,2,144,128]{3,2,1,0:T(8,128)S(1)}, f32[72,256]{1,0:T(8,128)S(1)}, f32[72,256]{1,0:T(8,128)S(1)}, f32[2,152,128]{2,1,0:T(8,128)S(1)}) custom-call(f32[8,128,256]{2,1,0:T(8,128)} %refs_0_.1, f32[8,128,256]{2,1,0:T(8,128)} %refs_1_.1, f32[8,128,256]{2,1,0:T(8,128)} %refs_2_.1, ...), custom_call_target="tpu_custom_call" | custom-call | tf_op jit(solution)/shard_map/load_and_pack/pallas_call | solution.py:590
  4.2 0.5 %collective-permute-start = (f32[72,256]{1,0:T(8,128)S(1)}, f32[72,256]{1,0:T(8,128)S(1)}, u32[]{:S(2)}, u32[]{:S(2)}) collective-permute-start(f32[72,256]{1,0:T(8,128)S(1)} %get-tuple-element.28), channel_id=1, source_target_pairs={{0,1},{1,0},{2,3},{3,2},{4,5},{5,4},{6,7},{7,6},{8,9},{9,8},{10,11... | collective-permute-start | bytes 221192 | tf_op jit(solution)/shard_map/ppermute | solution.py:611
  4.8 3.5 %collective-permute-start.1 = (f32[72,256]{1,0:T(8,128)S(1)}, f32[72,256]{1,0:T(8,128)S(1)}, u32[]{:S(2)}, u32[]{:S(2)}) collective-permute-start(f32[72,256]{1,0:T(8,128)S(1)} %get-tuple-element.29), channel_id=1, source_target_pairs={{0,7},{1,2},{2,1},{3,4},{4,3},{5,6},{6,5},{7,0},{8,15},{9,10},{10,... | collective-permute-start | bytes 221192 | tf_op jit(solution)/shard_map/ppermute | solution.py:612
  8.3 4.9 %section_one.1.s1.after.refs_2_ = f32[4,8,2,144,128]{4,3,2,1,0:T(8,128)S(1)} custom-call(f32[4,8,2,144,128]{4,3,2,1,0:T(8,128)S(1)} %get-tuple-element.24.s0.refs_0_, s32[8,2,144,128]{3,2,1,0:T(8,128)S(1)} %get-tuple-element.25.mk.refs_1_), custom_call_target="tpu_custom_call" | custom-call | flops 26214400 | bytes 9437184 | tf_op jit(solution)/shard_map/section_one/pallas_call | solution.py:614
  13.2 0.0 collective-permute-done.ya.refs_4_
  13.2 0.0 collective-permute-done.1.yb.refs_5_
  13.2 0.1 corners.1
  13.3 1.6 %collective-permute-start.2 = (f32[104,128]{1,0:T(8,128)S(1)}, f32[104,128]{1,0:T(8,128)S(1)}, u32[]{:S(2)}, u32[]{:S(2)}) collective-permute-start(f32[104,128]{1,0:T(8,128)S(1)} %get-tuple-element.30), channel_id=1, source_target_pairs={{0,8},{8,0},{16,24},{24,16},{1,9},{9,1},{17,25},{25,17},{2,10},{10... | collective-permute-start | bytes 159752 | tf_op jit(solution)/shard_map/ppermute | solution.py:633
  14.9 0.0 collective-permute-start.3
  14.9 5.7 %section_two.1 = (f32[4,8,128,256]{3,2,1,0:T(8,128)S(1)}, f32[8,128]{1,0:T(8,128)S(1)}) custom-call(f32[4,8,2,144,128]{4,3,2,1,0:T(8,128)S(1)} %get-tuple-element.24.s0.refs_0_, s32[8,2,144,128]{3,2,1,0:T(8,128)S(1)} %get-tuple-element.25.mk.refs_1_, f32[4,8,2,144,128]{4,3,2,1,0:T(8,128)S(1)} %section_one.1.s1.after.refs_2_), custom_call_target="tpu_custom_call" | custom-call | flops 28835840 | bytes 13631488 | tf_op jit(solution)/shard_map/section_two/pallas_call | solution.py:636
  20.5 0.0 collective-permute-done.2.refs_6_
  20.5 0.0 collective-permute-done.3.refs_7_
  20.6 1.1 %edges.1 = (f32[128,128]{1,0:T(8,128)S(1)}, f32[16,8,256]{2,1,0:T(8,128)S(1)}, f32[2,128]{1,0:T(2,128)S(1)}, f32[2,128]{1,0:T(2,128)S(1)}, f32[2,128]{1,0:T(2,128)S(1)}, /*index=5*/f32[2,128]{1,0:T(2,128)S(1)}) custom-call(f32[4,8,2,144,128]{4,3,2,1,0:T(8,128)S(1)} %get-tuple-element.24.s0.refs_0_, s32[8,2,144,128]{3,2,1,0:T(8,128)S(1)} %get-tuple-element.25.mk.refs_1_, ...), custom_call_target="tpu_custom_call" | custom-call | tf_op jit(solution)/shard_map/edges/pallas_call | solution.py:648
  21.7 3.2 %collective-permute-start.6 = (f32[2,128]{1,0:T(2,128)S(1)}, f32[2,128]{1,0:T(2,128)S(1)}, u32[]{:S(2)}, u32[]{:S(2)}) collective-permute-start(f32[2,128]{1,0:T(2,128)S(1)} %get-tuple-element.42), channel_id=1, source_target_pairs={{0,8},{8,0},{16,24},{24,16},{1,9},{9,1},{17,25},{25,17},{2,10},{10... | collective-permute-start | bytes 3080 | tf_op jit(solution)/shard_map/ppermute | solution.py:668
  24.9 0.0 collective-permute-start.5
  24.9 2.4 %collective-permute-start.4 = (f32[2,128]{1,0:T(2,128)S(1)}, f32[2,128]{1,0:T(2,128)S(1)}, u32[]{:S(2)}, u32[]{:S(2)}) collective-permute-start(f32[2,128]{1,0:T(2,128)S(1)} %get-tuple-element.40), channel_id=1, source_target_pairs={{0,24},{8,16},{16,8},{24,0},{1,25},{9,17},{17,9},{25,1},{2,26},{10... | collective-permute-start | bytes 3080 | tf_op jit(solution)/shard_map/ppermute | solution.py:668
  27.3 2.3 %write.1 = (f32[8,128,256]{2,1,0:T(8,128)}, f32[8,128,256]{2,1,0:T(8,128)}, f32[8,128,256]{2,1,0:T(8,128)}, f32[8,128,256]{2,1,0:T(8,128)}) custom-call(f32[4,8,128,256]{3,2,1,0:T(8,128)S(1)} %get-tuple-element.26.s2, f32[128,128]{1,0:T(8,128)S(1)} %get-tuple-element.33.zp, f32[16,8,256]{2,1,0:T(8,128)S(1)} %get-tuple-element.34.yp), custom_call_target="tpu_custom_call" | custom-call | flops 262144 | bytes 8388608 | tf_op jit(solution)/shard_map/write/pallas_call | solution.py:672
  29.6 0.0 collective-permute-done.6
  29.6 0.0 collective-permute-done.5
  29.6 0.7 %collective-permute-done.4 = f32[2,128]{1,0:T(2,128)S(1)} collective-permute-done((f32[2,128]{1,0:T(2,128)S(1)}, f32[2,128]{1,0:T(2,128)S(1)}, u32[]{:S(2)}, u32[]{:S(2)}) %collective-permute-start.4) | collective-permute-done | bytes 1056 | tf_op jit(solution)/shard_map/ppermute | solution.py:668
  30.3 0.6 %add_add_fusion = f32[2,128]{1,0:T(2,128)} fusion(f32[2,128]{1,0:T(2,128)S(1)} %collective-permute-done.6, f32[2,128]{1,0:T(2,128)S(1)} %collective-permute-done.5, f32[2,128]{1,0:T(2,128)S(1)} %get-tuple-element.39, f32[2,128]{1,0:T(2,128)S(1)} %collective-permute-done.4), kind=kLoop, calls=%fused_computation | loop fusion | flops 768 | bytes 5120 | tf_op jit(solution)/shard_map/add | solution.py:668
Async XLA Ops:
  4.2 8.9 %collective-permute-start = (f32[72,256]{1,0:T(8,128)S(1)}, f32[72,256]{1,0:T(8,128)S(1)}, u32[]{:S(2)}, u32[]{:S(2)}) collective-permute-start(f32[72,256]{1,0:T(8,128)S(1)} %get-tuple-element.28), channel_id=1, source_target_pairs={{0,1},{1,0},{2,3},{3,2},{4,5},{5,4},{6,7},{7,6},{8,9},{9,8},{10,11... | collective-permute-start | bytes 221192 | tf_op jit(solution)/shard_map/ppermute | solution.py:611
  4.8 8.4 %collective-permute-start.1 = (f32[72,256]{1,0:T(8,128)S(1)}, f32[72,256]{1,0:T(8,128)S(1)}, u32[]{:S(2)}, u32[]{:S(2)}) collective-permute-start(f32[72,256]{1,0:T(8,128)S(1)} %get-tuple-element.29), channel_id=1, source_target_pairs={{0,7},{1,2},{2,1},{3,4},{4,3},{5,6},{6,5},{7,0},{8,15},{9,10},{10,... | collective-permute-start | bytes 221192 | tf_op jit(solution)/shard_map/ppermute | solution.py:612
  13.3 7.3 %collective-permute-start.2 = (f32[104,128]{1,0:T(8,128)S(1)}, f32[104,128]{1,0:T(8,128)S(1)}, u32[]{:S(2)}, u32[]{:S(2)}) collective-permute-start(f32[104,128]{1,0:T(8,128)S(1)} %get-tuple-element.30), channel_id=1, source_target_pairs={{0,8},{8,0},{16,24},{24,16},{1,9},{9,1},{17,25},{25,17},{2,10},{10... | collective-permute-start | bytes 159752 | tf_op jit(solution)/shard_map/ppermute | solution.py:633
  14.9 5.7 %collective-permute-start.3 = (f32[104,128]{1,0:T(8,128)S(1)}, f32[104,128]{1,0:T(8,128)S(1)}, u32[]{:S(2)}, u32[]{:S(2)}) collective-permute-start(f32[104,128]{1,0:T(8,128)S(1)} %get-tuple-element.31), channel_id=1, source_target_pairs={{0,1},{1,0},{2,3},{3,2},{4,5},{5,4},{6,7},{7,6},{8,16},{9,17},{10,... | collective-permute-start | bytes 159752 | tf_op jit(solution)/shard_map/ppermute | solution.py:634
  21.7 7.9 %collective-permute-start.6 = (f32[2,128]{1,0:T(2,128)S(1)}, f32[2,128]{1,0:T(2,128)S(1)}, u32[]{:S(2)}, u32[]{:S(2)}) collective-permute-start(f32[2,128]{1,0:T(2,128)S(1)} %get-tuple-element.42), channel_id=1, source_target_pairs={{0,8},{8,0},{16,24},{24,16},{1,9},{9,1},{17,25},{25,17},{2,10},{10... | collective-permute-start | bytes 3080 | tf_op jit(solution)/shard_map/ppermute | solution.py:668
  24.9 4.7 %collective-permute-start.5 = (f32[2,128]{1,0:T(2,128)S(1)}, f32[2,128]{1,0:T(2,128)S(1)}, u32[]{:S(2)}, u32[]{:S(2)}) collective-permute-start(f32[2,128]{1,0:T(2,128)S(1)} %get-tuple-element.41), channel_id=1, source_target_pairs={{0,16},{8,24},{16,0},{24,8},{1,17},{9,25},{17,1},{25,9},{2,18},{10... | collective-permute-start | bytes 3080 | tf_op jit(solution)/shard_map/ppermute | solution.py:668
  24.9 5.4 %collective-permute-start.4 = (f32[2,128]{1,0:T(2,128)S(1)}, f32[2,128]{1,0:T(2,128)S(1)}, u32[]{:S(2)}, u32[]{:S(2)}) collective-permute-start(f32[2,128]{1,0:T(2,128)S(1)} %get-tuple-element.40), channel_id=1, source_target_pairs={{0,24},{8,16},{16,8},{24,0},{1,25},{9,17},{17,9},{25,1},{2,26},{10... | collective-permute-start | bytes 3080 | tf_op jit(solution)/shard_map/ppermute | solution.py:668

commit v3 on v2

--- a/solution.py
+++ b/solution.py
@@ -96,95 +96,89 @@
     return ref[pl.ds(lead + start, x, stride=x_stride), :]
 
 
-def pack_kernel(dims, *refs):
+def pack_kernel(dims, parts, *refs):
     x_n, h_n, ny = dims
     ins = refs[:5]
     s0, mk, ys_a, ys_b, zown, part, turned, sem = refs[5:]
     nyp = ny + 2 * PAD
     lane = lane_iota()
+    sub = lax.broadcasted_iota(jnp.int32, (8, LANES), 0)
+    size = ny // parts
     copies = []
-    for f in range(5):
-        for h in range(h_n):
-            dst = s0.at[f] if f < 4 else mk
-            copies.append(
-                pltpu.make_async_copy(
-                    ins[f].at[:, :, pl.ds(h * LANES, LANES)],
-                    dst.at[:, h, pl.ds(PAD, ny), :],
-                    sem.at[f, h],
+    for p in range(parts):
+        for f in range(5):
+            for h in range(h_n):
+                dst = s0.at[f] if f < 4 else mk
+                copies.append(
+                    pltpu.make_async_copy(
+                        ins[f].at[:, pl.ds(p * size, size), pl.ds(h * LANES, LANES)],
+                        dst.at[:, h, pl.ds(PAD + p * size, size), :],
+                        sem.at[p, f, h],
+                    )
                 )
-            )
     for c in copies:
         c.start()
+    group = lane // 8
+
+    def columns(t):
+        y = PAD + t * 8
+        for a in range(2):
+            acc = jnp.zeros((8, LANES), jnp.float32)
+            for g in range(16):
+                f, x = a * 2 + g // 8, g % 8
+                lo, hi = s0[f, x, 0, pl.ds(y, 8), :], s0[f, x, h_n - 1, pl.ds(y, 8), :]
+                both = jnp.where(lane < LANES // 2, lo, hi)
+                acc = jnp.where(group == g, pltpu.roll(both, (g * 8 + 4) % LANES, 1), acc)
+            part[a, pl.ds(t * 8, 8), :] = acc
+        bits = jnp.zeros((8, LANES), jnp.int32)
+        for x in range(x_n):
+            lo, hi = mk[x, 0, pl.ds(y, 8), :], mk[x, h_n - 1, pl.ds(y, 8), :]
+            bits = bits + jnp.where(lane < LANES // 2, lo, hi) * (1 << x)
+        part[2, pl.ds(t * 8, 8), :] = bits.astype(jnp.float32)
+
+    for p in range(parts):
+        for c in copies[p * 5 * h_n : (p + 1) * 5 * h_n]:
+            c.wait()
+        for t in range(p * size // 8, (p + 1) * size // 8):
+            columns(t)
+
     even = lax.rem(lax.axis_index("gy"), 2) == 0
     s0_flat, mk_flat = flat(s0), flat(mk)
     stride = h_n * nyp
-    group = lane // 8
-
-    def arrived(f):
-        for c in copies[f * h_n : (f + 1) * h_n]:
-            c.wait()
-
-    def pack_columns(a):
-        def tile(t, carry):
-            y = pl.multiple_of(PAD + t * 8, 8)
-            yo = pl.multiple_of(t * 8, 8)
-            acc = jnp.zeros((8, LANES), jnp.float32)
-            for g in range(16 if a < 2 else 8):
-                f, x = a * 2 + g // 8, g % 8
-                if a < 2:
-                    lo, hi = s0[f, x, 0, pl.ds(y, 8), :], s0[f, x, h_n - 1, pl.ds(y, 8), :]
-                else:
-                    lo, hi = mk[x, 0, pl.ds(y, 8), :], mk[x, h_n - 1, pl.ds(y, 8), :]
-                both = jnp.where(lane < LANES // 2, lo, hi).astype(jnp.float32)
-                acc = jnp.where(group == g, pltpu.roll(both, (g * 8 + 4) % LANES, 1), acc)
-            part[a, pl.ds(yo, 8), :] = acc
-            return carry
-
-        lax.fori_loop(0, ny // 8, tile, 0, unroll=4)
-        for b in range(ny // LANES):
-            turned[a, b] = part[a, b * LANES : (b + 1) * LANES, :].T
-
-    def rows(dst, ys):
-        for r, y in enumerate(ys):
-            for h in range(h_n):
-                cols = slice(h * LANES, (h + 1) * LANES)
-                for f in range(4):
-                    block = row_of(s0_flat, (f * x_n * h_n + h) * nyp, stride, PAD + y, x_n)
-                    dst[(r * 4 + f) * 8 : (r * 4 + f) * 8 + 8, cols] = block
-                if r == 0:
-                    block = row_of(mk_flat, h * nyp, stride, PAD + y, x_n)
-                    dst[64:72, cols] = block.astype(jnp.float32)
-
-    for a, fields in enumerate(((0, 1), (2, 3), (4,))):
-        for f in fields:
-            arrived(f)
-        pack_columns(a)
-
-    first, last = (0, 1), (ny - 1, ny - 2)
-
-    @pl.when(even)
-    def _():
-        rows(ys_a, last)
-        rows(ys_b, first)
-
-    @pl.when(jnp.logical_not(even))
-    def _():
-        rows(ys_a, first)
-        rows(ys_b, last)
-
-    for side in range(2):
-        for l in range(4):
-            j = 4 + l if side == 0 else 3 - l
-            for b in range(ny // LANES):
-                cols = slice(b * LANES, (b + 1) * LANES)
+    for h in range(h_n):
+        cols = slice(h * LANES, (h + 1) * LANES)
+        for k in range(9):
+            r, f = k // 4 % 2, k % 4
+
+            def row(y):
+                if k == 8:
+                    return row_of(mk_flat, h * nyp, stride, PAD + y, x_n).astype(jnp.float32)
+                return row_of(s0_flat, (f * x_n * h_n + h) * nyp, stride, PAD + y, x_n)
+
+            first, last = row(r), row(ny - 1 - r)
+            ys_a[k * 8 : k * 8 + 8, cols] = jnp.where(even, last, first)
+            ys_b[k * 8 : k * 8 + 8, cols] = jnp.where(even, first, last)
+
+    bit = jnp.zeros((8, LANES), jnp.int32)
+    for x in range(x_n):
+        bit = jnp.where(sub == x, 1 << x, bit)
+    for b in range(ny // LANES):
+        cols = slice(b * LANES, (b + 1) * LANES)
+        for a in range(3):
+            turned[a, b] = part[a, cols, :].T
+        for side in range(2):
+            for l in range(4):
+                j = 4 + l if side == 0 else 3 - l
                 for f in range(4):
                     k = f * 4 + l
                     zown[side, k * 8 : k * 8 + 8, cols] = turned[
                         f // 2, b, pl.ds((f % 2) * 64 + j, 8, stride=8), :
                     ]
                 if l < 3:
-                    k = 16 + l
-                    zown[side, k * 8 : k * 8 + 8, cols] = turned[2, b, pl.ds(j, 8, stride=8), :]
+                    k, at = 16 + l, l if side == 0 else LANES - 1 - l
+                    row = jnp.broadcast_to(turned[2, b, at : at + 1, :], (8, LANES))
+                    has = jnp.bitwise_and(row.astype(jnp.int32), bit) != 0
+                    zown[side, k * 8 : k * 8 + 8, cols] = jnp.where(has, 1.0, 0.0)
 
 
 def y_halo(even, a_ref, b_ref, k, cols):
@@ -206,7 +200,7 @@
     return out
 
 
-def corner_kernel(dims, ya, yb, zown, after, zs_a, zs_b):
+def corner_kernel(dims, yb, ya, zown, after, zs_a, zs_b):
     del after
     x_n, h_n, ny = dims
     lane = lane_iota()
@@ -266,19 +260,67 @@
                 s1[f, x, h, pl.ds(y, 8), :] = jnp.where(open_cell, r[f], 0.0)
 
     def body(t, carry):
-        for j in range(2):
-            y = pl.multiple_of(PAD + t * 16 + j * 8, 8)
+        for j in range(4):
+            y = pl.multiple_of(PAD + t * 32 + j * 8, 8)
             for x in range(x_n):
                 tile(y, x)
         return carry
 
-    lax.fori_loop(0, ny // 16, body, 0)
-
-
-def section_two_kernel(dims, s0, mk, s1, s2, path, acc):
+    lax.fori_loop(0, ny // 32, body, 0)
+
+
+def outer_rows(dims, s0, mk, ya, yb, s1):
+    x_n, h_n, ny = dims
+    nyp = ny + 2 * PAD
+    lane = lane_iota()
+    even = lax.rem(lax.axis_index("gy"), 2) == 0
+    s0_flat, s1_flat, mk_flat = flat(s0), flat(s1), flat(mk)
+    stride = h_n * nyp
+    blk = [slice(h * LANES, (h + 1) * LANES) for h in range(h_n)]
+    for side in range(2):
+
+        def start(f, h, r):
+            return (f * x_n * h_n + h) * nyp + PAD + (r if side == 0 else ny - 1 - r)
+
+        def halo(k):
+            return [y_halo(even, ya, yb, k, blk[h])[side] for h in range(h_n)]
+
+        zero = {-2: [halo(4 + f) for f in range(4)], -1: [halo(f) for f in range(4)]}
+        for r in range(2):
+            zero[r] = [
+                [row_of(s0_flat, 0, stride, start(f, h, r), x_n) for h in range(h_n)]
+                for f in range(4)
+            ]
+        open_at = {
+            -1: [m != 0.0 for m in halo(8)],
+            0: [row_of(mk_flat, 0, stride, start(0, h, 0), x_n) != 0 for h in range(h_n)],
+        }
+        for r in (-1, 0):
+            pairs = [height_pair(zero[r][f], lane) for f in range(4)]
+            ahead, behind = (r + 1, r - 1) if side == 0 else (r - 1, r + 1)
+            for h in range(h_n):
+                c = [zero[r][f][h] for f in range(4)]
+                q = stepped(
+                    c,
+                    c,
+                    [east(v) for v in c],
+                    [west(v) for v in c],
+                    [zero[ahead][f][h] for f in range(4)],
+                    [zero[behind][f][h] for f in range(4)],
+                    [p[0][h] for p in pairs],
+                    [p[1][h] for p in pairs],
+                    1.0,
+                )
+                for f in range(4):
+                    v = q[f] if f == 0 else jnp.where(open_at[r][h], q[f], 0.0)
+                    s1_flat[pl.ds(start(f, h, r), x_n, stride=stride), :] = v
+
+
+def section_two_kernel(dims, s0, mk, s1_in, yb, ya, s2, path, s1, acc):
+    del s1_in
     x_n, h_n, ny = dims
     lane = lane_iota()
-    sub = lax.broadcasted_iota(jnp.int32, (8, LANES), 0)
+    outer_rows(dims, s0, mk, ya, yb, s1)
 
     def tile(y, yo, x):
         c = [load4(s1, x, h, y) for h in range(h_n)]
@@ -311,119 +353,34 @@
         return total
 
     def body(t, carry):
-        for j in range(2):
-            y = pl.multiple_of(PAD + t * 16 + j * 8, 8)
-            yo = pl.multiple_of(t * 16 + j * 8, 8)
+        for j in range(4):
+            y = pl.multiple_of(PAD + t * 32 + j * 8, 8)
+            yo = pl.multiple_of(t * 32 + j * 8, 8)
             for x in range(x_n):
                 acc[x, pl.ds(yo, 8), :] = tile(y, yo, x)
         return carry
 
-    lax.fori_loop(0, ny // 16, body, 0)
-    ones = jnp.ones((LANES, LANES), jnp.bfloat16)
-    diagonal = lax.broadcasted_iota(jnp.int32, (LANES, LANES), 0) == lax.broadcasted_iota(
-        jnp.int32, (LANES, LANES), 1
-    )
-    for b in range(ny // LANES):
-        cols = slice(b * LANES, (b + 1) * LANES)
-        rows = jnp.concatenate([acc[x, cols, :] for x in range(x_n)], axis=0)
-        high = rows.astype(jnp.bfloat16)
-        rest = (rows - high.astype(jnp.float32)).astype(jnp.bfloat16)
-        sums = jnp.dot(high, ones, preferred_element_type=jnp.float32)
-        sums = sums + jnp.dot(rest, ones, preferred_element_type=jnp.float32)
-        for x in range(x_n):
-            one = jnp.where(diagonal, sums[x * LANES : (x + 1) * LANES], 0.0)
-            path[x : x + 1, cols] = jnp.sum(one, axis=0, keepdims=True)
+    lax.fori_loop(0, ny // 32, body, 0)
+    for x in range(x_n):
+        for b in range(ny // LANES):
+            cols = slice(b * LANES, (b + 1) * LANES)
+            path[x : x + 1, cols] = jnp.sum(acc[x, cols, :].T, axis=0, keepdims=True)
 
 
 def edge_kernel(dims, count_z, *refs):
     x_n, h_n, ny = dims
-    s0, mk, s1, zown, ya, yb, za, zb, path_in = refs[:9]
-    zp, yp, own = refs[9:12]
-    sends = refs[12 : 12 + count_z - 1]
-    turned, path = refs[12 + count_z - 1 :]
-    nyp = ny + 2 * PAD
+    zown, yb, ya, zb, za, path_in = refs[:6]
+    zp, own = refs[6:8]
+    sends = refs[8 : 8 + count_z - 1]
+    turned, path = refs[8 + count_z - 1 :]
     nb = ny // LANES
     lane = lane_iota()
     even = lax.rem(lax.axis_index("gy"), 2) == 0
     gz = lax.axis_index("gz")
     even_z = lax.rem(gz, 2) == 0
-    s0_flat, s1_flat, mk_flat = flat(s0), flat(s1), flat(mk)
-    stride = h_n * nyp
-    blk = [slice(b * LANES, (b + 1) * LANES) for b in range(max(nb, h_n))]
-
-    y_sums = []
-    for side in range(2):
-
-        def at(r):
-            return PAD + (r if side == 0 else ny - 1 - r)
-
-        def own_rows(ref, r):
-            return [
-                [row_of(ref, (f * x_n * h_n + h) * nyp, stride, at(r), x_n) for h in range(h_n)]
-                for f in range(4)
-            ]
-
-        def halo(k):
-            return [y_halo(even, ya, yb, k, blk[h])[side] for h in range(h_n)]
-
-        zero = {
-            -2: [halo(4 + f) for f in range(4)],
-            -1: [halo(f) for f in range(4)],
-        }
-        for r in range(3):
-            zero[r] = own_rows(s0_flat, r)
-        open_at = {-1: [m != 0.0 for m in halo(8)]}
-        for r in range(2):
-            open_at[r] = [
-                row_of(mk_flat, h * nyp, stride, at(r), x_n) != 0 for h in range(h_n)
-            ]
-        one = {r: own_rows(s1_flat, r) for r in (1, 2)}
-
-        def advance(state, base, r, scale, fields=4):
-            pairs = [height_pair(state[r][f], lane) for f in range(4)]
-            ahead, behind = (r + 1, r - 1) if side == 0 else (r - 1, r + 1)
-            out = [[None] * h_n for _ in range(4)]
-            for h in range(h_n):
-                c = [state[r][f][h] for f in range(4)]
-                q = stepped(
-                    [base[f][h] for f in range(4)],
-                    c,
-                    [east(v) for v in c],
-                    [west(v) for v in c],
-                    [state[ahead][f][h] for f in range(4)],
-                    [state[behind][f][h] for f in range(4)],
-                    [p[0][h] for p in pairs],
-                    [p[1][h] for p in pairs],
-                    scale,
-                )
-                for f in range(4):
-                    out[f][h] = q[f] if f == 0 else jnp.where(open_at[r][h], q[f], 0.0)
-            return out
-
-        for r in (-1, 0):
-            one[r] = advance(zero, zero[r], r, 1.0)
-        for r in (0, 1):
-            base = [
-                [0.5 * (zero[r][f][h] + one[r][f][h]) for h in range(h_n)] for f in range(4)
-            ]
-            two = advance(one, base, r, 0.5)
-            for f in range(4):
-                for h in range(h_n):
-                    yp[side * 8 + r * 4 + f, :, blk[h]] = two[f][h]
-            total = None
-            for h in range(h_n):
-                refr = 1.0 - jnp.exp(two[0][h] * (-0.125))
-                if h == 0:
-                    refr = jnp.where(lane < 2, 0.0, refr)
-                if h == h_n - 1:
-                    refr = jnp.where(lane >= LANES - 2, 0.0, refr)
-                total = refr if total is None else total + refr
-            y_sums.append((r if side == 0 else ny - 1 - r, jnp.sum(total, axis=1, keepdims=True)))
+    blk = [slice(b * LANES, (b + 1) * LANES) for b in range(nb)]
 
     sums = [path_in[:, blk[b]] for b in range(nb)]
-    for y, value in y_sums:
-        b = y // LANES
-        sums[b] = jnp.where(lane == y % LANES, value, sums[b])
 
     for side in range(2):
         exists = (gz > 0) if side == 0 else (gz < count_z - 1)
@@ -507,49 +464,31 @@
             sends[k - 1][:, blk[b]] = path[b, pl.ds((gz ^ k) * per, per), :]
 
 
-def write_kernel(dims, s2, zp, yp, *refs):
+def write_kernel(dims, pieces, s2, zp, *refs):
     x_n, h_n, ny = dims
     outs, (buf, sem) = refs[:4], refs[4:]
     lane = lane_iota()
-    sub = lax.broadcasted_iota(jnp.int32, (8, LANES), 0)
-    tiles = ny // 8
+    size = x_n // pieces
     copies = []
     for f in range(4):
         for x in range(x_n):
-            shift = (LANES - ((f * x_n + x) * 4 + 2)) % LANES
-
-            def tile(t, f=f, x=x, shift=shift):
-                y = t * 8
-                edge = pltpu.roll(zp[pl.ds(y, 8), :], shift, 1)
+            for t in range(ny // 8):
+                rows = slice(t * 8, t * 8 + 8)
+                edge = pltpu.roll(zp[rows, :], (LANES - ((f * x_n + x) * 4 + 2)) % LANES, 1)
                 for h in range(h_n):
                     cols = slice(h * LANES, (h + 1) * LANES)
-                    v = s2[f, x, pl.ds(y, 8), cols]
+                    v = s2[f, x, rows, cols]
                     if h == 0:
                         v = jnp.where(lane < 2, edge, v)
                     if h == h_n - 1:
                         v = jnp.where(lane >= LANES - 2, edge, v)
-                    buf[f, x, pl.ds(y, 8), cols] = v
-
-            for t in range(tiles):
-                tile(t)
-            for side in range(2):
-                t = 0 if side == 0 else tiles - 1
-                for h in range(h_n):
-                    cols = slice(h * LANES, (h + 1) * LANES)
-                    v = buf[f, x, t * 8 : t * 8 + 8, cols]
-                    for r in range(2):
-                        at = r if side == 0 else 7 - r
-                        row = yp[side * 8 + r * 4 + f, x : x + 1, cols]
-                        keep = sub == at
-                        if h == 0:
-                            keep = keep & (lane >= 2)
-                        if h == h_n - 1:
-                            keep = keep & (lane < LANES - 2)
-                        v = jnp.where(keep, row, v)
-                    buf[f, x, t * 8 : t * 8 + 8, cols] = v
-        copy = pltpu.make_async_copy(buf.at[f], outs[f], sem.at[f])
-        copy.start()
-        copies.append(copy)
+                    buf[f, x, rows, cols] = v
+            if (x + 1) % size == 0:
+                part = pl.ds(x + 1 - size, size)
+                copies.append(
+                    pltpu.make_async_copy(buf.at[f, part], outs[f].at[part], sem.at[f, x // size])
+                )
+                copies[-1].start()
     for c in copies:
         c.wait()
 
@@ -588,7 +527,7 @@
         return pl.CostEstimate(flops=flops, bytes_accessed=moved, transcendentals=0)
 
     s0, mk, ys_a, ys_b, zown = pl.pallas_call(
-        functools.partial(pack_kernel, dims),
+        functools.partial(pack_kernel, dims, 2),
         out_shape=(
             fields,
             pltpu.VMEM((x_n, h_n, nyp, LANES), jnp.int32),
@@ -601,15 +540,15 @@
         scratch_shapes=[
             pltpu.VMEM((3, ny, LANES), f32),
             pltpu.VMEM((3, ny // LANES, LANES, LANES), f32),
-            pltpu.SemaphoreType.DMA((5, h_n)),
+            pltpu.SemaphoreType.DMA((2, 5, h_n)),
         ],
         compiler_params=params(),
         name="load_and_pack",
     )(*args)
 
     y_pairs = pairs_of(count_y)
+    yb = lax.ppermute(ys_b, "gy", y_pairs[1])
     ya = lax.ppermute(ys_a, "gy", y_pairs[0])
-    yb = lax.ppermute(ys_b, "gy", y_pairs[1])
 
     s1 = pl.pallas_call(
         functools.partial(section_one_kernel, dims),
@@ -628,57 +567,61 @@
         out_specs=(VMEM,) * 2,
         compiler_params=params(),
         name="corners",
-    )(ya, yb, zown, s1)
-
+    )(yb, ya, zown, s1)
+
+    zb = lax.ppermute(zs_b, ("gz", "gy"), inner_pairs(count_z, count_y))
     za = lax.ppermute(zs_a, "gz", pairs_of(count_z)[0])
-    zb = lax.ppermute(zs_b, ("gz", "gy"), inner_pairs(count_z, count_y))
-
-    s2, path = pl.pallas_call(
+
+    s2, path, _ = pl.pallas_call(
         functools.partial(section_two_kernel, dims),
-        out_shape=(pltpu.VMEM((4, x_n, ny, nz), f32), jax.ShapeDtypeStruct((x_n, ny), f32)),
-        in_specs=[VMEM] * 3,
-        out_specs=(VMEM,) * 2,
+        out_shape=(
+            pltpu.VMEM((4, x_n, ny, nz), f32),
+            jax.ShapeDtypeStruct((x_n, ny), f32),
+            fields,
+        ),
+        in_specs=[VMEM] * 5,
+        out_specs=(VMEM,) * 3,
+        input_output_aliases={2: 2},
         scratch_shapes=[pltpu.VMEM((x_n, ny, LANES), f32)],
         compiler_params=params(),
         cost_estimate=cost(110 * cells, 52 * cells),
         name="section_two",
-    )(s0, mk, s1)
+    )(s0, mk, s1, yb, ya)
 
     per, nb = x_n // count_z, ny // LANES
     edges = pl.pallas_call(
         functools.partial(edge_kernel, dims, count_z),
         out_shape=(
             jax.ShapeDtypeStruct((ny, LANES), f32),
-            jax.ShapeDtypeStruct((16, 8, nz), f32),
         )
         + (jax.ShapeDtypeStruct((per, ny), f32),) * count_z,
-        in_specs=[VMEM] * 9,
-        out_specs=(VMEM,) * (2 + count_z),
+        in_specs=[VMEM] * 6,
+        out_specs=(VMEM,) * (1 + count_z),
         scratch_shapes=[
             pltpu.VMEM((nb, LANES, LANES), f32),
             pltpu.VMEM((nb, x_n, LANES), f32),
         ],
         compiler_params=params(),
         name="edges",
-    )(s0, mk, s1, zown, ya, yb, za, zb, path)
-    zp, yp, own = edges[:3]
+    )(zown, yb, ya, zb, za, path)
+    zp, own = edges[:2]
 
     total = own
     for k in range(count_z - 1, 0, -1):
         total = total + lax.ppermute(
-            edges[2 + k], "gz", [(i, i ^ k) for i in range(count_z)]
+            edges[1 + k], "gz", [(i, i ^ k) for i in range(count_z)]
         )
 
     outs = pl.pallas_call(
-        functools.partial(write_kernel, dims),
+        functools.partial(write_kernel, dims, 4),
         out_shape=(pltpu.HBM((x_n, ny, nz), f32),) * 4,
-        in_specs=[VMEM] * 3,
+        in_specs=[VMEM] * 2,
         out_specs=(HBM,) * 4,
-        scratch_shapes=[pltpu.VMEM((4, x_n, ny, nz), f32), pltpu.SemaphoreType.DMA((4,))],
+        scratch_shapes=[pltpu.VMEM((4, x_n, ny, nz), f32), pltpu.SemaphoreType.DMA((4, 4))],
         compiler_params=params(),
         cost_estimate=cost(cells, 32 * cells),
         name="write",
-    )(s2, zp, yp)
+    )(s2, zp)
     return (*outs, total)
 
 

time: 31 us -> 29.1 us (0.939)
  Pallas kernels: 17.6 us -> 16.6 us
  waiting for transfers between devices: 0.67 us -> 0.02 us
    ppermute x3, starting transfers between devices: 5.65 us -> 4.45 us  [on_device(): lax.ppermute(edges[1 + k], 'gz', [(i, i ^ k) for i in range(count_z)])]
    ppermute x1, starting transfers between devices: 1.59 us -> 2.65 us  [on_device(): za = lax.ppermute(zs_a, 'gz', pairs_of(count_z)[0])]
    ppermute x3, waiting for transfers between devices: 0.66 us -> 0.01 us  [on_device(): lax.ppermute(edges[1 + k], 'gz', [(i, i ^ k) for i in range(count_z)])]
    ppermute x1, starting transfers between devices: 0.54 us -> 0.01 us  [on_device(): ya = lax.ppermute(ys_a, 'gy', y_pairs[0])]
    pallas_call x1, Pallas kernels: 1.13 us -> 0.59 us  [on_device(): pl.pallas_call(functools.partial(edge_kernel, dims, count_z), out_shape=(...]
    ppermute x1, starting transfers between devices: 0.01 us -> 0.52 us  [on_device(): zb = lax.ppermute(zs_b, ('gz', 'gy'), inner_pairs(count_z, count_y))]
    pallas_call x2, Pallas kernels: 5.83 us -> 5.51 us  [the longest x1 3.28 us: on_device(): pl.pallas_call(functools.partial(pack_kernel, dims, 2), out_shape=(fields...]
  transfers between devices with their start and end apart: 7 -> 7, of which waited for: 1 -> 0; matrix products, arithmetic and copies ran while one was open for 0% -> 0% of each run, Pallas kernels for 41% -> 44%
where the time goes in v3:
time: 29.1 us; the launch traced here: 29 us
  Pallas kernels  16.6 us (57%)
  starting transfers between devices  11 us (38%)
  between operations  0.73 us (3%)
  other arithmetic  0.57 us (2%)
    pallas_call x1, Pallas kernels, on_device(): pl.pallas_call(functools.partial(section_two_kernel, dims), out_shape=(pl...  5.68 us
    pallas_call x1, Pallas kernels, on_device(): pl.pallas_call(functools.partial(section_one_kernel, dims), out_shape=fie...  4.78 us
    ppermute x3, starting transfers between devices, on_device(): lax.ppermute(edges[1 + k], 'gz', [(i, i ^ k) for i in range(count_z)])  4.45 us
    ppermute x1, starting transfers between devices, on_device(): yb = lax.ppermute(ys_b, 'gy', y_pairs[1])  3.4 us
    pallas_call x1, Pallas kernels, on_device(): pl.pallas_call(functools.partial(pack_kernel, dims, 2), out_shape=(fields...  3.28 us
    ppermute x1, starting transfers between devices, on_device(): za = lax.ppermute(zs_a, 'gz', pairs_of(count_z)[0])  2.65 us
    pallas_call x1, Pallas kernels, on_device(): pl.pallas_call(functools.partial(write_kernel, dims, 4), out_shape=(pltpu...  2.23 us
    pallas_call x1, Pallas kernels, on_device(): pl.pallas_call(functools.partial(edge_kernel, dims, count_z), out_shape=(...  0.59 us
  transfers between devices with their start and end apart: 7, of which 0 were waited for; matrix products, arithmetic and copies ran while one was open for 0% of the time, Pallas kernels for 44%

profile of v3, /device:TPU:0, one launch (start us, length us, event | category | flops | bytes accessed | tf_op | source)
XLA Modules:
  0.0 29.0 jit_solution(714557951728367451)
XLA Ops:
  0.6 3.3 %load_and_pack.1 = (f32[4,8,2,144,128]{4,3,2,1,0:T(8,128)S(1)}, s32[8,2,144,128]{3,2,1,0:T(8,128)S(1)}, f32[72,256]{1,0:T(8,128)S(1)}, f32[72,256]{1,0:T(8,128)S(1)}, f32[2,152,128]{2,1,0:T(8,128)S(1)}) custom-call(f32[8,128,256]{2,1,0:T(8,128)} %refs_0_.1, f32[8,128,256]{2,1,0:T(8,128)} %refs_1_.1, f32[8,128,256]{2,1,0:T(8,128)} %refs_2_.1, ...), custom_call_target="tpu_custom_call" | custom-call | tf_op jit(solution)/shard_map/load_and_pack/pallas_call | solution.py:529
  3.9 3.4 %collective-permute-start = (f32[72,256]{1,0:T(8,128)S(1)}, f32[72,256]{1,0:T(8,128)S(1)}, u32[]{:S(2)}, u32[]{:S(2)}) collective-permute-start(f32[72,256]{1,0:T(8,128)S(1)} %get-tuple-element.25), channel_id=1, source_target_pairs={{0,7},{1,2},{2,1},{3,4},{4,3},{5,6},{6,5},{7,0},{8,15},{9,10},{10,... | collective-permute-start | bytes 221192 | tf_op jit(solution)/shard_map/ppermute | solution.py:550
  7.3 0.0 collective-permute-start.1
  7.3 4.8 %section_one.1.s1_in.after = f32[4,8,2,144,128]{4,3,2,1,0:T(8,128)S(1)} custom-call(f32[4,8,2,144,128]{4,3,2,1,0:T(8,128)S(1)} %get-tuple-element.23.s0, s32[8,2,144,128]{3,2,1,0:T(8,128)S(1)} %get-tuple-element.24.mk), custom_call_target="tpu_custom_call" | custom-call | flops 26214400 | bytes 9437184 | tf_op jit(solution)/shard_map/section_one/pallas_call | solution.py:553
  12.1 0.0 collective-permute-done.yb.refs_1_
  12.1 0.0 collective-permute-done.1.ya.refs_2_
  12.1 0.1 corners.1
  12.2 0.5 %collective-permute-start.2 = (f32[104,128]{1,0:T(8,128)S(1)}, f32[104,128]{1,0:T(8,128)S(1)}, u32[]{:S(2)}, u32[]{:S(2)}) collective-permute-start(f32[104,128]{1,0:T(8,128)S(1)} %get-tuple-element.29), channel_id=1, source_target_pairs={{0,1},{1,0},{2,3},{3,2},{4,5},{5,4},{6,7},{7,6},{8,16},{9,17},{10,... | collective-permute-start | bytes 159752 | tf_op jit(solution)/shard_map/ppermute | solution.py:572
  12.7 2.6 %collective-permute-start.3 = (f32[104,128]{1,0:T(8,128)S(1)}, f32[104,128]{1,0:T(8,128)S(1)}, u32[]{:S(2)}, u32[]{:S(2)}) collective-permute-start(f32[104,128]{1,0:T(8,128)S(1)} %get-tuple-element.30), channel_id=1, source_target_pairs={{0,8},{8,0},{16,24},{24,16},{1,9},{9,1},{17,25},{25,17},{2,10},{10... | collective-permute-start | bytes 159752 | tf_op jit(solution)/shard_map/ppermute | solution.py:573
  15.4 5.7 %section_two.1 = (f32[4,8,128,256]{3,2,1,0:T(8,128)S(1)}, f32[8,128]{1,0:T(8,128)S(1)}, f32[4,8,2,144,128]{4,3,2,1,0:T(8,128)S(1)}) custom-call(f32[4,8,2,144,128]{4,3,2,1,0:T(8,128)S(1)} %get-tuple-element.23.s0, s32[8,2,144,128]{3,2,1,0:T(8,128)S(1)} %get-tuple-element.24.mk, ...), custom_call_target="tpu_custom_call", output_to_operand_aliasing={{2}: (2, {})} | custom-call | flops 28835840 | bytes 13631488 | tf_op jit(solution)/shard_map/section_two/pallas_call | solution.py:575
  21.1 0.0 collective-permute-done.2.refs_3_
  21.1 0.0 collective-permute-done.3.refs_4_
  21.1 0.6 %edges.1 = (f32[128,128]{1,0:T(8,128)S(1)}, f32[2,128]{1,0:T(2,128)S(1)}, f32[2,128]{1,0:T(2,128)S(1)}, f32[2,128]{1,0:T(2,128)S(1)}, f32[2,128]{1,0:T(2,128)S(1)}) custom-call(f32[2,152,128]{2,1,0:T(8,128)S(1)} %get-tuple-element.28.zown.refs_0_, f32[72,256]{1,0:T(8,128)S(1)} %collective-permute-done.yb.refs_1_, ...), custom_call_target="tpu_custom_call" | custom-call | tf_op jit(solution)/shard_map/edges/pallas_call | solution.py:592
  21.7 1.4 %collective-permute-start.4 = (f32[2,128]{1,0:T(2,128)S(1)}, f32[2,128]{1,0:T(2,128)S(1)}, u32[]{:S(2)}, u32[]{:S(2)}) collective-permute-start(f32[2,128]{1,0:T(2,128)S(1)} %get-tuple-element.38), channel_id=1, source_target_pairs={{0,24},{8,16},{16,8},{24,0},{1,25},{9,17},{17,9},{25,1},{2,26},{10... | collective-permute-start | bytes 3080 | tf_op jit(solution)/shard_map/ppermute | solution.py:611
  23.1 0.2 collective-permute-start.5
  23.4 2.8 %collective-permute-start.6 = (f32[2,128]{1,0:T(2,128)S(1)}, f32[2,128]{1,0:T(2,128)S(1)}, u32[]{:S(2)}, u32[]{:S(2)}) collective-permute-start(f32[2,128]{1,0:T(2,128)S(1)} %get-tuple-element.40), channel_id=1, source_target_pairs={{0,8},{8,0},{16,24},{24,16},{1,9},{9,1},{17,25},{25,17},{2,10},{10... | collective-permute-start | bytes 3080 | tf_op jit(solution)/shard_map/ppermute | solution.py:611
  26.2 2.2 %write.1 = (f32[8,128,256]{2,1,0:T(8,128)}, f32[8,128,256]{2,1,0:T(8,128)}, f32[8,128,256]{2,1,0:T(8,128)}, f32[8,128,256]{2,1,0:T(8,128)}) custom-call(f32[4,8,128,256]{3,2,1,0:T(8,128)S(1)} %get-tuple-element.27.s2, f32[128,128]{1,0:T(8,128)S(1)} %get-tuple-element.32.zp), custom_call_target="tpu_custom_call" | custom-call | flops 262144 | bytes 8388608 | tf_op jit(solution)/shard_map/write/pallas_call | solution.py:615
  28.4 0.0 collective-permute-done.4
  28.4 0.0 collective-permute-done.5
  28.4 0.0 collective-permute-done.6
  28.4 0.6 %add_add_fusion = f32[2,128]{1,0:T(2,128)} fusion(f32[2,128]{1,0:T(2,128)S(1)} %collective-permute-done.6, f32[2,128]{1,0:T(2,128)S(1)} %collective-permute-done.5, f32[2,128]{1,0:T(2,128)S(1)} %get-tuple-element.37, f32[2,128]{1,0:T(2,128)S(1)} %collective-permute-done.4), kind=kLoop, calls=%fused_computation | loop fusion | flops 768 | bytes 5120 | tf_op jit(solution)/shard_map/add | solution.py:611
Async XLA Ops:
  3.9 8.2 %collective-permute-start = (f32[72,256]{1,0:T(8,128)S(1)}, f32[72,256]{1,0:T(8,128)S(1)}, u32[]{:S(2)}, u32[]{:S(2)}) collective-permute-start(f32[72,256]{1,0:T(8,128)S(1)} %get-tuple-element.25), channel_id=1, source_target_pairs={{0,7},{1,2},{2,1},{3,4},{4,3},{5,6},{6,5},{7,0},{8,15},{9,10},{10,... | collective-permute-start | bytes 221192 | tf_op jit(solution)/shard_map/ppermute | solution.py:550
  7.3 4.8 %collective-permute-start.1 = (f32[72,256]{1,0:T(8,128)S(1)}, f32[72,256]{1,0:T(8,128)S(1)}, u32[]{:S(2)}, u32[]{:S(2)}) collective-permute-start(f32[72,256]{1,0:T(8,128)S(1)} %get-tuple-element.26), channel_id=1, source_target_pairs={{0,1},{1,0},{2,3},{3,2},{4,5},{5,4},{6,7},{7,6},{8,9},{9,8},{10,11... | collective-permute-start | bytes 221192 | tf_op jit(solution)/shard_map/ppermute | solution.py:551
  12.2 8.9 %collective-permute-start.2 = (f32[104,128]{1,0:T(8,128)S(1)}, f32[104,128]{1,0:T(8,128)S(1)}, u32[]{:S(2)}, u32[]{:S(2)}) collective-permute-start(f32[104,128]{1,0:T(8,128)S(1)} %get-tuple-element.29), channel_id=1, source_target_pairs={{0,1},{1,0},{2,3},{3,2},{4,5},{5,4},{6,7},{7,6},{8,16},{9,17},{10,... | collective-permute-start | bytes 159752 | tf_op jit(solution)/shard_map/ppermute | solution.py:572
  12.7 8.3 %collective-permute-start.3 = (f32[104,128]{1,0:T(8,128)S(1)}, f32[104,128]{1,0:T(8,128)S(1)}, u32[]{:S(2)}, u32[]{:S(2)}) collective-permute-start(f32[104,128]{1,0:T(8,128)S(1)} %get-tuple-element.30), channel_id=1, source_target_pairs={{0,8},{8,0},{16,24},{24,16},{1,9},{9,1},{17,25},{25,17},{2,10},{10... | collective-permute-start | bytes 159752 | tf_op jit(solution)/shard_map/ppermute | solution.py:573
  21.7 6.7 %collective-permute-start.4 = (f32[2,128]{1,0:T(2,128)S(1)}, f32[2,128]{1,0:T(2,128)S(1)}, u32[]{:S(2)}, u32[]{:S(2)}) collective-permute-start(f32[2,128]{1,0:T(2,128)S(1)} %get-tuple-element.38), channel_id=1, source_target_pairs={{0,24},{8,16},{16,8},{24,0},{1,25},{9,17},{17,9},{25,1},{2,26},{10... | collective-permute-start | bytes 3080 | tf_op jit(solution)/shard_map/ppermute | solution.py:611
  23.1 5.3 %collective-permute-start.5 = (f32[2,128]{1,0:T(2,128)S(1)}, f32[2,128]{1,0:T(2,128)S(1)}, u32[]{:S(2)}, u32[]{:S(2)}) collective-permute-start(f32[2,128]{1,0:T(2,128)S(1)} %get-tuple-element.39), channel_id=1, source_target_pairs={{0,16},{8,24},{16,0},{24,8},{1,17},{9,25},{17,1},{25,9},{2,18},{10... | collective-permute-start | bytes 3080 | tf_op jit(solution)/shard_map/ppermute | solution.py:611
  23.4 5.1 %collective-permute-start.6 = (f32[2,128]{1,0:T(2,128)S(1)}, f32[2,128]{1,0:T(2,128)S(1)}, u32[]{:S(2)}, u32[]{:S(2)}) collective-permute-start(f32[2,128]{1,0:T(2,128)S(1)} %get-tuple-element.40), channel_id=1, source_target_pairs={{0,8},{8,0},{16,24},{24,16},{1,9},{9,1},{17,25},{25,17},{2,10},{10... | collective-permute-start | bytes 3080 | tf_op jit(solution)/shard_map/ppermute | solution.py:611

commit v4 on v3

--- a/solution.py
+++ b/solution.py
@@ -259,14 +259,9 @@
             for f in range(1, 4):
                 s1[f, x, h, pl.ds(y, 8), :] = jnp.where(open_cell, r[f], 0.0)
 
-    def body(t, carry):
-        for j in range(4):
-            y = pl.multiple_of(PAD + t * 32 + j * 8, 8)
-            for x in range(x_n):
-                tile(y, x)
-        return carry
-
-    lax.fori_loop(0, ny // 32, body, 0)
+    for t in range(ny // 8):
+        for x in range(x_n):
+            tile(PAD + t * 8, x)
 
 
 def outer_rows(dims, s0, mk, ya, yb, s1):
@@ -316,11 +311,10 @@
                     s1_flat[pl.ds(start(f, h, r), x_n, stride=stride), :] = v
 
 
-def section_two_kernel(dims, s0, mk, s1_in, yb, ya, s2, path, s1, acc):
+def section_two_kernel(dims, s0, mk, s1_in, yb, ya, s2, acc, s1):
     del s1_in
     x_n, h_n, ny = dims
     lane = lane_iota()
-    outer_rows(dims, s0, mk, ya, yb, s1)
 
     def tile(y, yo, x):
         c = [load4(s1, x, h, y) for h in range(h_n)]
@@ -352,24 +346,42 @@
             total = refr if total is None else total + refr
         return total
 
-    def body(t, carry):
-        for j in range(4):
-            y = pl.multiple_of(PAD + t * 32 + j * 8, 8)
-            yo = pl.multiple_of(t * 32 + j * 8, 8)
+    def tiles(places):
+        for t in places:
             for x in range(x_n):
-                acc[x, pl.ds(yo, 8), :] = tile(y, yo, x)
-        return carry
-
-    lax.fori_loop(0, ny // 32, body, 0)
+                acc[x, t * 8 : t * 8 + 8, :] = tile(PAD + t * 8, t * 8, x)
+
+    last = ny // 8 - 1
+    tiles(range(1, last))
+    outer_rows(dims, s0, mk, ya, yb, s1)
+    tiles((0, last))
+
+
+def lane_sums(acc, b):
+    x_n = acc.shape[0]
+    rows = acc[:, b * LANES : (b + 1) * LANES, :].reshape(x_n * LANES, LANES)
+    ones = jnp.ones((LANES, LANES), jnp.bfloat16)
+    total = None
+    for _ in range(3):
+        piece = rows.astype(jnp.bfloat16)
+        rows = rows - piece.astype(jnp.float32)
+        got = jnp.dot(piece, ones, preferred_element_type=jnp.float32)
+        total = got if total is None else total + got
+    shape = (LANES, LANES)
+    diagonal = lax.broadcasted_iota(jnp.int32, shape, 0) == lax.broadcasted_iota(
+        jnp.int32, shape, 1
+    )
+    sub = lax.broadcasted_iota(jnp.int32, (8, LANES), 0)
+    out = jnp.zeros((8, LANES), jnp.float32)
     for x in range(x_n):
-        for b in range(ny // LANES):
-            cols = slice(b * LANES, (b + 1) * LANES)
-            path[x : x + 1, cols] = jnp.sum(acc[x, cols, :].T, axis=0, keepdims=True)
+        part = jnp.where(diagonal, total[x * LANES : (x + 1) * LANES], 0.0)
+        out = jnp.where(sub == x, jnp.sum(part, axis=0, keepdims=True), out)
+    return out
 
 
 def edge_kernel(dims, count_z, *refs):
     x_n, h_n, ny = dims
-    zown, yb, ya, zb, za, path_in = refs[:6]
+    zown, yb, ya, zb, za, acc = refs[:6]
     zp, own = refs[6:8]
     sends = refs[8 : 8 + count_z - 1]
     turned, path = refs[8 + count_z - 1 :]
@@ -380,7 +392,7 @@
     even_z = lax.rem(gz, 2) == 0
     blk = [slice(b * LANES, (b + 1) * LANES) for b in range(nb)]
 
-    sums = [path_in[:, blk[b]] for b in range(nb)]
+    sums = [lane_sums(acc, b) for b in range(nb)]
 
     for side in range(2):
         exists = (gz > 0) if side == 0 else (gz < count_z - 1)
@@ -572,17 +584,16 @@
     zb = lax.ppermute(zs_b, ("gz", "gy"), inner_pairs(count_z, count_y))
     za = lax.ppermute(zs_a, "gz", pairs_of(count_z)[0])
 
-    s2, path, _ = pl.pallas_call(
+    s2, acc, _ = pl.pallas_call(
         functools.partial(section_two_kernel, dims),
         out_shape=(
             pltpu.VMEM((4, x_n, ny, nz), f32),
-            jax.ShapeDtypeStruct((x_n, ny), f32),
+            pltpu.VMEM((x_n, ny, LANES), f32),
             fields,
         ),
         in_specs=[VMEM] * 5,
         out_specs=(VMEM,) * 3,
         input_output_aliases={2: 2},
-        scratch_shapes=[pltpu.VMEM((x_n, ny, LANES), f32)],
         compiler_params=params(),
         cost_estimate=cost(110 * cells, 52 * cells),
         name="section_two",
@@ -603,7 +614,7 @@
         ],
         compiler_params=params(),
         name="edges",
-    )(zown, yb, ya, zb, za, path)
+    )(zown, yb, ya, zb, za, acc)
     zp, own = edges[:2]
 
     total = own

time: 29.1 us -> 28 us (0.962)
  Pallas kernels: 16.6 us -> 15.5 us
    pallas_call x1, Pallas kernels: 5.68 us -> 4.87 us  [on_device(): pl.pallas_call(functools.partial(section_two_kernel, dims), out_shape=(pl...]
    pallas_call x1, Pallas kernels: 4.78 us -> 4.24 us  [on_device(): pl.pallas_call(functools.partial(section_one_kernel, dims), out_shape=fie...]
  transfers between devices with their start and end apart: 7 -> 7, of which waited for: 0 -> 0; matrix products, arithmetic and copies ran while one was open for 0% -> 0% of each run, Pallas kernels for 44% -> 41%
where the time goes in v4:
time: 28 us; the launch traced here: 27.9 us
  Pallas kernels  15.5 us (55%)
  starting transfers between devices  11.1 us (40%)
  between operations  0.74 us (3%)
  other arithmetic  0.57 us (2%)
    pallas_call x1, Pallas kernels, on_device(): pl.pallas_call(functools.partial(section_two_kernel, dims), out_shape=(pl...  4.87 us
    ppermute x3, starting transfers between devices, on_device(): lax.ppermute(edges[1 + k], 'gz', [(i, i ^ k) for i in range(count_z)])  4.45 us
    pallas_call x1, Pallas kernels, on_device(): pl.pallas_call(functools.partial(section_one_kernel, dims), out_shape=fie...  4.24 us
    ppermute x1, starting transfers between devices, on_device(): yb = lax.ppermute(ys_b, 'gy', y_pairs[1])  3.4 us
    pallas_call x1, Pallas kernels, on_device(): pl.pallas_call(functools.partial(pack_kernel, dims, 2), out_shape=(fields...  3.28 us
    ppermute x1, starting transfers between devices, on_device(): za = lax.ppermute(zs_a, 'gz', pairs_of(count_z)[0])  2.65 us
    pallas_call x1, Pallas kernels, on_device(): pl.pallas_call(functools.partial(write_kernel, dims, 4), out_shape=(pltpu...  2.23 us
    pallas_call x1, Pallas kernels, on_device(): pl.pallas_call(functools.partial(edge_kernel, dims, count_z), out_shape=(...  0.67 us
  transfers between devices with their start and end apart: 7, of which 0 were waited for; matrix products, arithmetic and copies ran while one was open for 0% of the time, Pallas kernels for 41%

profile of v4, /device:TPU:0, one launch (start us, length us, event | category | flops | bytes accessed | tf_op | source)
XLA Modules:
  0.0 27.9 jit_solution(9936791543360106333)
XLA Ops:
  0.6 3.3 %load_and_pack.1 = (f32[4,8,2,144,128]{4,3,2,1,0:T(8,128)S(1)}, s32[8,2,144,128]{3,2,1,0:T(8,128)S(1)}, f32[72,256]{1,0:T(8,128)S(1)}, f32[72,256]{1,0:T(8,128)S(1)}, f32[2,152,128]{2,1,0:T(8,128)S(1)}) custom-call(f32[8,128,256]{2,1,0:T(8,128)} %refs_0_.1, f32[8,128,256]{2,1,0:T(8,128)} %refs_1_.1, f32[8,128,256]{2,1,0:T(8,128)} %refs_2_.1, ...), custom_call_target="tpu_custom_call" | custom-call | tf_op jit(solution)/shard_map/load_and_pack/pallas_call | solution.py:541
  3.9 3.4 %collective-permute-start = (f32[72,256]{1,0:T(8,128)S(1)}, f32[72,256]{1,0:T(8,128)S(1)}, u32[]{:S(2)}, u32[]{:S(2)}) collective-permute-start(f32[72,256]{1,0:T(8,128)S(1)} %get-tuple-element.25), channel_id=1, source_target_pairs={{0,7},{1,2},{2,1},{3,4},{4,3},{5,6},{6,5},{7,0},{8,15},{9,10},{10,... | collective-permute-start | bytes 221192 | tf_op jit(solution)/shard_map/ppermute | solution.py:562
  7.3 0.0 collective-permute-start.1
  7.3 4.2 %section_one.1.s1_in.after = f32[4,8,2,144,128]{4,3,2,1,0:T(8,128)S(1)} custom-call(f32[4,8,2,144,128]{4,3,2,1,0:T(8,128)S(1)} %get-tuple-element.23.s0, s32[8,2,144,128]{3,2,1,0:T(8,128)S(1)} %get-tuple-element.24.mk), custom_call_target="tpu_custom_call" | custom-call | flops 26214400 | bytes 9437184 | tf_op jit(solution)/shard_map/section_one/pallas_call | solution.py:565
  11.6 0.0 collective-permute-done.yb.refs_1_
  11.6 0.0 collective-permute-done.1.ya.refs_2_
  11.6 0.2 corners.1
  11.8 0.6 %collective-permute-start.2 = (f32[104,128]{1,0:T(8,128)S(1)}, f32[104,128]{1,0:T(8,128)S(1)}, u32[]{:S(2)}, u32[]{:S(2)}) collective-permute-start(f32[104,128]{1,0:T(8,128)S(1)} %get-tuple-element.29), channel_id=1, source_target_pairs={{0,1},{1,0},{2,3},{3,2},{4,5},{5,4},{6,7},{7,6},{8,16},{9,17},{10,... | collective-permute-start | bytes 159752 | tf_op jit(solution)/shard_map/ppermute | solution.py:584
  12.4 2.6 %collective-permute-start.3 = (f32[104,128]{1,0:T(8,128)S(1)}, f32[104,128]{1,0:T(8,128)S(1)}, u32[]{:S(2)}, u32[]{:S(2)}) collective-permute-start(f32[104,128]{1,0:T(8,128)S(1)} %get-tuple-element.30), channel_id=1, source_target_pairs={{0,8},{8,0},{16,24},{24,16},{1,9},{9,1},{17,25},{25,17},{2,10},{10... | collective-permute-start | bytes 159752 | tf_op jit(solution)/shard_map/ppermute | solution.py:585
  15.0 4.9 %section_two.1 = (f32[4,8,128,256]{3,2,1,0:T(8,128)S(1)}, f32[8,128,128]{2,1,0:T(8,128)S(1)}, f32[4,8,2,144,128]{4,3,2,1,0:T(8,128)S(1)}) custom-call(f32[4,8,2,144,128]{4,3,2,1,0:T(8,128)S(1)} %get-tuple-element.23.s0, s32[8,2,144,128]{3,2,1,0:T(8,128)S(1)} %get-tuple-element.24.mk, ...), custom_call_target="tpu_custom_call", output_to_operand_aliasing={{2}: (2, {})} | custom-call | flops 28835840 | bytes 13631488 | tf_op jit(solution)/shard_map/section_two/pallas_call | solution.py:587
  19.9 0.0 collective-permute-done.2.refs_3_
  19.9 0.0 collective-permute-done.3.refs_4_
  19.9 0.7 %edges.1 = (f32[128,128]{1,0:T(8,128)S(1)}, f32[2,128]{1,0:T(2,128)S(1)}, f32[2,128]{1,0:T(2,128)S(1)}, f32[2,128]{1,0:T(2,128)S(1)}, f32[2,128]{1,0:T(2,128)S(1)}) custom-call(f32[2,152,128]{2,1,0:T(8,128)S(1)} %get-tuple-element.28.zown.refs_0_, f32[72,256]{1,0:T(8,128)S(1)} %collective-permute-done.yb.refs_1_, ...), custom_call_target="tpu_custom_call" | custom-call | tf_op jit(solution)/shard_map/edges/pallas_call | solution.py:603
  20.6 1.4 %collective-permute-start.4 = (f32[2,128]{1,0:T(2,128)S(1)}, f32[2,128]{1,0:T(2,128)S(1)}, u32[]{:S(2)}, u32[]{:S(2)}) collective-permute-start(f32[2,128]{1,0:T(2,128)S(1)} %get-tuple-element.38), channel_id=1, source_target_pairs={{0,24},{8,16},{16,8},{24,0},{1,25},{9,17},{17,9},{25,1},{2,26},{10... | collective-permute-start | bytes 3080 | tf_op jit(solution)/shard_map/ppermute | solution.py:622
  22.0 0.2 collective-permute-start.5
  22.3 2.8 %collective-permute-start.6 = (f32[2,128]{1,0:T(2,128)S(1)}, f32[2,128]{1,0:T(2,128)S(1)}, u32[]{:S(2)}, u32[]{:S(2)}) collective-permute-start(f32[2,128]{1,0:T(2,128)S(1)} %get-tuple-element.40), channel_id=1, source_target_pairs={{0,8},{8,0},{16,24},{24,16},{1,9},{9,1},{17,25},{25,17},{2,10},{10... | collective-permute-start | bytes 3080 | tf_op jit(solution)/shard_map/ppermute | solution.py:622
  25.1 2.2 %write.1 = (f32[8,128,256]{2,1,0:T(8,128)}, f32[8,128,256]{2,1,0:T(8,128)}, f32[8,128,256]{2,1,0:T(8,128)}, f32[8,128,256]{2,1,0:T(8,128)}) custom-call(f32[4,8,128,256]{3,2,1,0:T(8,128)S(1)} %get-tuple-element.27.s2, f32[128,128]{1,0:T(8,128)S(1)} %get-tuple-element.32.zp), custom_call_target="tpu_custom_call" | custom-call | flops 262144 | bytes 8388608 | tf_op jit(solution)/shard_map/write/pallas_call | solution.py:626
  27.3 0.0 collective-permute-done.4
  27.3 0.0 collective-permute-done.5
  27.3 0.0 collective-permute-done.6
  27.3 0.6 %add_add_fusion = f32[2,128]{1,0:T(2,128)} fusion(f32[2,128]{1,0:T(2,128)S(1)} %collective-permute-done.6, f32[2,128]{1,0:T(2,128)S(1)} %collective-permute-done.5, f32[2,128]{1,0:T(2,128)S(1)} %get-tuple-element.37, f32[2,128]{1,0:T(2,128)S(1)} %collective-permute-done.4), kind=kLoop, calls=%fused_computation | loop fusion | flops 768 | bytes 5120 | tf_op jit(solution)/shard_map/add | solution.py:622
Async XLA Ops:
  3.9 7.7 %collective-permute-start = (f32[72,256]{1,0:T(8,128)S(1)}, f32[72,256]{1,0:T(8,128)S(1)}, u32[]{:S(2)}, u32[]{:S(2)}) collective-permute-start(f32[72,256]{1,0:T(8,128)S(1)} %get-tuple-element.25), channel_id=1, source_target_pairs={{0,7},{1,2},{2,1},{3,4},{4,3},{5,6},{6,5},{7,0},{8,15},{9,10},{10,... | collective-permute-start | bytes 221192 | tf_op jit(solution)/shard_map/ppermute | solution.py:562
  7.3 4.3 %collective-permute-start.1 = (f32[72,256]{1,0:T(8,128)S(1)}, f32[72,256]{1,0:T(8,128)S(1)}, u32[]{:S(2)}, u32[]{:S(2)}) collective-permute-start(f32[72,256]{1,0:T(8,128)S(1)} %get-tuple-element.26), channel_id=1, source_target_pairs={{0,1},{1,0},{2,3},{3,2},{4,5},{5,4},{6,7},{7,6},{8,9},{9,8},{10,11... | collective-permute-start | bytes 221192 | tf_op jit(solution)/shard_map/ppermute | solution.py:563
  11.8 8.1 %collective-permute-start.2 = (f32[104,128]{1,0:T(8,128)S(1)}, f32[104,128]{1,0:T(8,128)S(1)}, u32[]{:S(2)}, u32[]{:S(2)}) collective-permute-start(f32[104,128]{1,0:T(8,128)S(1)} %get-tuple-element.29), channel_id=1, source_target_pairs={{0,1},{1,0},{2,3},{3,2},{4,5},{5,4},{6,7},{7,6},{8,16},{9,17},{10,... | collective-permute-start | bytes 159752 | tf_op jit(solution)/shard_map/ppermute | solution.py:584
  12.4 7.5 %collective-permute-start.3 = (f32[104,128]{1,0:T(8,128)S(1)}, f32[104,128]{1,0:T(8,128)S(1)}, u32[]{:S(2)}, u32[]{:S(2)}) collective-permute-start(f32[104,128]{1,0:T(8,128)S(1)} %get-tuple-element.30), channel_id=1, source_target_pairs={{0,8},{8,0},{16,24},{24,16},{1,9},{9,1},{17,25},{25,17},{2,10},{10... | collective-permute-start | bytes 159752 | tf_op jit(solution)/shard_map/ppermute | solution.py:585
  20.6 6.7 %collective-permute-start.4 = (f32[2,128]{1,0:T(2,128)S(1)}, f32[2,128]{1,0:T(2,128)S(1)}, u32[]{:S(2)}, u32[]{:S(2)}) collective-permute-start(f32[2,128]{1,0:T(2,128)S(1)} %get-tuple-element.38), channel_id=1, source_target_pairs={{0,24},{8,16},{16,8},{24,0},{1,25},{9,17},{17,9},{25,1},{2,26},{10... | collective-permute-start | bytes 3080 | tf_op jit(solution)/shard_map/ppermute | solution.py:622
  22.0 5.3 %collective-permute-start.5 = (f32[2,128]{1,0:T(2,128)S(1)}, f32[2,128]{1,0:T(2,128)S(1)}, u32[]{:S(2)}, u32[]{:S(2)}) collective-permute-start(f32[2,128]{1,0:T(2,128)S(1)} %get-tuple-element.39), channel_id=1, source_target_pairs={{0,16},{8,24},{16,0},{24,8},{1,17},{9,25},{17,1},{25,9},{2,18},{10... | collective-permute-start | bytes 3080 | tf_op jit(solution)/shard_map/ppermute | solution.py:622
  22.3 5.1 %collective-permute-start.6 = (f32[2,128]{1,0:T(2,128)S(1)}, f32[2,128]{1,0:T(2,128)S(1)}, u32[]{:S(2)}, u32[]{:S(2)}) collective-permute-start(f32[2,128]{1,0:T(2,128)S(1)} %get-tuple-element.40), channel_id=1, source_target_pairs={{0,8},{8,0},{16,24},{24,16},{1,9},{9,1},{17,25},{25,17},{2,10},{10... | collective-permute-start | bytes 3080 | tf_op jit(solution)/shard_map/ppermute | solution.py:622

commit v5 on v4

--- a/solution.py
+++ b/solution.py
@@ -25,33 +25,36 @@
     return lax.broadcasted_iota(jnp.int32, (8, LANES), 1)
 
 
-def stepped(base, c, e, w, n, s, u, l, scale):
-    h = TIME_STEP * scale
+def stepped(base, c, e, w, n, s, u, l, given=None):
+    half = 0.5 * TIME_STEP
+    given = given or {}
     dx = [a - b for a, b in zip(e, w)]
     dy = [a - b for a, b in zip(n, s)]
-    dz = [a - b for a, b in zip(u, l)]
-    lap = [
-        ((a + b) + (p + q)) + ((r + t) - 6.0 * m)
-        for a, b, p, q, r, t, m in zip(e, w, n, s, u, l, c)
-    ]
+    dz = [given[f][0] if f in given else u[f] - l[f] for f in range(4)]
+    lz = [given[f][1] if f in given else (u[f] + l[f]) - 6.0 * c[f] for f in range(4)]
+    lap = [((a + b) + (p + q)) + t for a, b, p, q, t in zip(e, w, n, s, lz)]
     straight = dx[1] * dx[1] + dy[2] * dy[2] + dz[3] * dz[3]
     shear_a = dy[1] + dx[2]
     shear_b = dz[1] + dx[3]
     shear_c = dz[2] + dy[3]
     shear = shear_a * shear_a + shear_b * shear_b + shear_c * shear_c
-    k = (SMAG_COEF * h) ** 2
+    k = (2.0 * SMAG_COEF) ** 2
     arg = (straight + straight + shear) * (0.25 * k) + 0.01 * k
     eddy = arg * lax.rsqrt(arg)
-    c_mom = eddy + NU_BASE * h
-    c_heat = eddy * (1.0 / PRANDTL) + KAPPA_BASE * h
-    vel = [(0.5 * h) * q for q in c[1:]]
+    c_mom = eddy + 2.0 * NU_BASE
+    c_heat = eddy * (1.0 / PRANDTL) + 2.0 * KAPPA_BASE
     out = []
-    for i in range(4):
-        coef = c_heat if i == 0 else c_mom
-        adv = vel[0] * dx[i] + vel[1] * dy[i] + vel[2] * dz[i]
-        out.append((base[i] + coef * lap[i]) - adv)
-    out[3] = out[3] + (BUOYANCY * h) * c[0]
+    for f in range(4):
+        rate = (c_heat if f == 0 else c_mom) * lap[f]
+        rate = rate - (c[1] * dx[f] + c[2] * dy[f] + c[3] * dz[f])
+        if f == 3:
+            rate = rate + (c[0] if 2.0 * BUOYANCY == 1.0 else (2.0 * BUOYANCY) * c[0])
+        out.append(base[f] + half * rate)
     return out
+
+
+def bent(theta):
+    return 1.0 - jnp.exp2(theta * (-0.125 * math.log2(math.e)))
 
 
 def lane_next(blocks, lane):
@@ -96,10 +99,27 @@
     return ref[pl.ds(lead + start, x, stride=x_stride), :]
 
 
+def height_matrix(nz):
+    i = lax.broadcasted_iota(jnp.int32, (nz, 2 * nz), 0)
+    j = lax.broadcasted_iota(jnp.int32, (nz, 2 * nz), 1)
+    d = jnp.where(j < nz, i - j, i - j + nz)
+    one, next_one = jnp.where(d == 1, 1.0, 0.0), jnp.where(d == -1, 1.0, 0.0)
+    out = jnp.where(j < nz, one - next_one, one + next_one - jnp.where(d == 0, 6.0, 0.0))
+    return out.astype(jnp.bfloat16)
+
+
+def height_differences(rows, matrix):
+    high = rows.astype(jnp.bfloat16)
+    rest = (rows - high.astype(jnp.float32)).astype(jnp.bfloat16)
+    return jnp.dot(
+        jnp.concatenate([high, rest], axis=1), matrix, preferred_element_type=jnp.float32
+    )
+
+
 def pack_kernel(dims, parts, *refs):
     x_n, h_n, ny = dims
     ins = refs[:5]
-    s0, mk, ys_a, ys_b, zown, part, turned, sem = refs[5:]
+    s0, mk, ys_a, ys_b, zown, zd, part, turned, matrix, sem = refs[5:]
     nyp = ny + 2 * PAD
     lane = lane_iota()
     sub = lax.broadcasted_iota(jnp.int32, (8, LANES), 0)
@@ -120,6 +140,29 @@
         c.start()
     group = lane // 8
 
+    nz = h_n * LANES
+    once = height_matrix(nz)
+    matrix[0:nz, :] = once
+    matrix[nz:, :] = once
+
+    def heights(p):
+        rows = slice(PAD + p * size, PAD + (p + 1) * size)
+        q = jnp.concatenate(
+            [
+                jnp.concatenate([s0[0, x, h, rows, :] for h in range(h_n)], axis=1)
+                for x in range(x_n)
+            ],
+            axis=0,
+        )
+        got = height_differences(q, matrix[...])
+        for x in range(x_n):
+            for h in range(h_n):
+                for n in range(2):
+                    at = n * nz + h * LANES
+                    zd[n, x, h, p * size : (p + 1) * size, :] = got[
+                        x * size : (x + 1) * size, at : at + LANES
+                    ]
+
     def columns(t):
         y = PAD + t * 8
         for a in range(2):
@@ -141,6 +184,7 @@
             c.wait()
         for t in range(p * size // 8, (p + 1) * size // 8):
             columns(t)
+        heights(p)
 
     even = lax.rem(lax.axis_index("gy"), 2) == 0
     s0_flat, mk_flat = flat(s0), flat(mk)
@@ -235,13 +279,13 @@
     return [ref[f, x, h, pl.ds(y, 8), :] for f in range(4)]
 
 
-def section_one_kernel(dims, s0, mk, s1):
+def section_one_kernel(dims, s0, mk, zd, s1):
     x_n, h_n, ny = dims
     lane = lane_iota()
 
-    def tile(y, x):
+    def tile(y, yo, x):
         c = [load4(s0, x, h, y) for h in range(h_n)]
-        pairs = [height_pair([c[h][f] for h in range(h_n)], lane) for f in range(4)]
+        pairs = [None] + [height_pair([c[h][f] for h in range(h_n)], lane) for f in range(1, 4)]
         for h in range(h_n):
             r = stepped(
                 c[h],
@@ -250,9 +294,9 @@
                 load4(s0, (x - 1) % x_n, h, y),
                 load4(s0, x, h, y + 1),
                 load4(s0, x, h, y - 1),
-                [p[0][h] for p in pairs],
-                [p[1][h] for p in pairs],
-                1.0,
+                [None] + [p[0][h] for p in pairs[1:]],
+                [None] + [p[1][h] for p in pairs[1:]],
+                {0: [zd[n, x, h, pl.ds(yo, 8), :] for n in range(2)]},
             )
             open_cell = mk[x, h, pl.ds(y, 8), :] != 0
             s1[0, x, h, pl.ds(y, 8), :] = r[0]
@@ -261,7 +305,7 @@
 
     for t in range(ny // 8):
         for x in range(x_n):
-            tile(PAD + t * 8, x)
+            tile(PAD + t * 8, t * 8, x)
 
 
 def outer_rows(dims, s0, mk, ya, yb, s1):
@@ -304,7 +348,6 @@
                     [zero[behind][f][h] for f in range(4)],
                     [p[0][h] for p in pairs],
                     [p[1][h] for p in pairs],
-                    1.0,
                 )
                 for f in range(4):
                     v = q[f] if f == 0 else jnp.where(open_at[r][h], q[f], 0.0)
@@ -323,7 +366,7 @@
         for h in range(h_n):
             start = load4(s0, x, h, y)
             r = stepped(
-                [0.5 * (a + b) for a, b in zip(start, c[h])],
+                [a + b for a, b in zip(start, c[h])],
                 c[h],
                 load4(s1, (x + 1) % x_n, h, y),
                 load4(s1, (x - 1) % x_n, h, y),
@@ -331,14 +374,14 @@
                 load4(s1, x, h, y - 1),
                 [p[0][h] for p in pairs],
                 [p[1][h] for p in pairs],
-                0.5,
             )
-            open_cell = mk[x, h, pl.ds(y, 8), :] != 0
+            part = jnp.where(mk[x, h, pl.ds(y, 8), :] != 0, 0.5, 0.0)
+            theta = 0.5 * r[0]
             cols = slice(h * LANES, (h + 1) * LANES)
-            s2[0, x, pl.ds(yo, 8), cols] = r[0]
+            s2[0, x, pl.ds(yo, 8), cols] = theta
             for f in range(1, 4):
-                s2[f, x, pl.ds(yo, 8), cols] = jnp.where(open_cell, r[f], 0.0)
-            refr = 1.0 - jnp.exp(r[0] * (-0.125))
+                s2[f, x, pl.ds(yo, 8), cols] = part * r[f]
+            refr = bent(theta)
             if h == 0:
                 refr = jnp.where(lane < 2, 0.0, refr)
             if h == h_n - 1:
@@ -425,7 +468,7 @@
         for l in range(2):
             open_at[l] = open_at[l] + [extra(4, l, (0,))[0] != 0.0]
 
-        def advance(state, base, l, scale, blocks):
+        def advance(state, base, l, blocks):
             norths = [lane_next(state[l][f], lane) for f in range(4)]
             souths = [lane_prev(state[l][f], lane) for f in range(4)]
             above, below = (l + 1, l - 1) if side == 0 else (l - 1, l + 1)
@@ -441,7 +484,6 @@
                     [souths[f][b] for f in range(4)],
                     [state[above][f][b] for f in range(4)],
                     [state[below][f][b] for f in range(4)],
-                    scale,
                 )
                 for f in range(4):
                     out[f][b] = q[f] if f == 0 else jnp.where(open_at[l][b], q[f], 0.0)
@@ -449,20 +491,20 @@
 
         one = {}
         for l in range(-1, 3):
-            got = advance(zero, zero[l], l, 1.0, nb + 1 if l in (0, 1) else nb)
+            got = advance(zero, zero[l], l, nb + 1 if l in (0, 1) else nb)
             if l == -1:
                 got = [[jnp.where(exists, v, 0.0) for v in row] for row in got]
             one[l] = got if l in (0, 1) else [row + blank for row in got]
         for l in range(2):
             base = [
-                [0.5 * (zero[l][f][b] + one[l][f][b]) for b in range(nb)] for f in range(4)
+                [zero[l][f][b] + one[l][f][b] for b in range(nb)] for f in range(4)
             ]
-            two = advance(one, base, l, 0.5, nb)
+            two = [[0.5 * v for v in row] for row in advance(one, base, l, nb)]
             slot = 2 + l if side == 0 else 1 - l
             for b in range(nb):
                 for f in range(4):
                     turned[b, pl.ds(f * 32 + slot, 8, stride=4), :] = two[f][b]
-                sums[b] = sums[b] + (1.0 - jnp.exp(two[0][b] * (-0.125)))
+                sums[b] = sums[b] + bent(two[0][b])
     for b in range(nb):
         zp[b * LANES : (b + 1) * LANES, :] = turned[b].T
 
@@ -538,7 +580,7 @@
     def cost(flops, moved):
         return pl.CostEstimate(flops=flops, bytes_accessed=moved, transcendentals=0)
 
-    s0, mk, ys_a, ys_b, zown = pl.pallas_call(
+    s0, mk, ys_a, ys_b, zown, zd = pl.pallas_call(
         functools.partial(pack_kernel, dims, 2),
         out_shape=(
             fields,
@@ -546,12 +588,14 @@
             jax.ShapeDtypeStruct((72, nz), f32),
             jax.ShapeDtypeStruct((72, nz), f32),
             jax.ShapeDtypeStruct((2, 152, ny), f32),
+            pltpu.VMEM((2, x_n, h_n, ny, LANES), f32),
         ),
         in_specs=[HBM] * 5,
-        out_specs=(VMEM,) * 5,
+        out_specs=(VMEM,) * 6,
         scratch_shapes=[
             pltpu.VMEM((3, ny, LANES), f32),
             pltpu.VMEM((3, ny // LANES, LANES, LANES), f32),
+            pltpu.VMEM((2 * nz, 2 * nz), jnp.bfloat16),
             pltpu.SemaphoreType.DMA((2, 5, h_n)),
         ],
         compiler_params=params(),
@@ -565,12 +609,12 @@
     s1 = pl.pallas_call(
         functools.partial(section_one_kernel, dims),
         out_shape=fields,
-        in_specs=[VMEM] * 2,
+        in_specs=[VMEM] * 3,
         out_specs=VMEM,
         compiler_params=params(),
         cost_estimate=cost(100 * cells, 36 * cells),
         name="section_one",
-    )(s0, mk)
+    )(s0, mk, zd)
 
     zs_a, zs_b = pl.pallas_call(
         functools.partial(corner_kernel, dims),

time: 28 us -> 26.9 us (0.961)
  Pallas kernels: 15.5 us -> 14.4 us
    pallas_call x1, Pallas kernels: 4.24 us -> 3.65 us  [on_device(): pl.pallas_call(functools.partial(section_one_kernel, dims), out_shape=fie...]
    pallas_call x1, Pallas kernels: 4.87 us -> 4.4 us  [on_device(): pl.pallas_call(functools.partial(section_two_kernel, dims), out_shape=(pl...]
  transfers between devices with their start and end apart: 7 -> 7, of which waited for: 0 -> 0; matrix products, arithmetic and copies ran while one was open for 0% -> 0% of each run, Pallas kernels for 41% -> 39%
where the time goes in v5:
time: 26.9 us; the launch traced here: 26.7 us
  Pallas kernels  14.4 us (54%)
  starting transfers between devices  11 us (41%)
  between operations  0.73 us (3%)
  other arithmetic  0.57 us (2%)
    ppermute x3, starting transfers between devices, on_device(): lax.ppermute(edges[1 + k], 'gz', [(i, i ^ k) for i in range(count_z)])  4.45 us
    pallas_call x1, Pallas kernels, on_device(): pl.pallas_call(functools.partial(section_two_kernel, dims), out_shape=(pl...  4.4 us
    pallas_call x1, Pallas kernels, on_device(): pl.pallas_call(functools.partial(section_one_kernel, dims), out_shape=fie...  3.65 us
    ppermute x1, starting transfers between devices, on_device(): yb = lax.ppermute(ys_b, 'gy', y_pairs[1])  3.4 us
    pallas_call x1, Pallas kernels, on_device(): pl.pallas_call(functools.partial(pack_kernel, dims, 2), out_shape=(fields...  3.33 us
    ppermute x1, starting transfers between devices, on_device(): za = lax.ppermute(zs_a, 'gz', pairs_of(count_z)[0])  2.65 us
    pallas_call x1, Pallas kernels, on_device(): pl.pallas_call(functools.partial(write_kernel, dims, 4), out_shape=(pltpu...  2.23 us
    pallas_call x1, Pallas kernels, on_device(): pl.pallas_call(functools.partial(edge_kernel, dims, count_z), out_shape=(...  0.65 us
  transfers between devices with their start and end apart: 7, of which 0 were waited for; matrix products, arithmetic and copies ran while one was open for 0% of the time, Pallas kernels for 39%

profile of v5, /device:TPU:0, one launch (start us, length us, event | category | flops | bytes accessed | tf_op | source)
XLA Modules:
  0.0 26.7 jit_solution(11243259989395709202)
XLA Ops:
  0.6 3.3 %load_and_pack.1 = (f32[4,8,2,144,128]{4,3,2,1,0:T(8,128)S(1)}, s32[8,2,144,128]{3,2,1,0:T(8,128)S(1)}, f32[72,256]{1,0:T(8,128)S(1)}, f32[72,256]{1,0:T(8,128)S...) custom-call(f32[8,128,256]{2,1,0:T(8,128)} %refs_0_.1, f32[8,128,256]{2,1,0:T(8,128)} %refs_1_.1, ...), custom_call_target="tpu_custom_call" | custom-call | tf_op jit(solution)/shard_map/load_and_pack/pallas_call | solution.py:583
  4.0 3.4 %collective-permute-start = (f32[72,256]{1,0:T(8,128)S(1)}, f32[72,256]{1,0:T(8,128)S(1)}, u32[]{:S(2)}, u32[]{:S(2)}) collective-permute-start(f32[72,256]{1,0:T(8,128)S(1)} %get-tuple-element.27), channel_id=1, source_target_pairs={{0,7},{1,2},{2,1},{3,4},{4,3},{5,6},{6,5},{7,0},{8,15},{9,10},{10,... | collective-permute-start | bytes 221192 | tf_op jit(solution)/shard_map/ppermute | solution.py:606
  7.4 0.0 collective-permute-start.1
  7.4 3.7 %section_one.1.s1_in.after = f32[4,8,2,144,128]{4,3,2,1,0:T(8,128)S(1)} custom-call(f32[4,8,2,144,128]{4,3,2,1,0:T(8,128)S(1)} %get-tuple-element.24.s0, s32[8,2,144,128]{3,2,1,0:T(8,128)S(1)} %get-tuple-element.25.mk, f32[2,8,2,128,128]{4,3,2,1,0:T(8,128)S(1)} %get-tuple-element.26.zd), custom_call_target="tpu_custom_call" | custom-call | flops 26214400 | bytes 9437184 | tf_op jit(solution)/shard_map/section_one/pallas_call | solution.py:609
  11.0 0.0 collective-permute-done.yb.refs_1_
  11.0 0.0 collective-permute-done.1.ya.refs_2_
  11.1 0.1 corners.1
  11.2 0.5 %collective-permute-start.2 = (f32[104,128]{1,0:T(8,128)S(1)}, f32[104,128]{1,0:T(8,128)S(1)}, u32[]{:S(2)}, u32[]{:S(2)}) collective-permute-start(f32[104,128]{1,0:T(8,128)S(1)} %get-tuple-element.31), channel_id=1, source_target_pairs={{0,1},{1,0},{2,3},{3,2},{4,5},{5,4},{6,7},{7,6},{8,16},{9,17},{10,... | collective-permute-start | bytes 159752 | tf_op jit(solution)/shard_map/ppermute | solution.py:628
  11.7 2.6 %collective-permute-start.3 = (f32[104,128]{1,0:T(8,128)S(1)}, f32[104,128]{1,0:T(8,128)S(1)}, u32[]{:S(2)}, u32[]{:S(2)}) collective-permute-start(f32[104,128]{1,0:T(8,128)S(1)} %get-tuple-element.32), channel_id=1, source_target_pairs={{0,8},{8,0},{16,24},{24,16},{1,9},{9,1},{17,25},{25,17},{2,10},{10... | collective-permute-start | bytes 159752 | tf_op jit(solution)/shard_map/ppermute | solution.py:629
  14.3 4.4 %section_two.1 = (f32[4,8,128,256]{3,2,1,0:T(8,128)S(1)}, f32[8,128,128]{2,1,0:T(8,128)S(1)}, f32[4,8,2,144,128]{4,3,2,1,0:T(8,128)S(1)}) custom-call(f32[4,8,2,144,128]{4,3,2,1,0:T(8,128)S(1)} %get-tuple-element.24.s0, s32[8,2,144,128]{3,2,1,0:T(8,128)S(1)} %get-tuple-element.25.mk, ...), custom_call_target="tpu_custom_call", output_to_operand_aliasing={{2}: (2, {})} | custom-call | flops 28835840 | bytes 13631488 | tf_op jit(solution)/shard_map/section_two/pallas_call | solution.py:631
  18.7 0.0 collective-permute-done.2.refs_3_
  18.7 0.0 collective-permute-done.3.refs_4_
  18.7 0.6 %edges.1 = (f32[128,128]{1,0:T(8,128)S(1)}, f32[2,128]{1,0:T(2,128)S(1)}, f32[2,128]{1,0:T(2,128)S(1)}, f32[2,128]{1,0:T(2,128)S(1)}, f32[2,128]{1,0:T(2,128)S(1)}) custom-call(f32[2,152,128]{2,1,0:T(8,128)S(1)} %get-tuple-element.30.zown.refs_0_, f32[72,256]{1,0:T(8,128)S(1)} %collective-permute-done.yb.refs_1_, ...), custom_call_target="tpu_custom_call" | custom-call | tf_op jit(solution)/shard_map/edges/pallas_call | solution.py:647
  19.4 1.4 %collective-permute-start.4 = (f32[2,128]{1,0:T(2,128)S(1)}, f32[2,128]{1,0:T(2,128)S(1)}, u32[]{:S(2)}, u32[]{:S(2)}) collective-permute-start(f32[2,128]{1,0:T(2,128)S(1)} %get-tuple-element.40), channel_id=1, source_target_pairs={{0,24},{8,16},{16,8},{24,0},{1,25},{9,17},{17,9},{25,1},{2,26},{10... | collective-permute-start | bytes 3080 | tf_op jit(solution)/shard_map/ppermute | solution.py:666
  20.8 0.3 collective-permute-start.5
  21.1 2.8 %collective-permute-start.6 = (f32[2,128]{1,0:T(2,128)S(1)}, f32[2,128]{1,0:T(2,128)S(1)}, u32[]{:S(2)}, u32[]{:S(2)}) collective-permute-start(f32[2,128]{1,0:T(2,128)S(1)} %get-tuple-element.42), channel_id=1, source_target_pairs={{0,8},{8,0},{16,24},{24,16},{1,9},{9,1},{17,25},{25,17},{2,10},{10... | collective-permute-start | bytes 3080 | tf_op jit(solution)/shard_map/ppermute | solution.py:666
  23.9 2.2 %write.1 = (f32[8,128,256]{2,1,0:T(8,128)}, f32[8,128,256]{2,1,0:T(8,128)}, f32[8,128,256]{2,1,0:T(8,128)}, f32[8,128,256]{2,1,0:T(8,128)}) custom-call(f32[4,8,128,256]{3,2,1,0:T(8,128)S(1)} %get-tuple-element.29.s2, f32[128,128]{1,0:T(8,128)S(1)} %get-tuple-element.34.zp), custom_call_target="tpu_custom_call" | custom-call | flops 262144 | bytes 8388608 | tf_op jit(solution)/shard_map/write/pallas_call | solution.py:670
  26.1 0.0 collective-permute-done.4
  26.1 0.0 collective-permute-done.5
  26.1 0.0 collective-permute-done.6
  26.1 0.6 %add_add_fusion = f32[2,128]{1,0:T(2,128)} fusion(f32[2,128]{1,0:T(2,128)S(1)} %collective-permute-done.6, f32[2,128]{1,0:T(2,128)S(1)} %collective-permute-done.5, f32[2,128]{1,0:T(2,128)S(1)} %get-tuple-element.39, f32[2,128]{1,0:T(2,128)S(1)} %collective-permute-done.4), kind=kLoop, calls=%fused_computation | loop fusion | flops 768 | bytes 5120 | tf_op jit(solution)/shard_map/add | solution.py:666
Async XLA Ops:
  4.0 7.1 %collective-permute-start = (f32[72,256]{1,0:T(8,128)S(1)}, f32[72,256]{1,0:T(8,128)S(1)}, u32[]{:S(2)}, u32[]{:S(2)}) collective-permute-start(f32[72,256]{1,0:T(8,128)S(1)} %get-tuple-element.27), channel_id=1, source_target_pairs={{0,7},{1,2},{2,1},{3,4},{4,3},{5,6},{6,5},{7,0},{8,15},{9,10},{10,... | collective-permute-start | bytes 221192 | tf_op jit(solution)/shard_map/ppermute | solution.py:606
  7.4 3.7 %collective-permute-start.1 = (f32[72,256]{1,0:T(8,128)S(1)}, f32[72,256]{1,0:T(8,128)S(1)}, u32[]{:S(2)}, u32[]{:S(2)}) collective-permute-start(f32[72,256]{1,0:T(8,128)S(1)} %get-tuple-element.28), channel_id=1, source_target_pairs={{0,1},{1,0},{2,3},{3,2},{4,5},{5,4},{6,7},{7,6},{8,9},{9,8},{10,11... | collective-permute-start | bytes 221192 | tf_op jit(solution)/shard_map/ppermute | solution.py:607
  11.2 7.6 %collective-permute-start.2 = (f32[104,128]{1,0:T(8,128)S(1)}, f32[104,128]{1,0:T(8,128)S(1)}, u32[]{:S(2)}, u32[]{:S(2)}) collective-permute-start(f32[104,128]{1,0:T(8,128)S(1)} %get-tuple-element.31), channel_id=1, source_target_pairs={{0,1},{1,0},{2,3},{3,2},{4,5},{5,4},{6,7},{7,6},{8,16},{9,17},{10,... | collective-permute-start | bytes 159752 | tf_op jit(solution)/shard_map/ppermute | solution.py:628
  11.7 7.1 %collective-permute-start.3 = (f32[104,128]{1,0:T(8,128)S(1)}, f32[104,128]{1,0:T(8,128)S(1)}, u32[]{:S(2)}, u32[]{:S(2)}) collective-permute-start(f32[104,128]{1,0:T(8,128)S(1)} %get-tuple-element.32), channel_id=1, source_target_pairs={{0,8},{8,0},{16,24},{24,16},{1,9},{9,1},{17,25},{25,17},{2,10},{10... | collective-permute-start | bytes 159752 | tf_op jit(solution)/shard_map/ppermute | solution.py:629
  19.4 6.7 %collective-permute-start.4 = (f32[2,128]{1,0:T(2,128)S(1)}, f32[2,128]{1,0:T(2,128)S(1)}, u32[]{:S(2)}, u32[]{:S(2)}) collective-permute-start(f32[2,128]{1,0:T(2,128)S(1)} %get-tuple-element.40), channel_id=1, source_target_pairs={{0,24},{8,16},{16,8},{24,0},{1,25},{9,17},{17,9},{25,1},{2,26},{10... | collective-permute-start | bytes 3080 | tf_op jit(solution)/shard_map/ppermute | solution.py:666
  20.8 5.3 %collective-permute-start.5 = (f32[2,128]{1,0:T(2,128)S(1)}, f32[2,128]{1,0:T(2,128)S(1)}, u32[]{:S(2)}, u32[]{:S(2)}) collective-permute-start(f32[2,128]{1,0:T(2,128)S(1)} %get-tuple-element.41), channel_id=1, source_target_pairs={{0,16},{8,24},{16,0},{24,8},{1,17},{9,25},{17,1},{25,9},{2,18},{10... | collective-permute-start | bytes 3080 | tf_op jit(solution)/shard_map/ppermute | solution.py:666
  21.1 5.0 %collective-permute-start.6 = (f32[2,128]{1,0:T(2,128)S(1)}, f32[2,128]{1,0:T(2,128)S(1)}, u32[]{:S(2)}, u32[]{:S(2)}) collective-permute-start(f32[2,128]{1,0:T(2,128)S(1)} %get-tuple-element.42), channel_id=1, source_target_pairs={{0,8},{8,0},{16,24},{24,16},{1,9},{9,1},{17,25},{25,17},{2,10},{10... | collective-permute-start | bytes 3080 | tf_op jit(solution)/shard_map/ppermute | solution.py:666

commit v6 on v5

--- a/solution.py
+++ b/solution.py
@@ -424,7 +424,7 @@
 
 def edge_kernel(dims, count_z, *refs):
     x_n, h_n, ny = dims
-    zown, yb, ya, zb, za, acc = refs[:6]
+    zown, yb, ya, za, zb, acc = refs[:6]
     zp, own = refs[6:8]
     sends = refs[8 : 8 + count_z - 1]
     turned, path = refs[8 + count_z - 1 :]
@@ -658,11 +658,11 @@
         ],
         compiler_params=params(),
         name="edges",
-    )(zown, yb, ya, zb, za, acc)
+    )(zown, yb, ya, za, zb, acc)
     zp, own = edges[:2]
 
     total = own
-    for k in range(count_z - 1, 0, -1):
+    for k in (3, 1, 2) if count_z == 4 else range(count_z - 1, 0, -1):
         total = total + lax.ppermute(
             edges[1 + k], "gz", [(i, i ^ k) for i in range(count_z)]
         )

time: 26.9 us -> 26.3 us (0.978)
  starting transfers between devices: 11 us -> 9.69 us
  waiting for transfers between devices: 0.02 us -> 0.84 us
    ppermute x1, starting transfers between devices: 2.65 us -> 1.59 us  [on_device(): za = lax.ppermute(zs_a, 'gz', pairs_of(count_z)[0])]
    ppermute x3, waiting for transfers between devices: 0.01 us -> 0.83 us  [on_device(): lax.ppermute(edges[1 + k], 'gz', [(i, i ^ k) for i in range(count_z)])]
    ppermute x1, starting transfers between devices: 0.52 us -> 0.23 us  [on_device(): zb = lax.ppermute(zs_b, ('gz', 'gy'), inner_pairs(count_z, count_y))]
  transfers between devices with their start and end apart: 7 -> 7, of which waited for: 0 -> 1; matrix products, arithmetic and copies ran while one was open for 0% -> 0% of each run, Pallas kernels for 39% -> 39%
where the time goes in v6:
time: 26.3 us; the launch traced here: 26.2 us
  Pallas kernels  14.4 us (55%)
  starting transfers between devices  9.69 us (37%)
  waiting for transfers between devices  0.84 us (3%)
  between operations  0.72 us (3%)
  other arithmetic  0.57 us (2%)
    ppermute x3, starting transfers between devices, on_device(): lax.ppermute(edges[1 + k], 'gz', [(i, i ^ k) for i in range(count_z)])  4.46 us
    pallas_call x1, Pallas kernels, on_device(): pl.pallas_call(functools.partial(section_two_kernel, dims), out_shape=(pl...  4.4 us
    pallas_call x1, Pallas kernels, on_device(): pl.pallas_call(functools.partial(section_one_kernel, dims), out_shape=fie...  3.65 us
    ppermute x1, starting transfers between devices, on_device(): yb = lax.ppermute(ys_b, 'gy', y_pairs[1])  3.4 us
    pallas_call x1, Pallas kernels, on_device(): pl.pallas_call(functools.partial(pack_kernel, dims, 2), out_shape=(fields...  3.33 us
    pallas_call x1, Pallas kernels, on_device(): pl.pallas_call(functools.partial(write_kernel, dims, 4), out_shape=(pltpu...  2.23 us
    ppermute x1, starting transfers between devices, on_device(): za = lax.ppermute(zs_a, 'gz', pairs_of(count_z)[0])  1.59 us
    ppermute x3, waiting for transfers between devices, on_device(): lax.ppermute(edges[1 + k], 'gz', [(i, i ^ k) for i in range(count_z)])  0.83 us
  transfers between devices with their start and end apart: 7, of which 1 were waited for; matrix products, arithmetic and copies ran while one was open for 0% of the time, Pallas kernels for 39%

profile of v6, /device:TPU:0, one launch (start us, length us, event | category | flops | bytes accessed | tf_op | source)
XLA Modules:
  0.0 26.2 jit_solution(10962773440921965858)
XLA Ops:
  0.6 3.3 %load_and_pack.1 = (f32[4,8,2,144,128]{4,3,2,1,0:T(8,128)S(1)}, s32[8,2,144,128]{3,2,1,0:T(8,128)S(1)}, f32[72,256]{1,0:T(8,128)S(1)}, f32[72,256]{1,0:T(8,128)S...) custom-call(f32[8,128,256]{2,1,0:T(8,128)} %refs_0_.1, f32[8,128,256]{2,1,0:T(8,128)} %refs_1_.1, ...), custom_call_target="tpu_custom_call" | custom-call | tf_op jit(solution)/shard_map/load_and_pack/pallas_call | solution.py:583
  4.0 3.4 %collective-permute-start = (f32[72,256]{1,0:T(8,128)S(1)}, f32[72,256]{1,0:T(8,128)S(1)}, u32[]{:S(2)}, u32[]{:S(2)}) collective-permute-start(f32[72,256]{1,0:T(8,128)S(1)} %get-tuple-element.27), channel_id=1, source_target_pairs={{0,7},{1,2},{2,1},{3,4},{4,3},{5,6},{6,5},{7,0},{8,15},{9,10},{10,... | collective-permute-start | bytes 221192 | tf_op jit(solution)/shard_map/ppermute | solution.py:606
  7.4 0.0 collective-permute-start.1
  7.4 3.7 %section_one.1.s1_in.after = f32[4,8,2,144,128]{4,3,2,1,0:T(8,128)S(1)} custom-call(f32[4,8,2,144,128]{4,3,2,1,0:T(8,128)S(1)} %get-tuple-element.24.s0, s32[8,2,144,128]{3,2,1,0:T(8,128)S(1)} %get-tuple-element.25.mk, f32[2,8,2,128,128]{4,3,2,1,0:T(8,128)S(1)} %get-tuple-element.26.zd), custom_call_target="tpu_custom_call" | custom-call | flops 26214400 | bytes 9437184 | tf_op jit(solution)/shard_map/section_one/pallas_call | solution.py:609
  11.0 0.0 collective-permute-done.yb.refs_1_
  11.0 0.0 collective-permute-done.1.ya.refs_2_
  11.1 0.1 corners.1
  11.2 1.6 %collective-permute-start.2 = (f32[104,128]{1,0:T(8,128)S(1)}, f32[104,128]{1,0:T(8,128)S(1)}, u32[]{:S(2)}, u32[]{:S(2)}) collective-permute-start(f32[104,128]{1,0:T(8,128)S(1)} %get-tuple-element.31), channel_id=1, source_target_pairs={{0,8},{8,0},{16,24},{24,16},{1,9},{9,1},{17,25},{25,17},{2,10},{10... | collective-permute-start | bytes 159752 | tf_op jit(solution)/shard_map/ppermute | solution.py:629
  12.7 0.2 collective-permute-start.3
  13.0 4.4 %section_two.1 = (f32[4,8,128,256]{3,2,1,0:T(8,128)S(1)}, f32[8,128,128]{2,1,0:T(8,128)S(1)}, f32[4,8,2,144,128]{4,3,2,1,0:T(8,128)S(1)}) custom-call(f32[4,8,2,144,128]{4,3,2,1,0:T(8,128)S(1)} %get-tuple-element.24.s0, s32[8,2,144,128]{3,2,1,0:T(8,128)S(1)} %get-tuple-element.25.mk, ...), custom_call_target="tpu_custom_call", output_to_operand_aliasing={{2}: (2, {})} | custom-call | flops 28835840 | bytes 13631488 | tf_op jit(solution)/shard_map/section_two/pallas_call | solution.py:631
  17.4 0.0 collective-permute-done.2.refs_3_
  17.4 0.0 collective-permute-done.3.refs_4_
  17.4 0.6 %edges.1 = (f32[128,128]{1,0:T(8,128)S(1)}, f32[2,128]{1,0:T(2,128)S(1)}, f32[2,128]{1,0:T(2,128)S(1)}, f32[2,128]{1,0:T(2,128)S(1)}, f32[2,128]{1,0:T(2,128)S(1)}) custom-call(f32[2,152,128]{2,1,0:T(8,128)S(1)} %get-tuple-element.30.zown.refs_0_, f32[72,256]{1,0:T(8,128)S(1)} %collective-permute-done.yb.refs_1_, ...), custom_call_target="tpu_custom_call" | custom-call | tf_op jit(solution)/shard_map/edges/pallas_call | solution.py:647
  18.0 2.5 %collective-permute-start.4 = (f32[2,128]{1,0:T(2,128)S(1)}, f32[2,128]{1,0:T(2,128)S(1)}, u32[]{:S(2)}, u32[]{:S(2)}) collective-permute-start(f32[2,128]{1,0:T(2,128)S(1)} %get-tuple-element.40), channel_id=1, source_target_pairs={{0,24},{8,16},{16,8},{24,0},{1,25},{9,17},{17,9},{25,1},{2,26},{10... | collective-permute-start | bytes 3080 | tf_op jit(solution)/shard_map/ppermute | solution.py:666
  20.6 0.5 %collective-permute-start.5 = (f32[2,128]{1,0:T(2,128)S(1)}, f32[2,128]{1,0:T(2,128)S(1)}, u32[]{:S(2)}, u32[]{:S(2)}) collective-permute-start(f32[2,128]{1,0:T(2,128)S(1)} %get-tuple-element.41), channel_id=1, source_target_pairs={{0,8},{8,0},{16,24},{24,16},{1,9},{9,1},{17,25},{25,17},{2,10},{10... | collective-permute-start | bytes 3080 | tf_op jit(solution)/shard_map/ppermute | solution.py:666
  21.1 1.4 %collective-permute-start.6 = (f32[2,128]{1,0:T(2,128)S(1)}, f32[2,128]{1,0:T(2,128)S(1)}, u32[]{:S(2)}, u32[]{:S(2)}) collective-permute-start(f32[2,128]{1,0:T(2,128)S(1)} %get-tuple-element.42), channel_id=1, source_target_pairs={{0,16},{8,24},{16,0},{24,8},{1,17},{9,25},{17,1},{25,9},{2,18},{10... | collective-permute-start | bytes 3080 | tf_op jit(solution)/shard_map/ppermute | solution.py:666
  22.5 2.2 %write.1 = (f32[8,128,256]{2,1,0:T(8,128)}, f32[8,128,256]{2,1,0:T(8,128)}, f32[8,128,256]{2,1,0:T(8,128)}, f32[8,128,256]{2,1,0:T(8,128)}) custom-call(f32[4,8,128,256]{3,2,1,0:T(8,128)S(1)} %get-tuple-element.29.s2, f32[128,128]{1,0:T(8,128)S(1)} %get-tuple-element.34.zp), custom_call_target="tpu_custom_call" | custom-call | flops 262144 | bytes 8388608 | tf_op jit(solution)/shard_map/write/pallas_call | solution.py:670
  24.8 0.0 collective-permute-done.4
  24.8 0.0 collective-permute-done.5
  24.8 0.8 %collective-permute-done.6 = f32[2,128]{1,0:T(2,128)S(1)} collective-permute-done((f32[2,128]{1,0:T(2,128)S(1)}, f32[2,128]{1,0:T(2,128)S(1)}, u32[]{:S(2)}, u32[]{:S(2)}) %collective-permute-start.6) | collective-permute-done | bytes 1056 | tf_op jit(solution)/shard_map/ppermute | solution.py:666
  25.6 0.6 %add_add_fusion = f32[2,128]{1,0:T(2,128)} fusion(f32[2,128]{1,0:T(2,128)S(1)} %collective-permute-done.6, f32[2,128]{1,0:T(2,128)S(1)} %collective-permute-done.5, f32[2,128]{1,0:T(2,128)S(1)} %get-tuple-element.39, f32[2,128]{1,0:T(2,128)S(1)} %collective-permute-done.4), kind=kLoop, calls=%fused_computation | loop fusion | flops 768 | bytes 5120 | tf_op jit(solution)/shard_map/add | solution.py:666
Async XLA Ops:
  4.0 7.1 %collective-permute-start = (f32[72,256]{1,0:T(8,128)S(1)}, f32[72,256]{1,0:T(8,128)S(1)}, u32[]{:S(2)}, u32[]{:S(2)}) collective-permute-start(f32[72,256]{1,0:T(8,128)S(1)} %get-tuple-element.27), channel_id=1, source_target_pairs={{0,7},{1,2},{2,1},{3,4},{4,3},{5,6},{6,5},{7,0},{8,15},{9,10},{10,... | collective-permute-start | bytes 221192 | tf_op jit(solution)/shard_map/ppermute | solution.py:606
  7.4 3.7 %collective-permute-start.1 = (f32[72,256]{1,0:T(8,128)S(1)}, f32[72,256]{1,0:T(8,128)S(1)}, u32[]{:S(2)}, u32[]{:S(2)}) collective-permute-start(f32[72,256]{1,0:T(8,128)S(1)} %get-tuple-element.28), channel_id=1, source_target_pairs={{0,1},{1,0},{2,3},{3,2},{4,5},{5,4},{6,7},{7,6},{8,9},{9,8},{10,11... | collective-permute-start | bytes 221192 | tf_op jit(solution)/shard_map/ppermute | solution.py:607
  11.2 6.2 %collective-permute-start.2 = (f32[104,128]{1,0:T(8,128)S(1)}, f32[104,128]{1,0:T(8,128)S(1)}, u32[]{:S(2)}, u32[]{:S(2)}) collective-permute-start(f32[104,128]{1,0:T(8,128)S(1)} %get-tuple-element.31), channel_id=1, source_target_pairs={{0,8},{8,0},{16,24},{24,16},{1,9},{9,1},{17,25},{25,17},{2,10},{10... | collective-permute-start | bytes 159752 | tf_op jit(solution)/shard_map/ppermute | solution.py:629
  12.7 4.6 %collective-permute-start.3 = (f32[104,128]{1,0:T(8,128)S(1)}, f32[104,128]{1,0:T(8,128)S(1)}, u32[]{:S(2)}, u32[]{:S(2)}) collective-permute-start(f32[104,128]{1,0:T(8,128)S(1)} %get-tuple-element.32), channel_id=1, source_target_pairs={{0,1},{1,0},{2,3},{3,2},{4,5},{5,4},{6,7},{7,6},{8,16},{9,17},{10,... | collective-permute-start | bytes 159752 | tf_op jit(solution)/shard_map/ppermute | solution.py:628
  18.0 6.7 %collective-permute-start.4 = (f32[2,128]{1,0:T(2,128)S(1)}, f32[2,128]{1,0:T(2,128)S(1)}, u32[]{:S(2)}, u32[]{:S(2)}) collective-permute-start(f32[2,128]{1,0:T(2,128)S(1)} %get-tuple-element.40), channel_id=1, source_target_pairs={{0,24},{8,16},{16,8},{24,0},{1,25},{9,17},{17,9},{25,1},{2,26},{10... | collective-permute-start | bytes 3080 | tf_op jit(solution)/shard_map/ppermute | solution.py:666
  20.6 4.2 %collective-permute-start.5 = (f32[2,128]{1,0:T(2,128)S(1)}, f32[2,128]{1,0:T(2,128)S(1)}, u32[]{:S(2)}, u32[]{:S(2)}) collective-permute-start(f32[2,128]{1,0:T(2,128)S(1)} %get-tuple-element.41), channel_id=1, source_target_pairs={{0,8},{8,0},{16,24},{24,16},{1,9},{9,1},{17,25},{25,17},{2,10},{10... | collective-permute-start | bytes 3080 | tf_op jit(solution)/shard_map/ppermute | solution.py:666
  21.1 4.5 %collective-permute-start.6 = (f32[2,128]{1,0:T(2,128)S(1)}, f32[2,128]{1,0:T(2,128)S(1)}, u32[]{:S(2)}, u32[]{:S(2)}) collective-permute-start(f32[2,128]{1,0:T(2,128)S(1)} %get-tuple-element.42), channel_id=1, source_target_pairs={{0,16},{8,24},{16,0},{24,8},{1,17},{9,25},{17,1},{25,9},{2,18},{10... | collective-permute-start | bytes 3080 | tf_op jit(solution)/shard_map/ppermute | solution.py:666
